TPU v7x, 32 devices: a whole 2x2x4 slice. The times are simulated.
32 devices in a mesh: section: 4 (over z), tp: 8 (over y, x, core).
Axes of the slice: x: 2, y: 2, z: 4, core: 2. Of those that a mesh axis runs over, the one named last changes fastest.
Arguments:
- stash: bfloat16 [4, 4, 192, 1024], P('section', None, 'tp'), may hold values from -6 to 6
- w_in: bfloat16 [4, 1024, 65536], P('section', None, 'tp'), may hold values from -0.1875 to 0.1875
- w_out: bfloat16 [4, 65536, 1024], P('section', 'tp'), may hold values from -0.0234375 to 0.0234375
- gain: float32 [4, 1024], P('section'), may hold values from 0.1 to 1.9
- plan: int32 [3, 4], replicated, may hold values from 0 to 3
- arriving: bfloat16 [4, 192, 1024], P('section', 'tp'), may hold values from -6 to 6
- fresh: bfloat16 [2, 192, 1024], P(None, 'tp'), may hold values from -6 to 6
Outputs:
- input_grads: bfloat16 [3, 4, 192, 1024], P(None, 'section', 'tp')
All inputs are finite; a program needn't handle non-finite values.
Results may differ from a plain program's by a relative error of at most 0.0085.
Values may be sent and summed in bfloat16 or wider, within the bound.
No kernel may reach another device: no remote copies, remote signals or barrier semaphores. Data moves between devices by JAX's collectives and lax.ppermute only.
A program may use at most 128 MiB of HBM per device.

v0:
```python
import functools

import jax
import jax.numpy as jnp
from jax import lax
from jax.experimental import pallas as pl
from jax.experimental.pallas import tpu as pltpu
from jax.sharding import PartitionSpec as P

epsilon = 1e-06
MIB = 2**20
f32 = jnp.float32
bf16 = jnp.bfloat16
VMEM = pl.BlockSpec(memory_space=pltpu.VMEM)
HBM = pl.BlockSpec(memory_space=pltpu.HBM)
SMEM = pl.BlockSpec(memory_space=pltpu.SMEM)
ANY = pl.BlockSpec(memory_space=pl.ANY)


def shape_of(shape, dtype):
    return jax.ShapeDtypeStruct(shape, dtype)


def limit(mib):
    return pltpu.CompilerParams(vmem_limit_bytes=mib * MIB)


def in_vmem(value):
    return pltpu.with_memory_space_constraint(value, pltpu.VMEM)


def in_hbm(value):
    return pltpu.with_memory_space_constraint(value, pltpu.HBM)


def swapped(value, mask):
    return lax.ppermute(value, "tp", [(i, i ^ mask) for i in range(lax.axis_size("tp"))])


def from_mirror(value):
    count = lax.axis_size("section")
    return lax.ppermute(value, "section", [(i, (i + count // 2) % count) for i in range(count)])


def from_above(value, mask):
    sections, parts = lax.axis_size("section"), lax.axis_size("tp")
    pairs = [
        (((s + 1) % sections) * parts + (i ^ mask), s * parts + i)
        for s in range(sections)
        for i in range(parts)
    ]
    return lax.ppermute(value, ("section", "tp"), pairs)


def with_cores(chips):
    return chips + [swapped(value, 1) for value in chips]


def pick_kernel(plan, stash, picked, sems):
    sections = lax.axis_size("section")
    partner = lax.rem(lax.axis_index("section") + sections // 2, sections)
    copies = [
        pltpu.make_async_copy(stash.at[0, plan[tick, partner]], picked.at[tick], sems.at[tick])
        for tick in range(plan.shape[0])
    ]
    for copy in copies:
        copy.start()
    for copy in copies:
        copy.wait()


def pick(plan, stash):
    ticks, (_, _, rows, width) = plan.shape[0], stash.shape
    return pl.pallas_call(
        pick_kernel,
        out_shape=shape_of((ticks, rows, width), stash.dtype),
        in_specs=[SMEM, HBM],
        out_specs=VMEM,
        scratch_shapes=[pltpu.SemaphoreType.DMA((ticks,))],
        compiler_params=limit(2),
        name="pick",
    )(in_hbm(plan), in_hbm(stash))


def load_kernel(axis, weight, after, *refs):
    *pieces, token, sems = refs
    copies = []
    for at, piece in enumerate(pieces):
        where = [slice(None), slice(None)]
        where[axis] = pl.ds(at * piece.shape[axis], piece.shape[axis])
        copies.append(pltpu.make_async_copy(weight.at[0, *where], piece, sems.at[at]))
    for copy in copies:
        copy.start()
    token[...] = jnp.zeros_like(token)
    for copy in copies:
        copy.wait()


PIECES = 4


def load(weight, axis, after):
    shape = list(weight.shape[1:])
    shape[axis] //= PIECES
    piece = pltpu.VMEM(tuple(shape), weight.dtype)
    *pieces, token = pl.pallas_call(
        functools.partial(load_kernel, axis),
        out_shape=(*[piece] * PIECES, shape_of((8, 128), f32)),
        in_specs=[HBM, ANY],
        out_specs=tuple([VMEM] * (PIECES + 1)),
        scratch_shapes=[pltpu.SemaphoreType.DMA((PIECES,))],
        compiler_params=limit(2),
        cost_estimate=pl.CostEstimate(
            flops=0, bytes_accessed=4 * PIECES * shape[0] * shape[1], transcendentals=0
        ),
        name="load",
    )(in_hbm(weight), after)
    return pieces, token


def tie_kernel(*refs):
    pass


def tie(values, token):
    return pl.pallas_call(
        tie_kernel,
        out_shape=tuple(shape_of(value.shape, value.dtype) for value in values),
        in_specs=[ANY] * (len(values) + 1),
        out_specs=tuple([ANY] * len(values)),
        input_output_aliases={at: at for at in range(len(values))},
        compiler_params=limit(1),
        name="tie",
    )(*values, token)


def pack_kernel(many, one, after, out):
    count = many.shape[0]
    out[:count] = many[...]
    out[count] = one[0]


def pack(many, one, after):
    count, *block = many.shape
    return pl.pallas_call(
        pack_kernel,
        out_shape=shape_of((count + 1, *block), many.dtype),
        in_specs=[VMEM, VMEM, ANY],
        out_specs=VMEM,
        compiler_params=limit(2),
        name="pack",
    )(many, one, after)


def joined(blocks, at):
    return jnp.concatenate([block[at].astype(f32) for block in blocks], axis=0)


def kernel_blocks(blocks):
    if blocks[0].shape[1] % 8 == 0:
        return list(blocks)
    return [jnp.concatenate(blocks, axis=1)]


def normalised(values):
    inverse_rms = lax.rsqrt(jnp.mean(values * values, axis=-1, keepdims=True) + epsilon)
    return inverse_rms, values * inverse_rms


def gate_values(inputs, w_in, part):
    preact = jnp.dot(inputs, w_in[:, part], preferred_element_type=f32)
    return (2.0 * jnp.maximum(preact, 0.0)).T


def spans(size, chunk):
    chunk = min(chunk, size)
    return [pl.ds(at, chunk) for at in range(0, size, chunk)]


def gate_kernel(count, at, pieces, chunk, *refs):
    blocks, gain, w_ins = refs[:count], refs[count], refs[count + 1 : count + 1 + pieces]
    *outs, token = refs[-pieces - 1 :]
    token[...] = jnp.zeros_like(token)
    inputs = (normalised(joined(blocks, at))[1] * gain[...]).astype(bf16)
    chunk = min(chunk, outs[0].shape[0])
    for w_in, out in zip(w_ins, outs):

        def step(at, _, w_in=w_in, out=out):
            part = pl.ds(pl.multiple_of(at * chunk, chunk), chunk)
            out[part, :] = gate_values(inputs, w_in, part).astype(bf16)
            return 0

        lax.fori_loop(0, out.shape[0] // chunk, step, 0)


def gate(blocks, at, gain, w_ins, chunk, after, kept):
    blocks = kernel_blocks(blocks)
    tokens = sum(block.shape[1] for block in blocks)
    width, hidden = w_ins[0].shape
    pieces = len(w_ins)
    w_ins, kept = [[in_vmem(value) for value in values] for values in (w_ins, kept)]
    *gates, token = pl.pallas_call(
        functools.partial(gate_kernel, len(blocks), at, pieces, chunk),
        out_shape=(*[pltpu.VMEM((hidden, tokens), bf16)] * pieces, shape_of((8, 128), f32)),
        in_specs=[VMEM] * (len(blocks) + 1 + pieces) + [ANY] * (1 + len(kept)),
        out_specs=tuple([VMEM] * (pieces + 1)),
        compiler_params=limit(4),
        cost_estimate=pl.CostEstimate(
            flops=2 * tokens * width * hidden * pieces,
            bytes_accessed=(2 * width + 2 * tokens) * hidden * pieces,
            transcendentals=0,
        ),
        name="gate",
    )(*blocks, gain, *w_ins, after, *kept)
    return gates, token


def back_kernel(count, chunk, ticks, *refs):
    blocks, (*operands, own, other) = refs[:count], refs[count:]
    w_outs, w_ins, extra = operands[:PIECES], operands[PIECES : 2 * PIECES], operands[2 * PIECES :]
    paired = len(extra) == 1
    if paired:
        inputs = (normalised(joined(blocks, 0))[1] * extra[0][...]).astype(bf16)
    incoming = joined(blocks, ticks if paired else ...).T.astype(bf16)
    total = None
    for half, (w_out, w_in) in enumerate(zip(w_outs, w_ins)):
        for part in spans(w_out.shape[0], chunk):
            hidden_back = jnp.dot(w_out[part, :], incoming, preferred_element_type=f32)
            if paired:
                factor = gate_values(inputs, w_in, part)
            else:
                factor = extra[half][part, :].astype(f32)
            hidden_grad = (hidden_back * factor).astype(bf16)
            partial = jnp.dot(w_in[:, part], hidden_grad, preferred_element_type=f32)
            total = partial if total is None else total + partial
    sums = total.T
    rows = own.shape[0]
    own[...] = sums[:rows]
    other[...] = sums[rows:].astype(bf16)


def back(blocks, ticks, extra, w_outs, w_ins, chunk):
    paired = len(extra) == 1
    if paired:
        blocks = kernel_blocks(blocks)
    elif blocks[0].shape[0] % 8:
        blocks = [jnp.concatenate(blocks, axis=0)]
    tokens = sum(block.shape[-2] for block in blocks)
    width, hidden = w_ins[0].shape
    hidden *= PIECES
    extra = extra if paired else [in_vmem(part) for part in extra]
    operands = [*blocks, *[in_vmem(half) for half in (*w_outs, *w_ins)], *extra]
    return pl.pallas_call(
        functools.partial(back_kernel, len(blocks), chunk, ticks),
        out_shape=(
            shape_of((tokens // 2, width), f32),
            shape_of((tokens // 2, width), bf16),
        ),
        in_specs=[VMEM] * len(operands),
        out_specs=(VMEM, VMEM),
        compiler_params=limit(8 if paired else 6),
        cost_estimate=pl.CostEstimate(
            flops=(6 if paired else 4) * tokens * width * hidden,
            bytes_accessed=4 * width * hidden + 2 * tokens * hidden,
            transcendentals=0,
        ),
        name="first" if paired else "back",
    )(*operands)


def fold_values(own, received, rows):
    sums = own + received.astype(f32)
    return [sums[:rows]] + [
        sums[at : at + rows].astype(bf16) for at in range(rows, sums.shape[0], rows)
    ]


def fold_kernel(rows, own, received, *outs):
    for out, value in zip(outs, fold_values(own[...], received[...], rows)):
        out[...] = value


def fold(own, received, rows):
    if rows % 8:
        return fold_values(own, received, rows)
    half, width = own.shape
    return pl.pallas_call(
        functools.partial(fold_kernel, rows),
        out_shape=tuple(
            shape_of((rows, width), bf16 if at else f32) for at in range(half // rows)
        ),
        in_specs=[VMEM] * 2,
        out_specs=tuple([VMEM] * (half // rows)),
        compiler_params=limit(2),
        name="fold",
    )(own, received)


def finish_kernel(ending, ticks, tick, *refs):
    own, incoming, x_rows, gain, extra, _ = refs[:6]
    received, outs = (refs[6:-1], refs[-1:]) if ending else (refs[6:-2], refs[-2:])
    if ending:
        past, received = received[:ending], received[ending:]
    total = own[...]
    for block in received:
        total = total + block[...].astype(f32)
    inverse_rms, normed = normalised(x_rows[tick].astype(f32))
    scaled = total * gain[...]
    inner = jnp.mean(scaled * normed, axis=-1, keepdims=True)
    incoming_rows = incoming[ticks] if ticks else incoming[...]
    result = (incoming_rows.astype(f32) + inverse_rms * (scaled - normed * inner)).astype(bf16)
    if ending:
        for before in range(ending):
            outs[0][before, 0] = past[before][...]
        outs[0][ending, 0] = result
    else:
        outs[0][...] = result
        outs[1][...] = jnp.where(lax.axis_index("section") == 0, extra[tick], result)


def finish(own, received, incoming, x_rows, gain, fresh, tick, after, past=None):
    rows, width = own.shape
    ending = 0 if past is None else len(past)
    block = shape_of((rows, width), bf16)
    whole = shape_of((ending + 1, 1, rows, width), bf16)
    operands = [own, incoming, x_rows, gain, gain if ending else fresh, after]
    operands += (past if ending else []) + list(received)
    specs = [VMEM] * len(operands)
    specs[5] = ANY
    return pl.pallas_call(
        functools.partial(
            finish_kernel, ending, x_rows.shape[0] - 1 if incoming.ndim == 3 else 0, tick
        ),
        out_shape=whole if ending else (block, block),
        in_specs=specs,
        out_specs=VMEM if ending else (VMEM, VMEM),
        compiler_params=limit(2),
        name="finish",
    )(*operands)


def body(stash, w_in, w_out, gain, plan, arriving, fresh):
    ticks, rows = plan.shape[0], stash.shape[2]
    masks = range(2, lax.axis_size("tp"), 2)
    picked = pick(plan, stash)
    moved = from_mirror(picked)
    w_outs, token = load(w_out, 0, picked)
    packed = pack(moved, arriving, token)
    chips = [swapped(packed, mask) for mask in masks]
    w_ins, token = load(w_in, 1, packed)
    gathered = with_cores([packed, *tie(chips, token)])
    own, other = back(gathered, ticks, (gain,), w_outs, w_ins, 1024)
    incoming = packed
    results = []
    for tick in range(ticks):
        blocks = fold(own, swapped(other, 1), rows)
        received = [swapped(block, mask) for block, mask in zip(blocks[1:], masks)]
        if tick + 1 == ticks:
            return finish(blocks[0], received, incoming, packed, gain, None, tick, gain, results)
        half = PIECES // 2
        gates_a, token = gate(gathered, tick + 1, gain, w_ins[:half], 1024, blocks[0], w_outs)
        result, outgoing = finish(
            blocks[0], received, incoming, packed, gain, fresh, tick, token
        )
        results.append(result)
        chips = [from_above(outgoing, mask) for mask in [0, *masks]]
        gates_b, token = gate(gathered, tick + 1, gain, w_ins[half:], 1024, outgoing, w_outs)
        chips = tie(chips, token)
        incoming = chips[0]
        own, other = back(with_cores(list(chips)), ticks, (*gates_a, *gates_b), w_outs, w_ins, 1024)


def solution(mesh):
    placed = (
        P("section", None, "tp", None),
        P("section", None, "tp"),
        P("section", "tp", None),
        P("section", None),
        P(),
        P("section", "tp", None),
        P(None, "tp", None),
    )
    return jax.shard_map(
        body, mesh=mesh, in_specs=placed, out_specs=P(None, "section", "tp", None), check_vma=False
    )
```

profile of v0, /device:TPU:0, one launch (start us, length us, event | category | flops | bytes accessed | tf_op | source)
XLA Modules:
  0.0 114.8 jit_solution(9818484365630291336)
XLA Ops:
  0.0 1.6 %pick.1.after = bf16[3,24,1024]{2,1,0:T(8,128)(2,1)S(1)} custom-call(s32[3,4]{1,0:T(4,128)} %plan.1, bf16[1,4,24,1024]{3,2,1,0:T(8,128)(2,1)} %stash.1), custom_call_target="tpu_custom_call" | custom-call | tf_op jit(solution)/shard_map/pick/pallas_call | solution.py:74
  1.6 4.1 %collective-permute-start = (bf16[3,24,1024]{2,1,0:T(8,128)(2,1)S(1)}, bf16[3,24,1024]{2,1,0:T(8,128)(2,1)S(1)}, u32[]{:S(2)}, u32[]{:S(2)}) collective-permute-start(bf16[3,24,1024]{2,1,0:T(8,128)(2,1)S(1)} %pick.1.after), channel_id=1, source_target_pairs={{0,16},{8,24},{16,0},{24,8},{1,17},{9,25},{17,1},{25,9},{2,18},{10... | collective-permute-start | bytes 442376 | tf_op jit(solution)/shard_map/ppermute | solution.py:42
  5.7 5.9 %load.2 = (bf16[2048,1024]{1,0:T(8,128)(2,1)S(1)}, bf16[2048,1024]{1,0:T(8,128)(2,1)S(1)}, bf16[2048,1024]{1,0:T(8,128)(2,1)S(1)}, bf16[2048,1024]{1,0:T(8,128)(2,1)S(1)}, f32[8,128]{1,0:T(8,128)S(1)}) custom-call(bf16[1,8192,1024]{2,1,0:T(8,128)(2,1)} %weight.2, bf16[3,24,1024]{2,1,0:T(8,128)(2,1)S(1)} %pick.1.after), custom_call_target="tpu_custom_call" | custom-call | bytes 33554432 | tf_op jit(solution)/shard_map/load/pallas_call | solution.py:106
  11.6 1.1 collective-permute-done.many
  12.8 2.6 %collective-permute-start.3 = (bf16[4,24,1024]{2,1,0:T(8,128)(2,1)S(1)}, bf16[4,24,1024]{2,1,0:T(8,128)(2,1)S(1)}, u32[]{:S(2)}, u32[]{:S(2)}) collective-permute-start(bf16[4,24,1024]{2,1,0:T(8,128)(2,1)S(1)} %pack.1.after.refs_0_.refs_1_.refs_2_), channel_id=1, source_target_pairs={{0,6},{1,7},{2,4},{3,5},{4,2},{5,3},{6,0},{7,1},{8,14},{9,15},{10,... | collective-permute-start | bytes 589832 | tf_op jit(solution)/shard_map/ppermute | solution.py:37
  16.3 5.9 %load.3 = (bf16[1024,2048]{1,0:T(8,128)(2,1)S(1)}, bf16[1024,2048]{1,0:T(8,128)(2,1)S(1)}, bf16[1024,2048]{1,0:T(8,128)(2,1)S(1)}, bf16[1024,2048]{1,0:T(8,128)(2,1)S(1)}, f32[8,128]{1,0:T(8,128)S(1)}) custom-call(bf16[1,1024,8192]{2,1,0:T(8,128)(2,1)} %weight.3, bf16[4,24,1024]{2,1,0:T(8,128)(2,1)S(1)} %pack.1.after.refs_0_.refs_1_.refs_2_), custom_call_target="tpu_custom_call" | custom-call | bytes 33554432 | tf_op jit(solution)/shard_map/load/pallas_call | solution.py:106
  22.3 1.8 %collective-permute-done.2.refs_1_ = bf16[4,24,1024]{2,1,0:T(8,128)(2,1)S(1)} collective-permute-done((bf16[4,24,1024]{2,1,0:T(8,128)(2,1)S(1)}, bf16[4,24,1024]{2,1,0:T(8,128)(2,1)S(1)}, u32[]{:S(2)}, u32[]{:S(2)}) %collective-permute-start.2) | collective-permute-done | bytes 196640 | tf_op jit(solution)/shard_map/ppermute | solution.py:37
  26.0 13.5 %first.1 = (f32[96,1024]{1,0:T(8,128)S(1)}, bf16[96,1024]{1,0:T(8,128)(2,1)S(1)}) custom-call(bf16[4,24,1024]{2,1,0:T(8,128)(2,1)S(1)} %pack.1.after.refs_0_.refs_1_.refs_2_, bf16[4,24,1024]{2,1,0:T(8,128)(2,1)S(1)} %get-tuple-element.62.refs_1_, bf16[4,24,1024]{2,1,0:T(8,128)(2,1)S(1)} %get-tuple-element.63.refs_2_, ...), custom_call_target="tpu_custom_call" | custom-call | flops 9663676416 | bytes 36700160 | tf_op jit(solution)/shard_map/first/pallas_call | solution.py:253
  39.9 1.2 %collective-permute-done.8.received = bf16[96,1024]{1,0:T(8,128)(2,1)S(1)} collective-permute-done((bf16[96,1024]{1,0:T(8,128)(2,1)S(1)}, bf16[96,1024]{1,0:T(8,128)(2,1)S(1)}, u32[]{:S(2)}, u32[]{:S(2)}) %collective-permute-start.8) | collective-permute-done | bytes 196640 | tf_op jit(solution)/shard_map/ppermute | solution.py:37
  41.1 1.4 %collective-permute-start.9 = (bf16[24,1024]{1,0:T(8,128)(2,1)S(1)}, bf16[24,1024]{1,0:T(8,128)(2,1)S(1)}, u32[]{:S(2)}, u32[]{:S(2)}) collective-permute-start(bf16[24,1024]{1,0:T(8,128)(2,1)S(1)} %get-tuple-element.77), channel_id=1, source_target_pairs={{0,2},{1,3},{2,0},{3,1},{4,6},{5,7},{6,4},{7,5},{8,10},{9,11},{10,... | collective-permute-start | bytes 147464 | tf_op jit(solution)/shard_map/ppermute | solution.py:37
  42.5 0.9 collective-permute-start.10
  43.5 1.2 %collective-permute-start.11 = (bf16[24,1024]{1,0:T(8,128)(2,1)S(1)}, bf16[24,1024]{1,0:T(8,128)(2,1)S(1)}, u32[]{:S(2)}, u32[]{:S(2)}) collective-permute-start(bf16[24,1024]{1,0:T(8,128)(2,1)S(1)} %get-tuple-element.79), channel_id=1, source_target_pairs={{0,6},{1,7},{2,4},{3,5},{4,2},{5,3},{6,0},{7,1},{8,14},{9,15},{10,... | collective-permute-start | bytes 147464 | tf_op jit(solution)/shard_map/ppermute | solution.py:37
  44.7 3.1 %gate.4 = (bf16[2048,192]{1,0:T(8,128)(2,1)S(1)}, bf16[2048,192]{1,0:T(8,128)(2,1)S(1)}, f32[8,128]{1,0:T(8,128)S(1)}) custom-call(bf16[4,24,1024]{2,1,0:T(8,128)(2,1)S(1)} %pack.1.after.refs_0_.refs_1_.refs_2_, bf16[4,24,1024]{2,1,0:T(8,128)(2,1)S(1)} %get-tuple-element.62.refs_1_, bf16[4,24,1024]{2,1,0:T(8,128)(2,1)S(1)} %get-tuple-element.63.refs_2_, ...), custom_call_target="tpu_custom_call" | custom-call | flops 1610612736 | bytes 9961472 | tf_op jit(solution)/shard_map/gate/pallas_call | solution.py:202
  48.7 5.0 %collective-permute-start.15 = (bf16[24,1024]{1,0:T(8,128)(2,1)S(1)}, bf16[24,1024]{1,0:T(8,128)(2,1)S(1)}, u32[]{:S(2)}, u32[]{:S(2)}) collective-permute-start(bf16[24,1024]{1,0:T(8,128)(2,1)S(1)} %get-tuple-element.80.refs_11_), channel_id=1, source_target_pairs={{14,0},{15,1},{12,2},{13,3},{10,4},{11,5},{8,6},{9,7},{22,8},{23,9... | collective-permute-start | bytes 147464 | tf_op jit(solution)/shard_map/ppermute | solution.py:52
  53.8 1.1 collective-permute-start.13
  55.5 2.9 %gate.5 = (bf16[2048,192]{1,0:T(8,128)(2,1)S(1)}, bf16[2048,192]{1,0:T(8,128)(2,1)S(1)}, f32[8,128]{1,0:T(8,128)S(1)}) custom-call(bf16[4,24,1024]{2,1,0:T(8,128)(2,1)S(1)} %pack.1.after.refs_0_.refs_1_.refs_2_, bf16[4,24,1024]{2,1,0:T(8,128)(2,1)S(1)} %get-tuple-element.62.refs_1_, bf16[4,24,1024]{2,1,0:T(8,128)(2,1)S(1)} %get-tuple-element.63.refs_2_, ...), custom_call_target="tpu_custom_call" | custom-call | flops 1610612736 | bytes 9961472 | tf_op jit(solution)/shard_map/gate/pallas_call | solution.py:202
  61.6 11.1 %back.2 = (f32[96,1024]{1,0:T(8,128)S(1)}, bf16[96,1024]{1,0:T(8,128)(2,1)S(1)}) custom-call(bf16[24,1024]{1,0:T(8,128)(2,1)S(1)} %get-tuple-element.82.refs_0_.refs_1_, bf16[24,1024]{1,0:T(8,128)(2,1)S(1)} %get-tuple-element.83.refs_1_, bf16[24,1024]{1,0:T(8,128)(2,1)S(1)} %get-tuple-element.84.refs_2_, bf16[24,1024]{1,0:T(8,128)(2,1)S(1)} %get-tuple-element.85.refs_3_, ...), custom_call_target="tpu_custom_call" | custom-call | flops 6442450944 | bytes 36700160 | tf_op jit(solution)/shard_map/back/pallas_call | solution.py:253
  73.1 1.1 collective-permute-done.20.received
  74.3 1.0 collective-permute-start.21
  75.3 1.2 %collective-permute-start.22 = (bf16[24,1024]{1,0:T(8,128)(2,1)S(1)}, bf16[24,1024]{1,0:T(8,128)(2,1)S(1)}, u32[]{:S(2)}, u32[]{:S(2)}) collective-permute-start(bf16[24,1024]{1,0:T(8,128)(2,1)S(1)} %get-tuple-element.95), channel_id=1, source_target_pairs={{0,4},{1,5},{2,6},{3,7},{4,0},{5,1},{6,2},{7,3},{8,12},{9,13},{10,... | collective-permute-start | bytes 147464 | tf_op jit(solution)/shard_map/ppermute | solution.py:37
  76.4 1.4 %collective-permute-start.23 = (bf16[24,1024]{1,0:T(8,128)(2,1)S(1)}, bf16[24,1024]{1,0:T(8,128)(2,1)S(1)}, u32[]{:S(2)}, u32[]{:S(2)}) collective-permute-start(bf16[24,1024]{1,0:T(8,128)(2,1)S(1)} %get-tuple-element.96), channel_id=1, source_target_pairs={{0,6},{1,7},{2,4},{3,5},{4,2},{5,3},{6,0},{7,1},{8,14},{9,15},{10,... | collective-permute-start | bytes 147464 | tf_op jit(solution)/shard_map/ppermute | solution.py:37
  77.8 2.9 %gate.6 = (bf16[2048,192]{1,0:T(8,128)(2,1)S(1)}, bf16[2048,192]{1,0:T(8,128)(2,1)S(1)}, f32[8,128]{1,0:T(8,128)S(1)}) custom-call(bf16[4,24,1024]{2,1,0:T(8,128)(2,1)S(1)} %pack.1.after.refs_0_.refs_1_.refs_2_, bf16[4,24,1024]{2,1,0:T(8,128)(2,1)S(1)} %get-tuple-element.62.refs_1_, bf16[4,24,1024]{2,1,0:T(8,128)(2,1)S(1)} %get-tuple-element.63.refs_2_, ...), custom_call_target="tpu_custom_call" | custom-call | flops 1610612736 | bytes 9961472 | tf_op jit(solution)/shard_map/gate/pallas_call | solution.py:202
  81.6 4.0 %collective-permute-start.27 = (bf16[24,1024]{1,0:T(8,128)(2,1)S(1)}, bf16[24,1024]{1,0:T(8,128)(2,1)S(1)}, u32[]{:S(2)}, u32[]{:S(2)}) collective-permute-start(bf16[24,1024]{1,0:T(8,128)(2,1)S(1)} %get-tuple-element.97.refs_11_), channel_id=1, source_target_pairs={{14,0},{15,1},{12,2},{13,3},{10,4},{11,5},{8,6},{9,7},{22,8},{23,9... | collective-permute-start | bytes 147464 | tf_op jit(solution)/shard_map/ppermute | solution.py:52
  85.6 1.8 %collective-permute-start.26 = (bf16[24,1024]{1,0:T(8,128)(2,1)S(1)}, bf16[24,1024]{1,0:T(8,128)(2,1)S(1)}, u32[]{:S(2)}, u32[]{:S(2)}) collective-permute-start(bf16[24,1024]{1,0:T(8,128)(2,1)S(1)} %get-tuple-element.97.refs_11_), channel_id=1, source_target_pairs={{12,0},{13,1},{14,2},{15,3},{8,4},{9,5},{10,6},{11,7},{20,8},{21,9... | collective-permute-start | bytes 147464 | tf_op jit(solution)/shard_map/ppermute | solution.py:52
  88.4 2.9 %gate.7 = (bf16[2048,192]{1,0:T(8,128)(2,1)S(1)}, bf16[2048,192]{1,0:T(8,128)(2,1)S(1)}, f32[8,128]{1,0:T(8,128)S(1)}) custom-call(bf16[4,24,1024]{2,1,0:T(8,128)(2,1)S(1)} %pack.1.after.refs_0_.refs_1_.refs_2_, bf16[4,24,1024]{2,1,0:T(8,128)(2,1)S(1)} %get-tuple-element.62.refs_1_, bf16[4,24,1024]{2,1,0:T(8,128)(2,1)S(1)} %get-tuple-element.63.refs_2_, ...), custom_call_target="tpu_custom_call" | custom-call | flops 1610612736 | bytes 9961472 | tf_op jit(solution)/shard_map/gate/pallas_call | solution.py:202
  91.4 1.0 collective-permute-done.25.refs_1_
  94.3 11.1 %back.3 = (f32[96,1024]{1,0:T(8,128)S(1)}, bf16[96,1024]{1,0:T(8,128)(2,1)S(1)}) custom-call(bf16[24,1024]{1,0:T(8,128)(2,1)S(1)} %get-tuple-element.99.refs_0_.refs_1_, bf16[24,1024]{1,0:T(8,128)(2,1)S(1)} %get-tuple-element.100.refs_1_, bf16[24,1024]{1,0:T(8,128)(2,1)S(1)} %get-tuple-element.101.refs_2_, bf16[24,1024]{1,0:T(8,128)(2,1)S(1)} %get-tuple-element.102.refs_3_, ...), custom_call_target="tpu_custom_call" | custom-call | flops 6442450944 | bytes 36700160 | tf_op jit(solution)/shard_map/back/pallas_call | solution.py:253
  105.8 1.1 collective-permute-done.32.received
  106.9 1.2 %collective-permute-start.33 = (bf16[24,1024]{1,0:T(8,128)(2,1)S(1)}, bf16[24,1024]{1,0:T(8,128)(2,1)S(1)}, u32[]{:S(2)}, u32[]{:S(2)}) collective-permute-start(bf16[24,1024]{1,0:T(8,128)(2,1)S(1)} %get-tuple-element.112), channel_id=1, source_target_pairs={{0,2},{1,3},{2,0},{3,1},{4,6},{5,7},{6,4},{7,5},{8,10},{9,11},{10,... | collective-permute-start | bytes 147464 | tf_op jit(solution)/shard_map/ppermute | solution.py:37
  108.9 1.5 %collective-permute-start.35 = (bf16[24,1024]{1,0:T(8,128)(2,1)S(1)}, bf16[24,1024]{1,0:T(8,128)(2,1)S(1)}, u32[]{:S(2)}, u32[]{:S(2)}) collective-permute-start(bf16[24,1024]{1,0:T(8,128)(2,1)S(1)} %get-tuple-element.114), channel_id=1, source_target_pairs={{0,6},{1,7},{2,4},{3,5},{4,2},{5,3},{6,0},{7,1},{8,14},{9,15},{10,... | collective-permute-start | bytes 147464 | tf_op jit(solution)/shard_map/ppermute | solution.py:37
  111.1 1.1 collective-permute-done.34.refs_9_
  112.2 1.8 %collective-permute-done.35.refs_10_ = bf16[24,1024]{1,0:T(8,128)(2,1)S(1)} collective-permute-done((bf16[24,1024]{1,0:T(8,128)(2,1)S(1)}, bf16[24,1024]{1,0:T(8,128)(2,1)S(1)}, u32[]{:S(2)}, u32[]{:S(2)}) %collective-permute-start.35) | collective-permute-done | bytes 49184 | tf_op jit(solution)/shard_map/ppermute | solution.py:37
  (66 shorter events, 15.2 us)
Async XLA Ops:
  1.6 11.1 %collective-permute-start = (bf16[3,24,1024]{2,1,0:T(8,128)(2,1)S(1)}, bf16[3,24,1024]{2,1,0:T(8,128)(2,1)S(1)}, u32[]{:S(2)}, u32[]{:S(2)}) collective-permute-start(bf16[3,24,1024]{2,1,0:T(8,128)(2,1)S(1)} %pick.1.after), channel_id=1, source_target_pairs={{0,16},{8,24},{16,0},{24,8},{1,17},{9,25},{17,1},{25,9},{2,18},{10... | collective-permute-start | bytes 442376 | tf_op jit(solution)/shard_map/ppermute | solution.py:42
  12.8 9.5 %collective-permute-start.3 = (bf16[4,24,1024]{2,1,0:T(8,128)(2,1)S(1)}, bf16[4,24,1024]{2,1,0:T(8,128)(2,1)S(1)}, u32[]{:S(2)}, u32[]{:S(2)}) collective-permute-start(bf16[4,24,1024]{2,1,0:T(8,128)(2,1)S(1)} %pack.1.after.refs_0_.refs_1_.refs_2_), channel_id=1, source_target_pairs={{0,6},{1,7},{2,4},{3,5},{4,2},{5,3},{6,0},{7,1},{8,14},{9,15},{10,... | collective-permute-start | bytes 589832 | tf_op jit(solution)/shard_map/ppermute | solution.py:37
  15.3 8.7 %collective-permute-start.2 = (bf16[4,24,1024]{2,1,0:T(8,128)(2,1)S(1)}, bf16[4,24,1024]{2,1,0:T(8,128)(2,1)S(1)}, u32[]{:S(2)}, u32[]{:S(2)}) collective-permute-start(bf16[4,24,1024]{2,1,0:T(8,128)(2,1)S(1)} %pack.1.after.refs_0_.refs_1_.refs_2_), channel_id=1, source_target_pairs={{0,4},{1,5},{2,6},{3,7},{4,0},{5,1},{6,2},{7,3},{8,12},{9,13},{10,... | collective-permute-start | bytes 589832 | tf_op jit(solution)/shard_map/ppermute | solution.py:37
  15.8 8.2 %collective-permute-start.1 = (bf16[4,24,1024]{2,1,0:T(8,128)(2,1)S(1)}, bf16[4,24,1024]{2,1,0:T(8,128)(2,1)S(1)}, u32[]{:S(2)}, u32[]{:S(2)}) collective-permute-start(bf16[4,24,1024]{2,1,0:T(8,128)(2,1)S(1)} %pack.1.after.refs_0_.refs_1_.refs_2_), channel_id=1, source_target_pairs={{0,2},{1,3},{2,0},{3,1},{4,6},{5,7},{6,4},{7,5},{8,10},{9,11},{10,... | collective-permute-start | bytes 589832 | tf_op jit(solution)/shard_map/ppermute | solution.py:37
  16.3 8.3 %collective-permute-start.4 = (bf16[4,24,1024]{2,1,0:T(8,128)(2,1)S(1)}, bf16[4,24,1024]{2,1,0:T(8,128)(2,1)S(1)}, u32[]{:S(2)}, u32[]{:S(2)}) collective-permute-start(bf16[4,24,1024]{2,1,0:T(8,128)(2,1)S(1)} %pack.1.after.refs_0_.refs_1_.refs_2_), channel_id=1, source_target_pairs={{0,1},{1,0},{2,3},{3,2},{4,5},{5,4},{6,7},{7,6},{8,9},{9,8},{10,11... | collective-permute-start | bytes 589832 | tf_op jit(solution)/shard_map/ppermute | solution.py:37
  24.0 1.4 %collective-permute-start.5 = (bf16[4,24,1024]{2,1,0:T(8,128)(2,1)S(1)}, bf16[4,24,1024]{2,1,0:T(8,128)(2,1)S(1)}, u32[]{:S(2)}, u32[]{:S(2)}) collective-permute-start(bf16[4,24,1024]{2,1,0:T(8,128)(2,1)S(1)} %get-tuple-element.62.refs_1_), channel_id=1, source_target_pairs={{0,1},{1,0},{2,3},{3,2},{4,5},{5,4},{6,7},{7,6},{8,9},{9,8},{10,11... | collective-permute-start | bytes 589832 | tf_op jit(solution)/shard_map/ppermute | solution.py:37
  24.0 1.7 %collective-permute-start.6 = (bf16[4,24,1024]{2,1,0:T(8,128)(2,1)S(1)}, bf16[4,24,1024]{2,1,0:T(8,128)(2,1)S(1)}, u32[]{:S(2)}, u32[]{:S(2)}) collective-permute-start(bf16[4,24,1024]{2,1,0:T(8,128)(2,1)S(1)} %get-tuple-element.63.refs_2_), channel_id=1, source_target_pairs={{0,1},{1,0},{2,3},{3,2},{4,5},{5,4},{6,7},{7,6},{8,9},{9,8},{10,11... | collective-permute-start | bytes 589832 | tf_op jit(solution)/shard_map/ppermute | solution.py:37
  24.6 1.5 %collective-permute-start.7 = (bf16[4,24,1024]{2,1,0:T(8,128)(2,1)S(1)}, bf16[4,24,1024]{2,1,0:T(8,128)(2,1)S(1)}, u32[]{:S(2)}, u32[]{:S(2)}) collective-permute-start(bf16[4,24,1024]{2,1,0:T(8,128)(2,1)S(1)} %get-tuple-element.64.refs_3_), channel_id=1, source_target_pairs={{0,1},{1,0},{2,3},{3,2},{4,5},{5,4},{6,7},{7,6},{8,9},{9,8},{10,11... | collective-permute-start | bytes 589832 | tf_op jit(solution)/shard_map/ppermute | solution.py:37
  39.6 1.5 %collective-permute-start.8 = (bf16[96,1024]{1,0:T(8,128)(2,1)S(1)}, bf16[96,1024]{1,0:T(8,128)(2,1)S(1)}, u32[]{:S(2)}, u32[]{:S(2)}) collective-permute-start(bf16[96,1024]{1,0:T(8,128)(2,1)S(1)} %get-tuple-element.74), channel_id=1, source_target_pairs={{0,1},{1,0},{2,3},{3,2},{4,5},{5,4},{6,7},{7,6},{8,9},{9,8},{10,11... | collective-permute-start | bytes 589832 | tf_op jit(solution)/shard_map/ppermute | solution.py:37
  41.1 6.7 %collective-permute-start.9 = (bf16[24,1024]{1,0:T(8,128)(2,1)S(1)}, bf16[24,1024]{1,0:T(8,128)(2,1)S(1)}, u32[]{:S(2)}, u32[]{:S(2)}) collective-permute-start(bf16[24,1024]{1,0:T(8,128)(2,1)S(1)} %get-tuple-element.77), channel_id=1, source_target_pairs={{0,2},{1,3},{2,0},{3,1},{4,6},{5,7},{6,4},{7,5},{8,10},{9,11},{10,... | collective-permute-start | bytes 147464 | tf_op jit(solution)/shard_map/ppermute | solution.py:37
  42.5 5.2 %collective-permute-start.10 = (bf16[24,1024]{1,0:T(8,128)(2,1)S(1)}, bf16[24,1024]{1,0:T(8,128)(2,1)S(1)}, u32[]{:S(2)}, u32[]{:S(2)}) collective-permute-start(bf16[24,1024]{1,0:T(8,128)(2,1)S(1)} %get-tuple-element.78), channel_id=1, source_target_pairs={{0,4},{1,5},{2,6},{3,7},{4,0},{5,1},{6,2},{7,3},{8,12},{9,13},{10,... | collective-permute-start | bytes 147464 | tf_op jit(solution)/shard_map/ppermute | solution.py:37
  43.5 5.0 %collective-permute-start.11 = (bf16[24,1024]{1,0:T(8,128)(2,1)S(1)}, bf16[24,1024]{1,0:T(8,128)(2,1)S(1)}, u32[]{:S(2)}, u32[]{:S(2)}) collective-permute-start(bf16[24,1024]{1,0:T(8,128)(2,1)S(1)} %get-tuple-element.79), channel_id=1, source_target_pairs={{0,6},{1,7},{2,4},{3,5},{4,2},{5,3},{6,0},{7,1},{8,14},{9,15},{10,... | collective-permute-start | bytes 147464 | tf_op jit(solution)/shard_map/ppermute | solution.py:37
  48.7 9.7 %collective-permute-start.15 = (bf16[24,1024]{1,0:T(8,128)(2,1)S(1)}, bf16[24,1024]{1,0:T(8,128)(2,1)S(1)}, u32[]{:S(2)}, u32[]{:S(2)}) collective-permute-start(bf16[24,1024]{1,0:T(8,128)(2,1)S(1)} %get-tuple-element.80.refs_11_), channel_id=1, source_target_pairs={{14,0},{15,1},{12,2},{13,3},{10,4},{11,5},{8,6},{9,7},{22,8},{23,9... | collective-permute-start | bytes 147464 | tf_op jit(solution)/shard_map/ppermute | solution.py:52
  53.7 5.0 %collective-permute-start.14 = (bf16[24,1024]{1,0:T(8,128)(2,1)S(1)}, bf16[24,1024]{1,0:T(8,128)(2,1)S(1)}, u32[]{:S(2)}, u32[]{:S(2)}) collective-permute-start(bf16[24,1024]{1,0:T(8,128)(2,1)S(1)} %get-tuple-element.80.refs_11_), channel_id=1, source_target_pairs={{12,0},{13,1},{14,2},{15,3},{8,4},{9,5},{10,6},{11,7},{20,8},{21,9... | collective-permute-start | bytes 147464 | tf_op jit(solution)/shard_map/ppermute | solution.py:52
  53.8 5.6 %collective-permute-start.13 = (bf16[24,1024]{1,0:T(8,128)(2,1)S(1)}, bf16[24,1024]{1,0:T(8,128)(2,1)S(1)}, u32[]{:S(2)}, u32[]{:S(2)}) collective-permute-start(bf16[24,1024]{1,0:T(8,128)(2,1)S(1)} %get-tuple-element.80.refs_11_), channel_id=1, source_target_pairs={{10,0},{11,1},{8,2},{9,3},{14,4},{15,5},{12,6},{13,7},{18,8},{19,9... | collective-permute-start | bytes 147464 | tf_op jit(solution)/shard_map/ppermute | solution.py:52
  54.9 4.8 %collective-permute-start.12 = (bf16[24,1024]{1,0:T(8,128)(2,1)S(1)}, bf16[24,1024]{1,0:T(8,128)(2,1)S(1)}, u32[]{:S(2)}, u32[]{:S(2)}) collective-permute-start(bf16[24,1024]{1,0:T(8,128)(2,1)S(1)} %get-tuple-element.80.refs_11_), channel_id=1, source_target_pairs={{8,0},{9,1},{10,2},{11,3},{12,4},{13,5},{14,6},{15,7},{16,8},{17,9... | collective-permute-start | bytes 147464 | tf_op jit(solution)/shard_map/ppermute | solution.py:52
  59.7 1.4 %collective-permute-start.18 = (bf16[24,1024]{1,0:T(8,128)(2,1)S(1)}, bf16[24,1024]{1,0:T(8,128)(2,1)S(1)}, u32[]{:S(2)}, u32[]{:S(2)}) collective-permute-start(bf16[24,1024]{1,0:T(8,128)(2,1)S(1)} %get-tuple-element.84.refs_2_), channel_id=1, source_target_pairs={{0,1},{1,0},{2,3},{3,2},{4,5},{5,4},{6,7},{7,6},{8,9},{9,8},{10,11... | collective-permute-start | bytes 147464 | tf_op jit(solution)/shard_map/ppermute | solution.py:37
  60.2 1.4 %collective-permute-start.16 = (bf16[24,1024]{1,0:T(8,128)(2,1)S(1)}, bf16[24,1024]{1,0:T(8,128)(2,1)S(1)}, u32[]{:S(2)}, u32[]{:S(2)}) collective-permute-start(bf16[24,1024]{1,0:T(8,128)(2,1)S(1)} %get-tuple-element.82.refs_0_.refs_1_), channel_id=1, source_target_pairs={{0,1},{1,0},{2,3},{3,2},{4,5},{5,4},{6,7},{7,6},{8,9},{9,8},{10,11... | collective-permute-start | bytes 147464 | tf_op jit(solution)/shard_map/ppermute | solution.py:37
  72.7 1.5 %collective-permute-start.20 = (bf16[96,1024]{1,0:T(8,128)(2,1)S(1)}, bf16[96,1024]{1,0:T(8,128)(2,1)S(1)}, u32[]{:S(2)}, u32[]{:S(2)}) collective-permute-start(bf16[96,1024]{1,0:T(8,128)(2,1)S(1)} %get-tuple-element.91), channel_id=1, source_target_pairs={{0,1},{1,0},{2,3},{3,2},{4,5},{5,4},{6,7},{7,6},{8,9},{9,8},{10,11... | collective-permute-start | bytes 589832 | tf_op jit(solution)/shard_map/ppermute | solution.py:37
  74.3 6.5 %collective-permute-start.21 = (bf16[24,1024]{1,0:T(8,128)(2,1)S(1)}, bf16[24,1024]{1,0:T(8,128)(2,1)S(1)}, u32[]{:S(2)}, u32[]{:S(2)}) collective-permute-start(bf16[24,1024]{1,0:T(8,128)(2,1)S(1)} %get-tuple-element.94), channel_id=1, source_target_pairs={{0,2},{1,3},{2,0},{3,1},{4,6},{5,7},{6,4},{7,5},{8,10},{9,11},{10,... | collective-permute-start | bytes 147464 | tf_op jit(solution)/shard_map/ppermute | solution.py:37
  75.3 5.5 %collective-permute-start.22 = (bf16[24,1024]{1,0:T(8,128)(2,1)S(1)}, bf16[24,1024]{1,0:T(8,128)(2,1)S(1)}, u32[]{:S(2)}, u32[]{:S(2)}) collective-permute-start(bf16[24,1024]{1,0:T(8,128)(2,1)S(1)} %get-tuple-element.95), channel_id=1, source_target_pairs={{0,4},{1,5},{2,6},{3,7},{4,0},{5,1},{6,2},{7,3},{8,12},{9,13},{10,... | collective-permute-start | bytes 147464 | tf_op jit(solution)/shard_map/ppermute | solution.py:37
  76.4 5.0 %collective-permute-start.23 = (bf16[24,1024]{1,0:T(8,128)(2,1)S(1)}, bf16[24,1024]{1,0:T(8,128)(2,1)S(1)}, u32[]{:S(2)}, u32[]{:S(2)}) collective-permute-start(bf16[24,1024]{1,0:T(8,128)(2,1)S(1)} %get-tuple-element.96), channel_id=1, source_target_pairs={{0,6},{1,7},{2,4},{3,5},{4,2},{5,3},{6,0},{7,1},{8,14},{9,15},{10,... | collective-permute-start | bytes 147464 | tf_op jit(solution)/shard_map/ppermute | solution.py:37
  81.6 9.7 %collective-permute-start.27 = (bf16[24,1024]{1,0:T(8,128)(2,1)S(1)}, bf16[24,1024]{1,0:T(8,128)(2,1)S(1)}, u32[]{:S(2)}, u32[]{:S(2)}) collective-permute-start(bf16[24,1024]{1,0:T(8,128)(2,1)S(1)} %get-tuple-element.97.refs_11_), channel_id=1, source_target_pairs={{14,0},{15,1},{12,2},{13,3},{10,4},{11,5},{8,6},{9,7},{22,8},{23,9... | collective-permute-start | bytes 147464 | tf_op jit(solution)/shard_map/ppermute | solution.py:52
  85.6 5.8 %collective-permute-start.26 = (bf16[24,1024]{1,0:T(8,128)(2,1)S(1)}, bf16[24,1024]{1,0:T(8,128)(2,1)S(1)}, u32[]{:S(2)}, u32[]{:S(2)}) collective-permute-start(bf16[24,1024]{1,0:T(8,128)(2,1)S(1)} %get-tuple-element.97.refs_11_), channel_id=1, source_target_pairs={{12,0},{13,1},{14,2},{15,3},{8,4},{9,5},{10,6},{11,7},{20,8},{21,9... | collective-permute-start | bytes 147464 | tf_op jit(solution)/shard_map/ppermute | solution.py:52
  87.4 5.0 %collective-permute-start.25 = (bf16[24,1024]{1,0:T(8,128)(2,1)S(1)}, bf16[24,1024]{1,0:T(8,128)(2,1)S(1)}, u32[]{:S(2)}, u32[]{:S(2)}) collective-permute-start(bf16[24,1024]{1,0:T(8,128)(2,1)S(1)} %get-tuple-element.97.refs_11_), channel_id=1, source_target_pairs={{10,0},{11,1},{8,2},{9,3},{14,4},{15,5},{12,6},{13,7},{18,8},{19,9... | collective-permute-start | bytes 147464 | tf_op jit(solution)/shard_map/ppermute | solution.py:52
  88.3 4.1 %collective-permute-start.24 = (bf16[24,1024]{1,0:T(8,128)(2,1)S(1)}, bf16[24,1024]{1,0:T(8,128)(2,1)S(1)}, u32[]{:S(2)}, u32[]{:S(2)}) collective-permute-start(bf16[24,1024]{1,0:T(8,128)(2,1)S(1)} %get-tuple-element.97.refs_11_), channel_id=1, source_target_pairs={{8,0},{9,1},{10,2},{11,3},{12,4},{13,5},{14,6},{15,7},{16,8},{17,9... | collective-permute-start | bytes 147464 | tf_op jit(solution)/shard_map/ppermute | solution.py:52
  92.4 1.4 %collective-permute-start.30 = (bf16[24,1024]{1,0:T(8,128)(2,1)S(1)}, bf16[24,1024]{1,0:T(8,128)(2,1)S(1)}, u32[]{:S(2)}, u32[]{:S(2)}) collective-permute-start(bf16[24,1024]{1,0:T(8,128)(2,1)S(1)} %get-tuple-element.101.refs_2_), channel_id=1, source_target_pairs={{0,1},{1,0},{2,3},{3,2},{4,5},{5,4},{6,7},{7,6},{8,9},{9,8},{10,11... | collective-permute-start | bytes 147464 | tf_op jit(solution)/shard_map/ppermute | solution.py:37
  93.0 1.3 %collective-permute-start.28 = (bf16[24,1024]{1,0:T(8,128)(2,1)S(1)}, bf16[24,1024]{1,0:T(8,128)(2,1)S(1)}, u32[]{:S(2)}, u32[]{:S(2)}) collective-permute-start(bf16[24,1024]{1,0:T(8,128)(2,1)S(1)} %get-tuple-element.99.refs_0_.refs_1_), channel_id=1, source_target_pairs={{0,1},{1,0},{2,3},{3,2},{4,5},{5,4},{6,7},{7,6},{8,9},{9,8},{10,11... | collective-permute-start | bytes 147464 | tf_op jit(solution)/shard_map/ppermute | solution.py:37
  105.4 1.5 %collective-permute-start.32 = (bf16[96,1024]{1,0:T(8,128)(2,1)S(1)}, bf16[96,1024]{1,0:T(8,128)(2,1)S(1)}, u32[]{:S(2)}, u32[]{:S(2)}) collective-permute-start(bf16[96,1024]{1,0:T(8,128)(2,1)S(1)} %get-tuple-element.108), channel_id=1, source_target_pairs={{0,1},{1,0},{2,3},{3,2},{4,5},{5,4},{6,7},{7,6},{8,9},{9,8},{10,11... | collective-permute-start | bytes 589832 | tf_op jit(solution)/shard_map/ppermute | solution.py:37
  106.9 4.2 %collective-permute-start.33 = (bf16[24,1024]{1,0:T(8,128)(2,1)S(1)}, bf16[24,1024]{1,0:T(8,128)(2,1)S(1)}, u32[]{:S(2)}, u32[]{:S(2)}) collective-permute-start(bf16[24,1024]{1,0:T(8,128)(2,1)S(1)} %get-tuple-element.112), channel_id=1, source_target_pairs={{0,2},{1,3},{2,0},{3,1},{4,6},{5,7},{6,4},{7,5},{8,10},{9,11},{10,... | collective-permute-start | bytes 147464 | tf_op jit(solution)/shard_map/ppermute | solution.py:37
  108.1 4.1 %collective-permute-start.34 = (bf16[24,1024]{1,0:T(8,128)(2,1)S(1)}, bf16[24,1024]{1,0:T(8,128)(2,1)S(1)}, u32[]{:S(2)}, u32[]{:S(2)}) collective-permute-start(bf16[24,1024]{1,0:T(8,128)(2,1)S(1)} %get-tuple-element.113), channel_id=1, source_target_pairs={{0,4},{1,5},{2,6},{3,7},{4,0},{5,1},{6,2},{7,3},{8,12},{9,13},{10,... | collective-permute-start | bytes 147464 | tf_op jit(solution)/shard_map/ppermute | solution.py:37
  108.9 5.0 %collective-permute-start.35 = (bf16[24,1024]{1,0:T(8,128)(2,1)S(1)}, bf16[24,1024]{1,0:T(8,128)(2,1)S(1)}, u32[]{:S(2)}, u32[]{:S(2)}) collective-permute-start(bf16[24,1024]{1,0:T(8,128)(2,1)S(1)} %get-tuple-element.114), channel_id=1, source_target_pairs={{0,6},{1,7},{2,4},{3,5},{4,2},{5,3},{6,0},{7,1},{8,14},{9,15},{10,... | collective-permute-start | bytes 147464 | tf_op jit(solution)/shard_map/ppermute | solution.py:37
  (7 other events, 33.2 us)
where the time goes:
time: 115 us
  Pallas kernels  62.3 us (54%)
  starting transfers between devices  35.7 us (31%)
  waiting for transfers between devices  16.6 us (14%)
    pallas_call x3, Pallas kernels, back(): pl.pallas_call(functools.partial(back_kernel, len(blocks), chunk, ticks),...  35.7 us
    ppermute x27, starting transfers between devices, swapped(): lax.ppermute(value, 'tp', [(i, i ^ mask) for i in range(lax.axis_size('tp...  18 us
    ppermute x8, starting transfers between devices, from_above(): return lax.ppermute(value, ('section', 'tp'), pairs)  13.6 us
    ppermute x27, waiting for transfers between devices, swapped(): lax.ppermute(value, 'tp', [(i, i ^ mask) for i in range(lax.axis_size('tp...  13.2 us
    pallas_call x4, Pallas kernels, gate(): pl.pallas_call(functools.partial(gate_kernel, len(blocks), at, pieces, ch...  11.8 us
    pallas_call x2, Pallas kernels, load(): pl.pallas_call(functools.partial(load_kernel, axis), out_shape=(*[piece]...  11.8 us
    ppermute x1, starting transfers between devices, from_mirror(): lax.ppermute(value, 'section', [(i, (i + count // 2) % count) for i in ra...  4.1 us
  transfers between devices with their start and end apart: 36, of which 25 were waited for; matrix products, arithmetic and copies ran while one was open for 0% of the time, Pallas kernels for 21%

commit v1 on v0

--- a/solution.py
+++ b/solution.py
@@ -77,7 +77,7 @@
         in_specs=[SMEM, HBM],
         out_specs=VMEM,
         scratch_shapes=[pltpu.SemaphoreType.DMA((ticks,))],
-        compiler_params=limit(2),
+        compiler_params=limit(6),
         name="pick",
     )(in_hbm(plan), in_hbm(stash))
 
@@ -96,7 +96,7 @@
         copy.wait()
 
 
-PIECES = 4
+PIECES = 8
 
 
 def load(weight, axis, after):
@@ -109,7 +109,7 @@
         in_specs=[HBM, ANY],
         out_specs=tuple([VMEM] * (PIECES + 1)),
         scratch_shapes=[pltpu.SemaphoreType.DMA((PIECES,))],
-        compiler_params=limit(2),
+        compiler_params=limit(6),
         cost_estimate=pl.CostEstimate(
             flops=0, bytes_accessed=4 * PIECES * shape[0] * shape[1], transcendentals=0
         ),
@@ -147,13 +147,17 @@
         out_shape=shape_of((count + 1, *block), many.dtype),
         in_specs=[VMEM, VMEM, ANY],
         out_specs=VMEM,
-        compiler_params=limit(2),
+        compiler_params=limit(6),
         name="pack",
     )(many, one, after)
 
 
 def joined(blocks, at):
     return jnp.concatenate([block[at].astype(f32) for block in blocks], axis=0)
+
+
+def joined_pairs(blocks):
+    return jnp.concatenate([block[at].astype(f32) for block in blocks for at in (0, 1)], axis=0)
 
 
 def kernel_blocks(blocks):
@@ -204,7 +208,7 @@
         out_shape=(*[pltpu.VMEM((hidden, tokens), bf16)] * pieces, shape_of((8, 128), f32)),
         in_specs=[VMEM] * (len(blocks) + 1 + pieces) + [ANY] * (1 + len(kept)),
         out_specs=tuple([VMEM] * (pieces + 1)),
-        compiler_params=limit(4),
+        compiler_params=limit(6),
         cost_estimate=pl.CostEstimate(
             flops=2 * tokens * width * hidden * pieces,
             bytes_accessed=(2 * width + 2 * tokens) * hidden * pieces,
@@ -221,7 +225,8 @@
     paired = len(extra) == 1
     if paired:
         inputs = (normalised(joined(blocks, 0))[1] * extra[0][...]).astype(bf16)
-    incoming = joined(blocks, ticks if paired else ...).T.astype(bf16)
+    incoming = joined(blocks, ticks) if paired else joined_pairs(blocks)
+    incoming = incoming.T.astype(bf16)
     total = None
     for half, (w_out, w_in) in enumerate(zip(w_outs, w_ins)):
         for part in spans(w_out.shape[0], chunk):
@@ -243,9 +248,9 @@
     paired = len(extra) == 1
     if paired:
         blocks = kernel_blocks(blocks)
-    elif blocks[0].shape[0] % 8:
-        blocks = [jnp.concatenate(blocks, axis=0)]
-    tokens = sum(block.shape[-2] for block in blocks)
+    elif blocks[0].shape[1] % 8:
+        blocks = [joined_pairs(blocks).astype(bf16).reshape(2, -1, blocks[0].shape[2])]
+    tokens = sum(block.shape[-2] for block in blocks) * (1 if paired else 2)
     width, hidden = w_ins[0].shape
     hidden *= PIECES
     extra = extra if paired else [in_vmem(part) for part in extra]
@@ -258,7 +263,7 @@
         ),
         in_specs=[VMEM] * len(operands),
         out_specs=(VMEM, VMEM),
-        compiler_params=limit(8 if paired else 6),
+        compiler_params=limit(6),
         cost_estimate=pl.CostEstimate(
             flops=(6 if paired else 4) * tokens * width * hidden,
             bytes_accessed=4 * width * hidden + 2 * tokens * hidden,
@@ -268,80 +273,97 @@
     )(*operands)
 
 
-def fold_values(own, received, rows):
+def fold_values(own, received, rows, near):
     sums = own + received.astype(f32)
-    return [sums[:rows]] + [
-        sums[at : at + rows].astype(bf16) for at in range(rows, sums.shape[0], rows)
-    ]
-
-
-def fold_kernel(rows, own, received, *outs):
-    for out, value in zip(outs, fold_values(own[...], received[...], rows)):
+    blocks = [sums[at : at + rows] for at in range(0, sums.shape[0], rows)]
+    if not near:
+        return blocks[:1] + [block.astype(bf16) for block in blocks[1:]]
+    pairs = [jnp.stack([blocks[at], blocks[at ^ 1]]) for at in range(len(blocks))]
+    return pairs[:1] + [pair.astype(bf16) for pair in pairs[1:]]
+
+
+def fold_kernel(rows, near, own, received, *outs):
+    for out, value in zip(outs, fold_values(own[...], received[...], rows, near)):
         out[...] = value
 
 
-def fold(own, received, rows):
+def fold(own, received, rows, near):
     if rows % 8:
-        return fold_values(own, received, rows)
+        return fold_values(own, received, rows, near)
     half, width = own.shape
-    return pl.pallas_call(
-        functools.partial(fold_kernel, rows),
-        out_shape=tuple(
-            shape_of((rows, width), bf16 if at else f32) for at in range(half // rows)
-        ),
+    shape = (2, rows, width) if near else (rows, width)
+    return pl.pallas_call(
+        functools.partial(fold_kernel, rows, near),
+        out_shape=tuple(shape_of(shape, bf16 if at else f32) for at in range(half // rows)),
         in_specs=[VMEM] * 2,
         out_specs=tuple([VMEM] * (half // rows)),
-        compiler_params=limit(2),
+        compiler_params=limit(6),
         name="fold",
     )(own, received)
 
 
-def finish_kernel(ending, ticks, tick, *refs):
-    own, incoming, x_rows, gain, extra, _ = refs[:6]
-    received, outs = (refs[6:-1], refs[-1:]) if ending else (refs[6:-2], refs[-2:])
-    if ending:
-        past, received = received[:ending], received[ending:]
-    total = own[...]
+def finished(own, received, incoming, x_rows, gain):
+    total = own
     for block in received:
-        total = total + block[...].astype(f32)
-    inverse_rms, normed = normalised(x_rows[tick].astype(f32))
-    scaled = total * gain[...]
+        total = total + block.astype(f32)
+    inverse_rms, normed = normalised(x_rows.astype(f32))
+    scaled = total * gain
     inner = jnp.mean(scaled * normed, axis=-1, keepdims=True)
-    incoming_rows = incoming[ticks] if ticks else incoming[...]
-    result = (incoming_rows.astype(f32) + inverse_rms * (scaled - normed * inner)).astype(bf16)
-    if ending:
-        for before in range(ending):
-            outs[0][before, 0] = past[before][...]
-        outs[0][ending, 0] = result
-    else:
-        outs[0][...] = result
-        outs[1][...] = jnp.where(lax.axis_index("section") == 0, extra[tick], result)
-
-
-def finish(own, received, incoming, x_rows, gain, fresh, tick, after, past=None):
-    rows, width = own.shape
-    ending = 0 if past is None else len(past)
-    block = shape_of((rows, width), bf16)
-    whole = shape_of((ending + 1, 1, rows, width), bf16)
-    operands = [own, incoming, x_rows, gain, gain if ending else fresh, after]
-    operands += (past if ending else []) + list(received)
-    specs = [VMEM] * len(operands)
-    specs[5] = ANY
-    return pl.pallas_call(
-        functools.partial(
-            finish_kernel, ending, x_rows.shape[0] - 1 if incoming.ndim == 3 else 0, tick
-        ),
-        out_shape=whole if ending else (block, block),
-        in_specs=specs,
-        out_specs=VMEM if ending else (VMEM, VMEM),
-        compiler_params=limit(2),
+    return (incoming.astype(f32) + inverse_rms * (scaled - normed * inner)).astype(bf16)
+
+
+def finish_kernel(count, tick, paired, x_own, x_near, gain, fresh, fresh_near, *refs):
+    (incoming, own, *received), (_, result, outgoing) = refs[:count], refs[count:]
+    for at, (x_rows, extra) in enumerate(((x_own, fresh), (x_near, fresh_near))):
+        rows = (x_own, x_near)[at][x_own.shape[0] - 1] if paired else incoming[at]
+        value = finished(
+            own[at], [block[at] for block in received], rows, x_rows[tick], gain[...]
+        )
+        if at == 0:
+            result[...] = value
+        outgoing[at] = jnp.where(lax.axis_index("section") == 0, extra[tick], value)
+
+
+def finish(own, received, incoming, gathered, gain, fresh, fresh_near, tick, after):
+    pair, rows, width = own.shape
+    paired = incoming.ndim == 3 and incoming.shape[0] != pair
+    operands = [gathered[0], gathered[1], gain, fresh, fresh_near, incoming, own, *received]
+    return pl.pallas_call(
+        functools.partial(finish_kernel, 2 + len(received), tick, paired),
+        out_shape=(shape_of((rows, width), bf16), shape_of((pair, rows, width), bf16)),
+        in_specs=[VMEM] * len(operands) + [ANY],
+        out_specs=(VMEM, VMEM),
+        compiler_params=limit(6),
         name="finish",
+    )(*operands, after)
+
+
+def end_kernel(count, x_own, gain, incoming, own, *refs):
+    received, (*past, out) = refs[:count], refs[count:]
+    for before, value in enumerate(past):
+        out[before, 0] = value[...]
+    received = [block[...] for block in received]
+    out[len(past), 0] = finished(
+        own[...], received, incoming[0], x_own[len(past)], gain[...]
+    )
+
+
+def end(own, received, incoming, x_own, gain, past):
+    operands = [x_own, gain, incoming, own, *received, *past]
+    return pl.pallas_call(
+        functools.partial(end_kernel, len(received)),
+        out_shape=shape_of((len(past) + 1, 1, *own.shape), bf16),
+        in_specs=[VMEM] * len(operands),
+        out_specs=VMEM,
+        compiler_params=limit(6),
+        name="end",
     )(*operands)
 
 
 def body(stash, w_in, w_out, gain, plan, arriving, fresh):
     ticks, rows = plan.shape[0], stash.shape[2]
-    masks = range(2, lax.axis_size("tp"), 2)
+    parts = lax.axis_size("tp")
+    masks = range(2, parts, 2)
     picked = pick(plan, stash)
     moved = from_mirror(picked)
     w_outs, token = load(w_out, 0, picked)
@@ -349,25 +371,27 @@
     chips = [swapped(packed, mask) for mask in masks]
     w_ins, token = load(w_in, 1, packed)
     gathered = with_cores([packed, *tie(chips, token)])
-    own, other = back(gathered, ticks, (gain,), w_outs, w_ins, 1024)
+    fresh_near = swapped(fresh, 2)
+    own, other = back(gathered, ticks, (gain,), w_outs, w_ins, 512)
     incoming = packed
     results = []
     for tick in range(ticks):
-        blocks = fold(own, swapped(other, 1), rows)
+        last = tick + 1 == ticks
+        blocks = fold(own, swapped(other, 1), rows, not last)
         received = [swapped(block, mask) for block, mask in zip(blocks[1:], masks)]
-        if tick + 1 == ticks:
-            return finish(blocks[0], received, incoming, packed, gain, None, tick, gain, results)
+        if last:
+            return end(blocks[0], received, incoming, packed, gain, results)
         half = PIECES // 2
         gates_a, token = gate(gathered, tick + 1, gain, w_ins[:half], 1024, blocks[0], w_outs)
         result, outgoing = finish(
-            blocks[0], received, incoming, packed, gain, fresh, tick, token
+            blocks[0], received, incoming, gathered, gain, fresh, fresh_near, tick, token
         )
         results.append(result)
-        chips = [from_above(outgoing, mask) for mask in [0, *masks]]
+        came = [from_above(outgoing, mask) for mask in range(0, parts, 4)]
         gates_b, token = gate(gathered, tick + 1, gain, w_ins[half:], 1024, outgoing, w_outs)
-        chips = tie(chips, token)
-        incoming = chips[0]
-        own, other = back(with_cores(list(chips)), ticks, (*gates_a, *gates_b), w_outs, w_ins, 1024)
+        halves = with_cores(list(tie(came, token)))
+        incoming = halves[0]
+        own, other = back(halves, ticks, (*gates_a, *gates_b), w_outs, w_ins, 512)
 
 
 def solution(mesh):

time: 115 us -> 110 us (0.957)
  Pallas kernels: 62.3 us -> 56 us
  waiting for transfers between devices: 16.6 us -> 22.5 us
  starting transfers between devices: 35.7 us -> 30.8 us
    ppermute x8 -> x4, starting transfers between devices: 13.6 us -> 8.4 us  [from_above(): return lax.ppermute(value, ('section', 'tp'), pairs)]
    pallas_call x4, Pallas kernels: 11.8 us -> 8.04 us  [gate(): pl.pallas_call(functools.partial(gate_kernel, len(blocks), at, pieces, ch...]
    ppermute x27 -> x24, waiting for transfers between devices: 13.2 us -> 16.4 us  [swapped(): lax.ppermute(value, 'tp', [(i, i ^ mask) for i in range(lax.axis_size('tp...]
    ppermute x8 -> x4, waiting for transfers between devices: 2.29 us -> 5.01 us  [from_above(): return lax.ppermute(value, ('section', 'tp'), pairs)]
    pallas_call x3, Pallas kernels: 35.7 us -> 33 us  [back(): pl.pallas_call(functools.partial(back_kernel, len(blocks), chunk, ticks),...]
    ppermute x27 -> x24, starting transfers between devices: 18 us -> 18.3 us  [swapped(): lax.ppermute(value, 'tp', [(i, i ^ mask) for i in range(lax.axis_size('tp...]
  transfers between devices with their start and end apart: 36 -> 29, of which waited for: 25 -> 20; matrix products, arithmetic and copies ran while one was open for 0% -> 0% of each run, Pallas kernels for 21% -> 18%
where the time goes in v1:
time: 110 us
  Pallas kernels  56 us (51%)
  starting transfers between devices  30.8 us (28%)
  waiting for transfers between devices  22.5 us (20%)
    pallas_call x3, Pallas kernels, back(): pl.pallas_call(functools.partial(back_kernel, len(blocks), chunk, ticks),...  33 us
    ppermute x24, starting transfers between devices, swapped(): lax.ppermute(value, 'tp', [(i, i ^ mask) for i in range(lax.axis_size('tp...  18.3 us
    ppermute x24, waiting for transfers between devices, swapped(): lax.ppermute(value, 'tp', [(i, i ^ mask) for i in range(lax.axis_size('tp...  16.4 us
    pallas_call x2, Pallas kernels, load(): pl.pallas_call(functools.partial(load_kernel, axis), out_shape=(*[piece]...  11.9 us
    ppermute x4, starting transfers between devices, from_above(): return lax.ppermute(value, ('section', 'tp'), pairs)  8.4 us
    pallas_call x4, Pallas kernels, gate(): pl.pallas_call(functools.partial(gate_kernel, len(blocks), at, pieces, ch...  8.04 us
    ppermute x4, waiting for transfers between devices, from_above(): return lax.ppermute(value, ('section', 'tp'), pairs)  5.01 us
    ppermute x1, starting transfers between devices, from_mirror(): lax.ppermute(value, 'section', [(i, (i + count // 2) % count) for i in ra...  4.1 us
  transfers between devices with their start and end apart: 29, of which 20 were waited for; matrix products, arithmetic and copies ran while one was open for 0% of the time, Pallas kernels for 18%

profile of v1, /device:TPU:0, one launch (start us, length us, event | category | flops | bytes accessed | tf_op | source)
XLA Modules:
  0.0 109.5 jit_solution(5542485725351239118)
XLA Ops:
  0.0 1.6 %pick.1.after = bf16[3,24,1024]{2,1,0:T(8,128)(2,1)S(1)} custom-call(s32[3,4]{1,0:T(4,128)} %plan.1, bf16[1,4,24,1024]{3,2,1,0:T(8,128)(2,1)} %stash.1), custom_call_target="tpu_custom_call" | custom-call | tf_op jit(solution)/shard_map/pick/pallas_call | solution.py:74
  1.6 4.1 %collective-permute-start = (bf16[3,24,1024]{2,1,0:T(8,128)(2,1)S(1)}, bf16[3,24,1024]{2,1,0:T(8,128)(2,1)S(1)}, u32[]{:S(2)}, u32[]{:S(2)}) collective-permute-start(bf16[3,24,1024]{2,1,0:T(8,128)(2,1)S(1)} %pick.1.after), channel_id=1, source_target_pairs={{0,16},{8,24},{16,0},{24,8},{1,17},{9,25},{17,1},{25,9},{2,18},{10... | collective-permute-start | bytes 442376 | tf_op jit(solution)/shard_map/ppermute | solution.py:42
  5.7 5.9 %load.2 = (bf16[1024,1024]{1,0:T(8,128)(2,1)S(1)}, bf16[1024,1024]{1,0:T(8,128)(2,1)S(1)}, bf16[1024,1024]{1,0:T(8,128)(2,1)S(1)}, bf16[1024,1024]{1,0:T(8,128)(...) custom-call(bf16[1,8192,1024]{2,1,0:T(8,128)(2,1)} %weight.2, ...), custom_call_target="tpu_custom_call" | custom-call | bytes 33554432 | tf_op jit(solution)/shard_map/load/pallas_call | solution.py:106
  11.7 1.1 collective-permute-done.many
  12.8 2.6 %collective-permute-start.3 = (bf16[4,24,1024]{2,1,0:T(8,128)(2,1)S(1)}, bf16[4,24,1024]{2,1,0:T(8,128)(2,1)S(1)}, u32[]{:S(2)}, u32[]{:S(2)}) collective-permute-start(bf16[4,24,1024]{2,1,0:T(8,128)(2,1)S(1)} %pack.1.after.refs_0_.x_own), channel_id=1, source_target_pairs={{0,6},{1,7},{2,4},{3,5},{4,2},{5,3},{6,0},{7,1},{8,14},{9,15},{10,... | collective-permute-start | bytes 589832 | tf_op jit(solution)/shard_map/ppermute | solution.py:37
  16.3 6.0 %load.3 = (bf16[1024,1024]{1,0:T(8,128)(2,1)S(1)}, bf16[1024,1024]{1,0:T(8,128)(2,1)S(1)}, bf16[1024,1024]{1,0:T(8,128)(2,1)S(1)}, bf16[1024,1024]{1,0:T(8,128)(...) custom-call(bf16[1,1024,8192]{2,1,0:T(8,128)(2,1)} %weight.3, ...), custom_call_target="tpu_custom_call" | custom-call | bytes 33554432 | tf_op jit(solution)/shard_map/load/pallas_call | solution.py:106
  22.3 1.7 %collective-permute-done.2.refs_1_ = bf16[4,24,1024]{2,1,0:T(8,128)(2,1)S(1)} collective-permute-done((bf16[4,24,1024]{2,1,0:T(8,128)(2,1)S(1)}, bf16[4,24,1024]{2,1,0:T(8,128)(2,1)S(1)}, u32[]{:S(2)}, u32[]{:S(2)}) %collective-permute-start.2) | collective-permute-done | bytes 196640 | tf_op jit(solution)/shard_map/ppermute | solution.py:37
  26.0 13.6 %first.1 = (f32[96,1024]{1,0:T(8,128)S(1)}, bf16[96,1024]{1,0:T(8,128)(2,1)S(1)}) custom-call(bf16[4,24,1024]{2,1,0:T(8,128)(2,1)S(1)} %pack.1.after.refs_0_.x_own, bf16[4,24,1024]{2,1,0:T(8,128)(2,1)S(1)} %get-tuple-element.74.refs_1_.x_near, bf16[4,24,1024]{2,1,0:T(8,128)(2,1)S(1)} %get-tuple-element.75.refs_2_, ...), custom_call_target="tpu_custom_call" | custom-call | flops 9663676416 | bytes 36700160 | tf_op jit(solution)/shard_map/first/pallas_call | solution.py:258
  39.9 1.4 %collective-permute-start.4 = (bf16[2,24,1024]{2,1,0:T(8,128)(2,1)S(1)}, bf16[2,24,1024]{2,1,0:T(8,128)(2,1)S(1)}, u32[]{:S(2)}, u32[]{:S(2)}) collective-permute-start(bf16[2,24,1024]{2,1,0:T(8,128)(2,1)S(1)} %copy-done), channel_id=1, source_target_pairs={{0,2},{1,3},{2,0},{3,1},{4,6},{5,7},{6,4},{7,5},{8,10},{9,11},{10,... | collective-permute-start | bytes 294920 | tf_op jit(solution)/shard_map/ppermute | solution.py:37
  41.3 1.3 %collective-permute-start.10 = (bf16[2,24,1024]{2,1,0:T(8,128)(2,1)S(1)}, bf16[2,24,1024]{2,1,0:T(8,128)(2,1)S(1)}, u32[]{:S(2)}, u32[]{:S(2)}) collective-permute-start(bf16[2,24,1024]{2,1,0:T(8,128)(2,1)S(1)} %get-tuple-element.96), channel_id=1, source_target_pairs={{0,2},{1,3},{2,0},{3,1},{4,6},{5,7},{6,4},{7,5},{8,10},{9,11},{10,... | collective-permute-start | bytes 294920 | tf_op jit(solution)/shard_map/ppermute | solution.py:37
  42.6 0.9 collective-permute-start.11
  43.5 1.3 %collective-permute-start.12 = (bf16[2,24,1024]{2,1,0:T(8,128)(2,1)S(1)}, bf16[2,24,1024]{2,1,0:T(8,128)(2,1)S(1)}, u32[]{:S(2)}, u32[]{:S(2)}) collective-permute-start(bf16[2,24,1024]{2,1,0:T(8,128)(2,1)S(1)} %get-tuple-element.98), channel_id=1, source_target_pairs={{0,6},{1,7},{2,4},{3,5},{4,2},{5,3},{6,0},{7,1},{8,14},{9,15},{10,... | collective-permute-start | bytes 294920 | tf_op jit(solution)/shard_map/ppermute | solution.py:37
  44.9 2.0 %gate.4 = (bf16[1024,192]{1,0:T(8,128)(2,1)S(1)}, bf16[1024,192]{1,0:T(8,128)(2,1)S(1)}, bf16[1024,192]{1,0:T(8,128)(2,1)S(1)}, bf16[1024,192]{1,0:T(8,128)(2,1)S(1)}, f32[8,128]{1,0:T(8,128)S(1)}) custom-call(bf16[4,24,1024]{2,1,0:T(8,128)(2,1)S(1)} %pack.1.after.refs_0_.x_own, bf16[4,24,1024]{2,1,0:T(8,128)(2,1)S(1)} %get-tuple-element.74.refs_1_.x_near, ...), custom_call_target="tpu_custom_call" | custom-call | flops 1610612736 | bytes 9961472 | tf_op jit(solution)/shard_map/gate/pallas_call | solution.py:206
  47.6 2.2 %collective-permute-done.12.refs_4_ = bf16[2,24,1024]{2,1,0:T(8,128)(2,1)S(1)} collective-permute-done((bf16[2,24,1024]{2,1,0:T(8,128)(2,1)S(1)}, bf16[2,24,1024]{2,1,0:T(8,128)(2,1)S(1)}, u32[]{:S(2)}, u32[]{:S(2)}) %collective-permute-start.12) | collective-permute-done | bytes 98336 | tf_op jit(solution)/shard_map/ppermute | solution.py:37
  50.1 4.6 %collective-permute-start.14 = (bf16[2,24,1024]{2,1,0:T(8,128)(2,1)S(1)}, bf16[2,24,1024]{2,1,0:T(8,128)(2,1)S(1)}, u32[]{:S(2)}, u32[]{:S(2)}) collective-permute-start(bf16[2,24,1024]{2,1,0:T(8,128)(2,1)S(1)} %get-tuple-element.100.refs_13_), channel_id=1, source_target_pairs={{12,0},{13,1},{14,2},{15,3},{8,4},{9,5},{10,6},{11,7},{20,8},{21,9... | collective-permute-start | bytes 294920 | tf_op jit(solution)/shard_map/ppermute | solution.py:52
  54.7 2.0 %gate.5 = (bf16[1024,192]{1,0:T(8,128)(2,1)S(1)}, bf16[1024,192]{1,0:T(8,128)(2,1)S(1)}, bf16[1024,192]{1,0:T(8,128)(2,1)S(1)}, bf16[1024,192]{1,0:T(8,128)(2,1)S(1)}, f32[8,128]{1,0:T(8,128)S(1)}) custom-call(bf16[4,24,1024]{2,1,0:T(8,128)(2,1)S(1)} %pack.1.after.refs_0_.x_own, bf16[4,24,1024]{2,1,0:T(8,128)(2,1)S(1)} %get-tuple-element.74.refs_1_.x_near, ...), custom_call_target="tpu_custom_call" | custom-call | flops 1610612736 | bytes 9961472 | tf_op jit(solution)/shard_map/gate/pallas_call | solution.py:206
  57.3 2.0 %collective-permute-done.13.refs_0_ = bf16[2,24,1024]{2,1,0:T(8,128)(2,1)S(1)} collective-permute-done((bf16[2,24,1024]{2,1,0:T(8,128)(2,1)S(1)}, bf16[2,24,1024]{2,1,0:T(8,128)(2,1)S(1)}, u32[]{:S(2)}, u32[]{:S(2)}) %collective-permute-start.13) | collective-permute-done | bytes 98336 | tf_op jit(solution)/shard_map/ppermute | solution.py:52
  60.7 9.7 %back.2 = (f32[96,1024]{1,0:T(8,128)S(1)}, bf16[96,1024]{1,0:T(8,128)(2,1)S(1)}) custom-call(bf16[2,24,1024]{2,1,0:T(8,128)(2,1)S(1)} %get-tuple-element.102.refs_0_, bf16[2,24,1024]{2,1,0:T(8,128)(2,1)S(1)} %get-tuple-element.103.refs_1_, bf16[2,24,1024]{2,1,0:T(8,128)(2,1)S(1)} %collective-permute-done.15.refs_2_, ...), custom_call_target="tpu_custom_call" | custom-call | flops 6442450944 | bytes 36700160 | tf_op jit(solution)/shard_map/back/pallas_call | solution.py:258
  70.9 1.1 collective-permute-done.17.received
  72.0 1.6 %collective-permute-start.18 = (bf16[2,24,1024]{2,1,0:T(8,128)(2,1)S(1)}, bf16[2,24,1024]{2,1,0:T(8,128)(2,1)S(1)}, u32[]{:S(2)}, u32[]{:S(2)}) collective-permute-start(bf16[2,24,1024]{2,1,0:T(8,128)(2,1)S(1)} %get-tuple-element.115), channel_id=1, source_target_pairs={{0,2},{1,3},{2,0},{3,1},{4,6},{5,7},{6,4},{7,5},{8,10},{9,11},{10,... | collective-permute-start | bytes 294920 | tf_op jit(solution)/shard_map/ppermute | solution.py:37
  74.3 1.3 %collective-permute-start.20 = (bf16[2,24,1024]{2,1,0:T(8,128)(2,1)S(1)}, bf16[2,24,1024]{2,1,0:T(8,128)(2,1)S(1)}, u32[]{:S(2)}, u32[]{:S(2)}) collective-permute-start(bf16[2,24,1024]{2,1,0:T(8,128)(2,1)S(1)} %get-tuple-element.117), channel_id=1, source_target_pairs={{0,6},{1,7},{2,4},{3,5},{4,2},{5,3},{6,0},{7,1},{8,14},{9,15},{10,... | collective-permute-start | bytes 294920 | tf_op jit(solution)/shard_map/ppermute | solution.py:37
  75.6 2.0 %gate.6 = (bf16[1024,192]{1,0:T(8,128)(2,1)S(1)}, bf16[1024,192]{1,0:T(8,128)(2,1)S(1)}, bf16[1024,192]{1,0:T(8,128)(2,1)S(1)}, bf16[1024,192]{1,0:T(8,128)(2,1)S(1)}, f32[8,128]{1,0:T(8,128)S(1)}) custom-call(bf16[4,24,1024]{2,1,0:T(8,128)(2,1)S(1)} %pack.1.after.refs_0_.x_own, bf16[4,24,1024]{2,1,0:T(8,128)(2,1)S(1)} %get-tuple-element.74.refs_1_.x_near, ...), custom_call_target="tpu_custom_call" | custom-call | flops 1610612736 | bytes 9961472 | tf_op jit(solution)/shard_map/gate/pallas_call | solution.py:206
  77.6 2.9 %collective-permute-done.19.refs_3_ = bf16[2,24,1024]{2,1,0:T(8,128)(2,1)S(1)} collective-permute-done((bf16[2,24,1024]{2,1,0:T(8,128)(2,1)S(1)}, bf16[2,24,1024]{2,1,0:T(8,128)(2,1)S(1)}, u32[]{:S(2)}, u32[]{:S(2)}) %collective-permute-start.19) | collective-permute-done | bytes 98336 | tf_op jit(solution)/shard_map/ppermute | solution.py:37
  80.7 3.7 %collective-permute-start.22 = (bf16[2,24,1024]{2,1,0:T(8,128)(2,1)S(1)}, bf16[2,24,1024]{2,1,0:T(8,128)(2,1)S(1)}, u32[]{:S(2)}, u32[]{:S(2)}) collective-permute-start(bf16[2,24,1024]{2,1,0:T(8,128)(2,1)S(1)} %get-tuple-element.119.refs_13_), channel_id=1, source_target_pairs={{12,0},{13,1},{14,2},{15,3},{8,4},{9,5},{10,6},{11,7},{20,8},{21,9... | collective-permute-start | bytes 294920 | tf_op jit(solution)/shard_map/ppermute | solution.py:52
  84.5 2.0 %gate.7 = (bf16[1024,192]{1,0:T(8,128)(2,1)S(1)}, bf16[1024,192]{1,0:T(8,128)(2,1)S(1)}, bf16[1024,192]{1,0:T(8,128)(2,1)S(1)}, bf16[1024,192]{1,0:T(8,128)(2,1)S(1)}, f32[8,128]{1,0:T(8,128)S(1)}) custom-call(bf16[4,24,1024]{2,1,0:T(8,128)(2,1)S(1)} %pack.1.after.refs_0_.x_own, bf16[4,24,1024]{2,1,0:T(8,128)(2,1)S(1)} %get-tuple-element.74.refs_1_.x_near, ...), custom_call_target="tpu_custom_call" | custom-call | flops 1610612736 | bytes 9961472 | tf_op jit(solution)/shard_map/gate/pallas_call | solution.py:206
  86.5 2.4 %collective-permute-done.21.refs_0_ = bf16[2,24,1024]{2,1,0:T(8,128)(2,1)S(1)} collective-permute-done((bf16[2,24,1024]{2,1,0:T(8,128)(2,1)S(1)}, bf16[2,24,1024]{2,1,0:T(8,128)(2,1)S(1)}, u32[]{:S(2)}, u32[]{:S(2)}) %collective-permute-start.21) | collective-permute-done | bytes 98336 | tf_op jit(solution)/shard_map/ppermute | solution.py:52
  90.4 9.7 %back.3 = (f32[96,1024]{1,0:T(8,128)S(1)}, bf16[96,1024]{1,0:T(8,128)(2,1)S(1)}) custom-call(bf16[2,24,1024]{2,1,0:T(8,128)(2,1)S(1)} %get-tuple-element.121.refs_0_.incoming, bf16[2,24,1024]{2,1,0:T(8,128)(2,1)S(1)} %get-tuple-element.122.refs_1_, bf16[2,24,1024]{2,1,0:T(8,128)(2,1)S(1)} %collective-permute-done.23.refs_2_, ...), custom_call_target="tpu_custom_call" | custom-call | flops 6442450944 | bytes 36700160 | tf_op jit(solution)/shard_map/back/pallas_call | solution.py:258
  100.5 1.1 collective-permute-done.25.received
  101.7 1.3 %collective-permute-start.26 = (bf16[24,1024]{1,0:T(8,128)(2,1)S(1)}, bf16[24,1024]{1,0:T(8,128)(2,1)S(1)}, u32[]{:S(2)}, u32[]{:S(2)}) collective-permute-start(bf16[24,1024]{1,0:T(8,128)(2,1)S(1)} %get-tuple-element.134), channel_id=1, source_target_pairs={{0,2},{1,3},{2,0},{3,1},{4,6},{5,7},{6,4},{7,5},{8,10},{9,11},{10,... | collective-permute-start | bytes 147464 | tf_op jit(solution)/shard_map/ppermute | solution.py:37
  103.7 1.6 %collective-permute-start.28 = (bf16[24,1024]{1,0:T(8,128)(2,1)S(1)}, bf16[24,1024]{1,0:T(8,128)(2,1)S(1)}, u32[]{:S(2)}, u32[]{:S(2)}) collective-permute-start(bf16[24,1024]{1,0:T(8,128)(2,1)S(1)} %get-tuple-element.136), channel_id=1, source_target_pairs={{0,6},{1,7},{2,4},{3,5},{4,2},{5,3},{6,0},{7,1},{8,14},{9,15},{10,... | collective-permute-start | bytes 147464 | tf_op jit(solution)/shard_map/ppermute | solution.py:37
  105.9 1.8 %collective-permute-done.27.refs_1_ = bf16[24,1024]{1,0:T(8,128)(2,1)S(1)} collective-permute-done((bf16[24,1024]{1,0:T(8,128)(2,1)S(1)}, bf16[24,1024]{1,0:T(8,128)(2,1)S(1)}, u32[]{:S(2)}, u32[]{:S(2)}) %collective-permute-start.27) | collective-permute-done | bytes 49184 | tf_op jit(solution)/shard_map/ppermute | solution.py:37
  107.6 1.0 collective-permute-done.28.refs_2_
  (52 shorter events, 12.0 us)
Async XLA Ops:
  1.6 11.1 %copy-start.2 = (bf16[1,24,1024]{2,1,0:T(8,128)(2,1)S(1)}, bf16[1,24,1024]{2,1,0:T(8,128)(2,1)}, u32[]{:S(2)}) copy-start(bf16[1,24,1024]{2,1,0:T(8,128)(2,1)} %one.1) | copy-start | bytes 147460
  1.6 11.1 %collective-permute-start = (bf16[3,24,1024]{2,1,0:T(8,128)(2,1)S(1)}, bf16[3,24,1024]{2,1,0:T(8,128)(2,1)S(1)}, u32[]{:S(2)}, u32[]{:S(2)}) collective-permute-start(bf16[3,24,1024]{2,1,0:T(8,128)(2,1)S(1)} %pick.1.after), channel_id=1, source_target_pairs={{0,16},{8,24},{16,0},{24,8},{1,17},{9,25},{17,1},{25,9},{2,18},{10... | collective-permute-start | bytes 442376 | tf_op jit(solution)/shard_map/ppermute | solution.py:42
  12.8 13.3 %copy-start.1 = (f32[1,1024]{1,0:T(1,128)S(1)}, f32[1,1024]{1,0:T(1,128)}, u32[]{:S(2)}) copy-start(f32[1,1024]{1,0:T(1,128)} %gain.5) | copy-start | bytes 12292
  12.8 9.5 %collective-permute-start.3 = (bf16[4,24,1024]{2,1,0:T(8,128)(2,1)S(1)}, bf16[4,24,1024]{2,1,0:T(8,128)(2,1)S(1)}, u32[]{:S(2)}, u32[]{:S(2)}) collective-permute-start(bf16[4,24,1024]{2,1,0:T(8,128)(2,1)S(1)} %pack.1.after.refs_0_.x_own), channel_id=1, source_target_pairs={{0,6},{1,7},{2,4},{3,5},{4,2},{5,3},{6,0},{7,1},{8,14},{9,15},{10,... | collective-permute-start | bytes 589832 | tf_op jit(solution)/shard_map/ppermute | solution.py:37
  15.3 8.7 %collective-permute-start.2 = (bf16[4,24,1024]{2,1,0:T(8,128)(2,1)S(1)}, bf16[4,24,1024]{2,1,0:T(8,128)(2,1)S(1)}, u32[]{:S(2)}, u32[]{:S(2)}) collective-permute-start(bf16[4,24,1024]{2,1,0:T(8,128)(2,1)S(1)} %pack.1.after.refs_0_.x_own), channel_id=1, source_target_pairs={{0,4},{1,5},{2,6},{3,7},{4,0},{5,1},{6,2},{7,3},{8,12},{9,13},{10,... | collective-permute-start | bytes 589832 | tf_op jit(solution)/shard_map/ppermute | solution.py:37
  15.8 8.2 %collective-permute-start.1 = (bf16[4,24,1024]{2,1,0:T(8,128)(2,1)S(1)}, bf16[4,24,1024]{2,1,0:T(8,128)(2,1)S(1)}, u32[]{:S(2)}, u32[]{:S(2)}) collective-permute-start(bf16[4,24,1024]{2,1,0:T(8,128)(2,1)S(1)} %pack.1.after.refs_0_.x_own), channel_id=1, source_target_pairs={{0,2},{1,3},{2,0},{3,1},{4,6},{5,7},{6,4},{7,5},{8,10},{9,11},{10,... | collective-permute-start | bytes 589832 | tf_op jit(solution)/shard_map/ppermute | solution.py:37
  16.3 8.3 %collective-permute-start.5 = (bf16[4,24,1024]{2,1,0:T(8,128)(2,1)S(1)}, bf16[4,24,1024]{2,1,0:T(8,128)(2,1)S(1)}, u32[]{:S(2)}, u32[]{:S(2)}) collective-permute-start(bf16[4,24,1024]{2,1,0:T(8,128)(2,1)S(1)} %pack.1.after.refs_0_.x_own), channel_id=1, source_target_pairs={{0,1},{1,0},{2,3},{3,2},{4,5},{5,4},{6,7},{7,6},{8,9},{9,8},{10,11... | collective-permute-start | bytes 589832 | tf_op jit(solution)/shard_map/ppermute | solution.py:37
  24.0 1.4 %collective-permute-start.7 = (bf16[4,24,1024]{2,1,0:T(8,128)(2,1)S(1)}, bf16[4,24,1024]{2,1,0:T(8,128)(2,1)S(1)}, u32[]{:S(2)}, u32[]{:S(2)}) collective-permute-start(bf16[4,24,1024]{2,1,0:T(8,128)(2,1)S(1)} %get-tuple-element.75.refs_2_), channel_id=1, source_target_pairs={{0,1},{1,0},{2,3},{3,2},{4,5},{5,4},{6,7},{7,6},{8,9},{9,8},{10,11... | collective-permute-start | bytes 589832 | tf_op jit(solution)/shard_map/ppermute | solution.py:37
  24.0 1.7 %collective-permute-start.8 = (bf16[4,24,1024]{2,1,0:T(8,128)(2,1)S(1)}, bf16[4,24,1024]{2,1,0:T(8,128)(2,1)S(1)}, u32[]{:S(2)}, u32[]{:S(2)}) collective-permute-start(bf16[4,24,1024]{2,1,0:T(8,128)(2,1)S(1)} %get-tuple-element.76.refs_3_), channel_id=1, source_target_pairs={{0,1},{1,0},{2,3},{3,2},{4,5},{5,4},{6,7},{7,6},{8,9},{9,8},{10,11... | collective-permute-start | bytes 589832 | tf_op jit(solution)/shard_map/ppermute | solution.py:37
  24.5 1.5 %collective-permute-start.6 = (bf16[4,24,1024]{2,1,0:T(8,128)(2,1)S(1)}, bf16[4,24,1024]{2,1,0:T(8,128)(2,1)S(1)}, u32[]{:S(2)}, u32[]{:S(2)}) collective-permute-start(bf16[4,24,1024]{2,1,0:T(8,128)(2,1)S(1)} %get-tuple-element.74.refs_1_.x_near), channel_id=1, source_target_pairs={{0,1},{1,0},{2,3},{3,2},{4,5},{5,4},{6,7},{7,6},{8,9},{9,8},{10,11... | collective-permute-start | bytes 589832 | tf_op jit(solution)/shard_map/ppermute | solution.py:37
  26.0 13.9 %copy-start = (bf16[2,24,1024]{2,1,0:T(8,128)(2,1)S(1)}, bf16[2,24,1024]{2,1,0:T(8,128)(2,1)}, u32[]{:S(2)}) copy-start(bf16[2,24,1024]{2,1,0:T(8,128)(2,1)} %fresh.3) | copy-start | bytes 294916
  39.6 1.7 %collective-permute-start.9 = (bf16[96,1024]{1,0:T(8,128)(2,1)S(1)}, bf16[96,1024]{1,0:T(8,128)(2,1)S(1)}, u32[]{:S(2)}, u32[]{:S(2)}) collective-permute-start(bf16[96,1024]{1,0:T(8,128)(2,1)S(1)} %get-tuple-element.94), channel_id=1, source_target_pairs={{0,1},{1,0},{2,3},{3,2},{4,5},{5,4},{6,7},{7,6},{8,9},{9,8},{10,11... | collective-permute-start | bytes 589832 | tf_op jit(solution)/shard_map/ppermute | solution.py:37
  39.9 7.0 %collective-permute-start.4 = (bf16[2,24,1024]{2,1,0:T(8,128)(2,1)S(1)}, bf16[2,24,1024]{2,1,0:T(8,128)(2,1)S(1)}, u32[]{:S(2)}, u32[]{:S(2)}) collective-permute-start(bf16[2,24,1024]{2,1,0:T(8,128)(2,1)S(1)} %copy-done), channel_id=1, source_target_pairs={{0,2},{1,3},{2,0},{3,1},{4,6},{5,7},{6,4},{7,5},{8,10},{9,11},{10,... | collective-permute-start | bytes 294920 | tf_op jit(solution)/shard_map/ppermute | solution.py:37
  41.3 6.3 %collective-permute-start.10 = (bf16[2,24,1024]{2,1,0:T(8,128)(2,1)S(1)}, bf16[2,24,1024]{2,1,0:T(8,128)(2,1)S(1)}, u32[]{:S(2)}, u32[]{:S(2)}) collective-permute-start(bf16[2,24,1024]{2,1,0:T(8,128)(2,1)S(1)} %get-tuple-element.96), channel_id=1, source_target_pairs={{0,2},{1,3},{2,0},{3,1},{4,6},{5,7},{6,4},{7,5},{8,10},{9,11},{10,... | collective-permute-start | bytes 294920 | tf_op jit(solution)/shard_map/ppermute | solution.py:37
  42.6 5.0 %collective-permute-start.11 = (bf16[2,24,1024]{2,1,0:T(8,128)(2,1)S(1)}, bf16[2,24,1024]{2,1,0:T(8,128)(2,1)S(1)}, u32[]{:S(2)}, u32[]{:S(2)}) collective-permute-start(bf16[2,24,1024]{2,1,0:T(8,128)(2,1)S(1)} %get-tuple-element.97), channel_id=1, source_target_pairs={{0,4},{1,5},{2,6},{3,7},{4,0},{5,1},{6,2},{7,3},{8,12},{9,13},{10,... | collective-permute-start | bytes 294920 | tf_op jit(solution)/shard_map/ppermute | solution.py:37
  43.5 6.3 %collective-permute-start.12 = (bf16[2,24,1024]{2,1,0:T(8,128)(2,1)S(1)}, bf16[2,24,1024]{2,1,0:T(8,128)(2,1)S(1)}, u32[]{:S(2)}, u32[]{:S(2)}) collective-permute-start(bf16[2,24,1024]{2,1,0:T(8,128)(2,1)S(1)} %get-tuple-element.98), channel_id=1, source_target_pairs={{0,6},{1,7},{2,4},{3,5},{4,2},{5,3},{6,0},{7,1},{8,14},{9,15},{10,... | collective-permute-start | bytes 294920 | tf_op jit(solution)/shard_map/ppermute | solution.py:37
  50.1 7.2 %collective-permute-start.14 = (bf16[2,24,1024]{2,1,0:T(8,128)(2,1)S(1)}, bf16[2,24,1024]{2,1,0:T(8,128)(2,1)S(1)}, u32[]{:S(2)}, u32[]{:S(2)}) collective-permute-start(bf16[2,24,1024]{2,1,0:T(8,128)(2,1)S(1)} %get-tuple-element.100.refs_13_), channel_id=1, source_target_pairs={{12,0},{13,1},{14,2},{15,3},{8,4},{9,5},{10,6},{11,7},{20,8},{21,9... | collective-permute-start | bytes 294920 | tf_op jit(solution)/shard_map/ppermute | solution.py:52
  54.7 4.6 %collective-permute-start.13 = (bf16[2,24,1024]{2,1,0:T(8,128)(2,1)S(1)}, bf16[2,24,1024]{2,1,0:T(8,128)(2,1)S(1)}, u32[]{:S(2)}, u32[]{:S(2)}) collective-permute-start(bf16[2,24,1024]{2,1,0:T(8,128)(2,1)S(1)} %get-tuple-element.100.refs_13_), channel_id=1, source_target_pairs={{8,0},{9,1},{10,2},{11,3},{12,4},{13,5},{14,6},{15,7},{16,8},{17,9... | collective-permute-start | bytes 294920 | tf_op jit(solution)/shard_map/ppermute | solution.py:52
  59.3 1.3 %collective-permute-start.16 = (bf16[2,24,1024]{2,1,0:T(8,128)(2,1)S(1)}, bf16[2,24,1024]{2,1,0:T(8,128)(2,1)S(1)}, u32[]{:S(2)}, u32[]{:S(2)}) collective-permute-start(bf16[2,24,1024]{2,1,0:T(8,128)(2,1)S(1)} %get-tuple-element.103.refs_1_), channel_id=1, source_target_pairs={{0,1},{1,0},{2,3},{3,2},{4,5},{5,4},{6,7},{7,6},{8,9},{9,8},{10,11... | collective-permute-start | bytes 294920 | tf_op jit(solution)/shard_map/ppermute | solution.py:37
  59.3 1.5 %collective-permute-start.15 = (bf16[2,24,1024]{2,1,0:T(8,128)(2,1)S(1)}, bf16[2,24,1024]{2,1,0:T(8,128)(2,1)S(1)}, u32[]{:S(2)}, u32[]{:S(2)}) collective-permute-start(bf16[2,24,1024]{2,1,0:T(8,128)(2,1)S(1)} %get-tuple-element.102.refs_0_), channel_id=1, source_target_pairs={{0,1},{1,0},{2,3},{3,2},{4,5},{5,4},{6,7},{7,6},{8,9},{9,8},{10,11... | collective-permute-start | bytes 294920 | tf_op jit(solution)/shard_map/ppermute | solution.py:37
  70.4 1.5 %collective-permute-start.17 = (bf16[96,1024]{1,0:T(8,128)(2,1)S(1)}, bf16[96,1024]{1,0:T(8,128)(2,1)S(1)}, u32[]{:S(2)}, u32[]{:S(2)}) collective-permute-start(bf16[96,1024]{1,0:T(8,128)(2,1)S(1)} %get-tuple-element.113), channel_id=1, source_target_pairs={{0,1},{1,0},{2,3},{3,2},{4,5},{5,4},{6,7},{7,6},{8,9},{9,8},{10,11... | collective-permute-start | bytes 589832 | tf_op jit(solution)/shard_map/ppermute | solution.py:37
  72.0 5.6 %collective-permute-start.18 = (bf16[2,24,1024]{2,1,0:T(8,128)(2,1)S(1)}, bf16[2,24,1024]{2,1,0:T(8,128)(2,1)S(1)}, u32[]{:S(2)}, u32[]{:S(2)}) collective-permute-start(bf16[2,24,1024]{2,1,0:T(8,128)(2,1)S(1)} %get-tuple-element.115), channel_id=1, source_target_pairs={{0,2},{1,3},{2,0},{3,1},{4,6},{5,7},{6,4},{7,5},{8,10},{9,11},{10,... | collective-permute-start | bytes 294920 | tf_op jit(solution)/shard_map/ppermute | solution.py:37
  73.6 6.9 %collective-permute-start.19 = (bf16[2,24,1024]{2,1,0:T(8,128)(2,1)S(1)}, bf16[2,24,1024]{2,1,0:T(8,128)(2,1)S(1)}, u32[]{:S(2)}, u32[]{:S(2)}) collective-permute-start(bf16[2,24,1024]{2,1,0:T(8,128)(2,1)S(1)} %get-tuple-element.116), channel_id=1, source_target_pairs={{0,4},{1,5},{2,6},{3,7},{4,0},{5,1},{6,2},{7,3},{8,12},{9,13},{10,... | collective-permute-start | bytes 294920 | tf_op jit(solution)/shard_map/ppermute | solution.py:37
  74.3 6.2 %collective-permute-start.20 = (bf16[2,24,1024]{2,1,0:T(8,128)(2,1)S(1)}, bf16[2,24,1024]{2,1,0:T(8,128)(2,1)S(1)}, u32[]{:S(2)}, u32[]{:S(2)}) collective-permute-start(bf16[2,24,1024]{2,1,0:T(8,128)(2,1)S(1)} %get-tuple-element.117), channel_id=1, source_target_pairs={{0,6},{1,7},{2,4},{3,5},{4,2},{5,3},{6,0},{7,1},{8,14},{9,15},{10,... | collective-permute-start | bytes 294920 | tf_op jit(solution)/shard_map/ppermute | solution.py:37
  80.7 5.9 %collective-permute-start.22 = (bf16[2,24,1024]{2,1,0:T(8,128)(2,1)S(1)}, bf16[2,24,1024]{2,1,0:T(8,128)(2,1)S(1)}, u32[]{:S(2)}, u32[]{:S(2)}) collective-permute-start(bf16[2,24,1024]{2,1,0:T(8,128)(2,1)S(1)} %get-tuple-element.119.refs_13_), channel_id=1, source_target_pairs={{12,0},{13,1},{14,2},{15,3},{8,4},{9,5},{10,6},{11,7},{20,8},{21,9... | collective-permute-start | bytes 294920 | tf_op jit(solution)/shard_map/ppermute | solution.py:52
  84.3 4.6 %collective-permute-start.21 = (bf16[2,24,1024]{2,1,0:T(8,128)(2,1)S(1)}, bf16[2,24,1024]{2,1,0:T(8,128)(2,1)S(1)}, u32[]{:S(2)}, u32[]{:S(2)}) collective-permute-start(bf16[2,24,1024]{2,1,0:T(8,128)(2,1)S(1)} %get-tuple-element.119.refs_13_), channel_id=1, source_target_pairs={{8,0},{9,1},{10,2},{11,3},{12,4},{13,5},{14,6},{15,7},{16,8},{17,9... | collective-permute-start | bytes 294920 | tf_op jit(solution)/shard_map/ppermute | solution.py:52
  88.9 1.3 %collective-permute-start.24 = (bf16[2,24,1024]{2,1,0:T(8,128)(2,1)S(1)}, bf16[2,24,1024]{2,1,0:T(8,128)(2,1)S(1)}, u32[]{:S(2)}, u32[]{:S(2)}) collective-permute-start(bf16[2,24,1024]{2,1,0:T(8,128)(2,1)S(1)} %get-tuple-element.122.refs_1_), channel_id=1, source_target_pairs={{0,1},{1,0},{2,3},{3,2},{4,5},{5,4},{6,7},{7,6},{8,9},{9,8},{10,11... | collective-permute-start | bytes 294920 | tf_op jit(solution)/shard_map/ppermute | solution.py:37
  89.0 1.5 %collective-permute-start.23 = (bf16[2,24,1024]{2,1,0:T(8,128)(2,1)S(1)}, bf16[2,24,1024]{2,1,0:T(8,128)(2,1)S(1)}, u32[]{:S(2)}, u32[]{:S(2)}) collective-permute-start(bf16[2,24,1024]{2,1,0:T(8,128)(2,1)S(1)} %get-tuple-element.121.refs_0_.incoming), channel_id=1, source_target_pairs={{0,1},{1,0},{2,3},{3,2},{4,5},{5,4},{6,7},{7,6},{8,9},{9,8},{10,11... | collective-permute-start | bytes 294920 | tf_op jit(solution)/shard_map/ppermute | solution.py:37
  100.1 1.5 %collective-permute-start.25 = (bf16[96,1024]{1,0:T(8,128)(2,1)S(1)}, bf16[96,1024]{1,0:T(8,128)(2,1)S(1)}, u32[]{:S(2)}, u32[]{:S(2)}) collective-permute-start(bf16[96,1024]{1,0:T(8,128)(2,1)S(1)} %get-tuple-element.132), channel_id=1, source_target_pairs={{0,1},{1,0},{2,3},{3,2},{4,5},{5,4},{6,7},{7,6},{8,9},{9,8},{10,11... | collective-permute-start | bytes 589832 | tf_op jit(solution)/shard_map/ppermute | solution.py:37
  101.7 4.2 %collective-permute-start.26 = (bf16[24,1024]{1,0:T(8,128)(2,1)S(1)}, bf16[24,1024]{1,0:T(8,128)(2,1)S(1)}, u32[]{:S(2)}, u32[]{:S(2)}) collective-permute-start(bf16[24,1024]{1,0:T(8,128)(2,1)S(1)} %get-tuple-element.134), channel_id=1, source_target_pairs={{0,2},{1,3},{2,0},{3,1},{4,6},{5,7},{6,4},{7,5},{8,10},{9,11},{10,... | collective-permute-start | bytes 147464 | tf_op jit(solution)/shard_map/ppermute | solution.py:37
  103.0 4.6 %collective-permute-start.27 = (bf16[24,1024]{1,0:T(8,128)(2,1)S(1)}, bf16[24,1024]{1,0:T(8,128)(2,1)S(1)}, u32[]{:S(2)}, u32[]{:S(2)}) collective-permute-start(bf16[24,1024]{1,0:T(8,128)(2,1)S(1)} %get-tuple-element.135), channel_id=1, source_target_pairs={{0,4},{1,5},{2,6},{3,7},{4,0},{5,1},{6,2},{7,3},{8,12},{9,13},{10,... | collective-permute-start | bytes 147464 | tf_op jit(solution)/shard_map/ppermute | solution.py:37
  103.7 5.0 %collective-permute-start.28 = (bf16[24,1024]{1,0:T(8,128)(2,1)S(1)}, bf16[24,1024]{1,0:T(8,128)(2,1)S(1)}, u32[]{:S(2)}, u32[]{:S(2)}) collective-permute-start(bf16[24,1024]{1,0:T(8,128)(2,1)S(1)} %get-tuple-element.136), channel_id=1, source_target_pairs={{0,6},{1,7},{2,4},{3,5},{4,2},{5,3},{6,0},{7,1},{8,14},{9,15},{10,... | collective-permute-start | bytes 147464 | tf_op jit(solution)/shard_map/ppermute | solution.py:37

commit v2 on v1

v2 whole, which is shorter than its diff:
```python
import functools

import jax
import jax.numpy as jnp
from jax import lax
from jax.experimental import pallas as pl
from jax.experimental.pallas import tpu as pltpu
from jax.sharding import PartitionSpec as P

epsilon = 1e-06
MIB = 2**20
f32 = jnp.float32
bf16 = jnp.bfloat16
VMEM = pl.BlockSpec(memory_space=pltpu.VMEM)
HBM = pl.BlockSpec(memory_space=pltpu.HBM)
SMEM = pl.BlockSpec(memory_space=pltpu.SMEM)
ANY = pl.BlockSpec(memory_space=pl.ANY)


def shape_of(shape, dtype):
    return jax.ShapeDtypeStruct(shape, dtype)


def limit(mib):
    return pltpu.CompilerParams(vmem_limit_bytes=mib * MIB)


def in_vmem(value):
    return pltpu.with_memory_space_constraint(value, pltpu.VMEM)


def in_hbm(value):
    return pltpu.with_memory_space_constraint(value, pltpu.HBM)


def swapped(value, mask):
    return lax.ppermute(value, "tp", [(i, i ^ mask) for i in range(lax.axis_size("tp"))])


def from_mirror(value):
    count = lax.axis_size("section")
    return lax.ppermute(value, "section", [(i, (i + count // 2) % count) for i in range(count)])


def from_above(value, mask):
    sections, parts = lax.axis_size("section"), lax.axis_size("tp")
    pairs = [
        (((s + 1) % sections) * parts + (i ^ mask), s * parts + i)
        for s in range(sections)
        for i in range(parts)
    ]
    return lax.ppermute(value, ("section", "tp"), pairs)


def with_cores(chips):
    return chips + [swapped(value, 1) for value in chips]


def pick_kernel(plan, stash, first, later, slots, stored, sems):
    sections = lax.axis_size("section")
    partner = lax.rem(lax.axis_index("section") + sections // 2, sections)
    copies = [
        pltpu.make_async_copy(plan, slots, sems.at[0]),
        pltpu.make_async_copy(stash.at[0], stored, sems.at[1]),
    ]
    for copy in copies:
        copy.start()
    for copy in copies:
        copy.wait()
    first[...] = stored[slots[0, partner]]
    for tick in range(later.shape[1]):
        later[0, tick] = stored[slots[tick + 1, partner]]


def pick(plan, stash):
    ticks, (_, _, rows, width) = plan.shape[0], stash.shape
    return pl.pallas_call(
        pick_kernel,
        out_shape=(
            shape_of((rows, width), stash.dtype),
            shape_of((1, ticks - 1, rows, width), stash.dtype),
        ),
        in_specs=[HBM, HBM],
        out_specs=(VMEM, VMEM),
        scratch_shapes=[
            pltpu.SMEM(plan.shape, plan.dtype),
            pltpu.VMEM(stash.shape[1:], stash.dtype),
            pltpu.SemaphoreType.DMA((2,)),
        ],
        compiler_params=limit(6),
        name="pick",
    )(in_hbm(plan), in_hbm(stash))


PIECES = 8
FIRST, SECOND = 4, 10


def piece_copies(wanted, weights, outs, sems):
    copies = []
    for at, ((which, piece), out) in enumerate(zip(wanted, outs)):
        where = [slice(None), slice(None)]
        axis = 1 - which
        where[axis] = pl.ds(piece * out.shape[axis], out.shape[axis])
        copies.append(pltpu.make_async_copy(weights[which].at[0, *where], out, sems.at[at]))
    return copies


def piece_shapes(wanted, weights):
    shapes = []
    for which, _ in wanted:
        shape = list(weights[which].shape[1:])
        shape[1 - which] //= PIECES
        shapes.append(pltpu.VMEM(tuple(shape), weights[which].dtype))
    return shapes


def load_kernel(wanted, w_in, w_out, after, *refs):
    *outs, token, sems = refs
    copies = piece_copies(wanted, (w_in, w_out), outs, sems)
    for copy in copies:
        copy.start()
    token[...] = jnp.zeros_like(token)
    for copy in copies:
        copy.wait()


def load(weights, wanted, after):
    shapes = piece_shapes(wanted, weights)
    *pieces, token = pl.pallas_call(
        functools.partial(load_kernel, wanted),
        out_shape=(*shapes, shape_of((8, 128), f32)),
        in_specs=[HBM, HBM, ANY],
        out_specs=tuple([VMEM] * (len(wanted) + 1)),
        scratch_shapes=[pltpu.SemaphoreType.DMA((len(wanted),))],
        compiler_params=limit(6),
        cost_estimate=pl.CostEstimate(
            flops=0,
            bytes_accessed=4 * sum(shape.shape[0] * shape.shape[1] for shape in shapes),
            transcendentals=0,
        ),
        name="load",
    )(*[in_hbm(weight) for weight in weights], after)
    return pieces, token


def tie_kernel(*refs):
    pass


def tie(values, token):
    return pl.pallas_call(
        tie_kernel,
        out_shape=tuple(shape_of(value.shape, value.dtype) for value in values),
        in_specs=[ANY] * (len(values) + 1),
        out_specs=tuple([ANY] * len(values)),
        input_output_aliases={at: at for at in range(len(values))},
        compiler_params=limit(1),
        name="tie",
    )(*values, token)


def pack_kernel(one, other, after, out):
    out[0] = one[...]
    out[1] = other[0]


def pack(one, other, after):
    return pl.pallas_call(
        pack_kernel,
        out_shape=shape_of((2, *one.shape), one.dtype),
        in_specs=[VMEM, VMEM, ANY],
        out_specs=VMEM,
        compiler_params=limit(6),
        name="pack",
    )(one, other, after)


def double_kernel(one, other, after, out):
    count = one.shape[0]
    out[:count] = one[...]
    out[count:] = other[...]


def double(one, other, after):
    count, *block = one.shape
    return pl.pallas_call(
        double_kernel,
        out_shape=shape_of((2 * count, *block), one.dtype),
        in_specs=[VMEM, VMEM, ANY],
        out_specs=VMEM,
        compiler_params=limit(6),
        name="double",
    )(one, other, after)


def joined(blocks, places):
    return jnp.concatenate([blocks[block][at].astype(f32) for block, at in places], axis=0)


def for_kernel(blocks, places):
    if blocks[0].shape[-2] % 8 == 0:
        return list(blocks), places
    return [joined(blocks, places).astype(bf16)], [(0, ...)]


def normalised(values):
    inverse_rms = lax.rsqrt(jnp.mean(values * values, axis=-1, keepdims=True) + epsilon)
    return inverse_rms, values * inverse_rms


def gate_values(inputs, w_in, part):
    preact = jnp.dot(inputs, w_in[:, part], preferred_element_type=f32)
    return (2.0 * jnp.maximum(preact, 0.0)).T


def spans(size, chunk):
    chunk = min(chunk, size)
    return [pl.ds(at, chunk) for at in range(0, size, chunk)]


def gate_kernel(places, counts, wanted, chunk, *refs):
    blocks, refs = refs[: counts[0]], refs[counts[0] :]
    gain, w_ins, refs = refs[0], refs[1 : 1 + counts[1]], refs[1 + counts[1] :]
    weights, refs = refs[:2], refs[2 + counts[2] :]
    gates, outs, (token, sems) = refs[: counts[1]], refs[counts[1] : -2], refs[-2:]
    copies = piece_copies(wanted, weights, outs, sems)
    for copy in copies:
        copy.start()
    token[...] = jnp.zeros_like(token)
    inputs = (normalised(joined(blocks, places))[1] * gain[...]).astype(bf16)
    for w_in, out in zip(w_ins, gates):
        for part in spans(out.shape[0], chunk):
            out[part, :] = gate_values(inputs, w_in, part).astype(bf16)
    for copy in copies:
        copy.wait()


def gate(blocks, places, gain, w_ins, chunk, weights, wanted, after):
    blocks, places = for_kernel(blocks, places)
    tokens = sum(block.shape[-2] for block in blocks) if places == [(0, ...)] else None
    if tokens is None:
        tokens = len(places) * blocks[0].shape[-2]
    width, hidden = w_ins[0].shape
    count = len(w_ins)
    *outs, token = pl.pallas_call(
        functools.partial(gate_kernel, places, (len(blocks), count, len(after)), wanted, chunk),
        out_shape=(
            *[pltpu.VMEM((hidden, tokens), bf16)] * count,
            *piece_shapes(wanted, weights),
            shape_of((8, 128), f32),
        ),
        in_specs=[VMEM] * (len(blocks) + 1 + count) + [HBM] * 2 + [ANY] * len(after),
        out_specs=tuple([VMEM] * (count + len(wanted) + 1)),
        scratch_shapes=[pltpu.SemaphoreType.DMA((max(len(wanted), 1),))],
        compiler_params=limit(6),
        cost_estimate=pl.CostEstimate(
            flops=2 * tokens * width * hidden * count,
            bytes_accessed=(2 * width + 2 * tokens) * hidden * count,
            transcendentals=0,
        ),
        name="gate",
    )(
        *blocks,
        gain,
        *[in_vmem(piece) for piece in w_ins],
        *[in_hbm(weight) for weight in weights],
        *after,
    )
    return outs[:count], outs[count:], token


def back_kernel(places, count, chunk, *refs):
    blocks, (*operands, own, other) = refs[:count], refs[count:]
    w_outs, w_ins, gates = [operands[at : at + PIECES] for at in range(0, 3 * PIECES, PIECES)]
    incoming = joined(blocks, places).T.astype(bf16)
    total = None
    for w_out, w_in, gate_piece in zip(w_outs, w_ins, gates):
        for part in spans(w_out.shape[0], chunk):
            hidden_back = jnp.dot(w_out[part, :], incoming, preferred_element_type=f32)
            hidden_grad = (hidden_back * gate_piece[part, :].astype(f32)).astype(bf16)
            partial = jnp.dot(w_in[:, part], hidden_grad, preferred_element_type=f32)
            total = partial if total is None else total + partial
    sums = total.T
    rows = own.shape[0]
    own[...] = sums[:rows]
    other[...] = sums[rows:].astype(bf16)


def back(blocks, places, gates, w_outs, w_ins, chunk):
    blocks, places = for_kernel(blocks, places)
    tokens = gates[0].shape[1]
    width, hidden = w_ins[0].shape
    hidden *= PIECES
    operands = [*blocks, *[in_vmem(piece) for piece in (*w_outs, *w_ins, *gates)]]
    return pl.pallas_call(
        functools.partial(back_kernel, places, len(blocks), chunk),
        out_shape=(
            shape_of((tokens // 2, width), f32),
            shape_of((tokens // 2, width), bf16),
        ),
        in_specs=[VMEM] * len(operands),
        out_specs=(VMEM, VMEM),
        compiler_params=limit(6),
        cost_estimate=pl.CostEstimate(
            flops=4 * tokens * width * hidden,
            bytes_accessed=4 * width * hidden + 2 * tokens * hidden,
            transcendentals=0,
        ),
        name="back",
    )(*operands)


def fold_values(own, received, rows, near):
    sums = own + received.astype(f32)
    blocks = [sums[at : at + rows] for at in range(0, sums.shape[0], rows)]
    if not near:
        return blocks[:1] + [block.astype(bf16) for block in blocks[1:]]
    pairs = [jnp.stack([blocks[at], blocks[at ^ 1]]) for at in range(len(blocks))]
    return pairs[:1] + [pair.astype(bf16) for pair in pairs[1:]]


def fold_kernel(rows, near, own, received, *outs):
    for out, value in zip(outs, fold_values(own[...], received[...], rows, near)):
        out[...] = value


def fold(own, received, rows, near):
    if rows % 8:
        return fold_values(own, received, rows, near)
    half, width = own.shape
    shape = (2, rows, width) if near else (rows, width)
    return pl.pallas_call(
        functools.partial(fold_kernel, rows, near),
        out_shape=tuple(shape_of(shape, bf16 if at else f32) for at in range(half // rows)),
        in_specs=[VMEM] * 2,
        out_specs=tuple([VMEM] * (half // rows)),
        compiler_params=limit(6),
        name="fold",
    )(own, received)


def finished(own, received, incoming, x_rows, gain):
    total = own
    for block in received:
        total = total + block.astype(f32)
    inverse_rms, normed = normalised(x_rows.astype(f32))
    scaled = total * gain
    inner = jnp.mean(scaled * normed, axis=-1, keepdims=True)
    return (incoming.astype(f32) + inverse_rms * (scaled - normed * inner)).astype(bf16)


def finish_kernel(places, count, tick, gain, fresh, fresh_near, *refs):
    blocks, refs = refs[: count[0]], refs[count[0] :]
    own, received, (_, result, outgoing) = refs[0], refs[1 : count[1]], refs[count[1] :]
    for at, extra in enumerate((fresh, fresh_near)):
        (x_block, x_at), (in_block, in_at) = places[at]
        value = finished(
            own[at],
            [block[at] for block in received],
            blocks[in_block][in_at],
            blocks[x_block][x_at],
            gain[...],
        )
        if at == 0:
            result[...] = value
        outgoing[at] = jnp.where(lax.axis_index("section") == 0, extra[tick], value)


def finish(own, received, blocks, places, gain, fresh, fresh_near, tick, after):
    pair, rows, width = own.shape
    operands = [gain, fresh, fresh_near, *blocks, own, *received]
    return pl.pallas_call(
        functools.partial(finish_kernel, places, (len(blocks), 1 + len(received)), tick),
        out_shape=(shape_of((rows, width), bf16), shape_of((pair, rows, width), bf16)),
        in_specs=[VMEM] * len(operands) + [ANY],
        out_specs=(VMEM, VMEM),
        compiler_params=limit(6),
        name="finish",
    )(*operands, after)


def end_kernel(places, count, gain, x_rows, incoming, own, *refs):
    received, (*past, out) = refs[:count], refs[count:]
    for before, value in enumerate(past):
        out[before, 0] = value[...]
    received = [block[...] for block in received]
    x_at, in_at = places
    out[len(past), 0] = finished(own[...], received, incoming[in_at], x_rows[x_at], gain[...])


def end(own, received, x_rows, incoming, places, gain, past):
    operands = [gain, x_rows, incoming, own, *received, *past]
    return pl.pallas_call(
        functools.partial(end_kernel, places, len(received)),
        out_shape=shape_of((len(past) + 1, 1, *own.shape), bf16),
        in_specs=[VMEM] * len(operands),
        out_specs=VMEM,
        compiler_params=limit(6),
        name="end",
    )(*operands)


def body(stash, w_in, w_out, gain, plan, arriving, fresh):
    ticks, rows = plan.shape[0], stash.shape[2]
    parts = lax.axis_size("tp")
    masks = range(2, parts, 2)
    weights = (w_in, w_out)
    order = [(which, piece) for which in (0, 1) for piece in range(PIECES)]
    stages = [order[:FIRST], order[FIRST:SECOND], order[SECOND:]]

    first, later = pick(plan, stash)
    moved = from_mirror(first)
    loaded, token = load(weights, stages[0], first)
    later, fresh_near = tie([later, fresh], token)
    later, fresh_near = from_mirror(later), swapped(fresh_near, masks[0])
    packed = pack(moved, arriving, token)
    chips = [swapped(packed, mask) for mask in masks]
    more, token = load(weights, stages[1], packed)
    loaded += more
    chips = tie(chips, token)
    gathered = with_cores([packed, *chips])
    x_blocks, x_places = gathered, [(block, 0) for block in range(parts)]
    in_blocks, in_places = gathered, [(block, 1) for block in range(parts)]

    (later,) = tie([later], token)
    near = swapped(later, masks[0])
    w_ins, w_outs = loaded[:PIECES], loaded[PIECES:]
    gates, more, token = gate(
        x_blocks, x_places, gain, w_ins, 1024, weights, stages[2], w_outs
    )
    w_outs += more
    later = double(later, near, token)
    for mask in masks[1:]:
        if mask & (mask - 1) == 0:
            near = swapped(later, mask)
            if 2 * mask < parts:
                later = double(later, near, token)

    results = []
    for tick in range(ticks):
        last = tick + 1 == ticks
        own, other = back(in_blocks, in_places, gates, w_outs, w_ins, 512)
        if tick == 0:
            later = double(later, near, own)
            later = [later, swapped(later, 1)]
        blocks = fold(own, swapped(other, 1), rows, not last)
        received = [swapped(block, mask) for block, mask in zip(blocks[1:], masks)]
        if last:
            places = (x_places[0][1], in_places[0][1])
            return end(blocks[0], received, x_blocks[0], in_blocks[0], places, gain, results)
        next_places = [(block, (chip, tick)) for block in (0, 1) for chip in range(parts // 2)]
        half = PIECES // 2
        gates_a, _, token = gate(
            later, next_places, gain, w_ins[:half], 1024, weights, [], (blocks[0], *w_outs)
        )
        places, used = [], []
        for at in (0, 1):
            places.append([])
            for from_blocks, from_places in ((x_blocks, x_places), (in_blocks, in_places)):
                block, where = from_places[at]
                places[at].append((len(used), where))
                used.append(from_blocks[block])
        result, outgoing = finish(
            blocks[0], received, used, places, gain, fresh, fresh_near, tick, token
        )
        results.append(result)
        came = [from_above(outgoing, mask) for mask in range(0, parts, 4)]
        gates_b, _, token = gate(
            later, next_places, gain, w_ins[half:], 1024, weights, [], (outgoing, *w_outs)
        )
        gates = gates_a + gates_b
        in_blocks = with_cores(list(tie(came, token)))
        in_places = [(block, at) for block in range(parts // 2) for at in (0, 1)]
        x_blocks, x_places = later, next_places


def solution(mesh):
    placed = (
        P("section", None, "tp", None),
        P("section", None, "tp"),
        P("section", "tp", None),
        P("section", None),
        P(),
        P("section", "tp", None),
        P(None, "tp", None),
    )
    return jax.shard_map(
        body, mesh=mesh, in_specs=placed, out_specs=P(None, "section", "tp", None), check_vma=False
    )
```

time: 110 us -> 107 us (0.973)
  waiting for transfers between devices: 22.5 us -> 17.4 us
  starting transfers between devices: 30.8 us -> 34.7 us
  Pallas kernels: 56 us -> 54.5 us
    ppermute x24 -> x27, waiting for transfers between devices: 16.4 us -> 12.6 us  [swapped(): lax.ppermute(value, 'tp', [(i, i ^ mask) for i in range(lax.axis_size('tp...]
    ppermute x24 -> x27, starting transfers between devices: 18.3 us -> 21.7 us  [swapped(): lax.ppermute(value, 'tp', [(i, i ^ mask) for i in range(lax.axis_size('tp...]
    ppermute x1 -> x2, starting transfers between devices: 4.1 us -> 5.64 us  [from_mirror(): lax.ppermute(value, 'section', [(i, (i + count // 2) % count) for i in ra...]
    pallas_call x14 -> x17, Pallas kernels: 55.9 us -> 54.4 us  [the longest x3 29.1 us: back(): pl.pallas_call(functools.partial(back_kernel, places, len(blocks), chunk)...]
  transfers between devices with their start and end apart: 29 -> 33, of which waited for: 20 -> 16; matrix products, arithmetic and copies ran while one was open for 0% -> 0% of each run, Pallas kernels for 18% -> 31%
where the time goes in v2:
time: 107 us
  Pallas kernels  54.5 us (51%)
  starting transfers between devices  34.7 us (32%)
  waiting for transfers between devices  17.4 us (16%)
    pallas_call x3, Pallas kernels, back(): pl.pallas_call(functools.partial(back_kernel, places, len(blocks), chunk)...  29.1 us
    ppermute x27, starting transfers between devices, swapped(): lax.ppermute(value, 'tp', [(i, i ^ mask) for i in range(lax.axis_size('tp...  21.7 us
    pallas_call x5, Pallas kernels, gate(): pl.pallas_call(functools.partial(gate_kernel, places, (len(blocks), count...  14.7 us
    ppermute x27, waiting for transfers between devices, swapped(): lax.ppermute(value, 'tp', [(i, i ^ mask) for i in range(lax.axis_size('tp...  12.6 us
    pallas_call x2, Pallas kernels, load(): pl.pallas_call(functools.partial(load_kernel, wanted), out_shape=(*shapes...  8.27 us
    ppermute x4, starting transfers between devices, from_above(): return lax.ppermute(value, ('section', 'tp'), pairs)  7.36 us
    ppermute x2, starting transfers between devices, from_mirror(): lax.ppermute(value, 'section', [(i, (i + count // 2) % count) for i in ra...  5.64 us
    ppermute x4, waiting for transfers between devices, from_above(): return lax.ppermute(value, ('section', 'tp'), pairs)  4.75 us
  transfers between devices with their start and end apart: 33, of which 16 were waited for; matrix products, arithmetic and copies ran while one was open for 0% of the time, Pallas kernels for 31%

profile of v2, /device:TPU:0, one launch (start us, length us, event | category | flops | bytes accessed | tf_op | source)
XLA Modules:
  0.0 107.0 jit_solution(2696656529203883562)
XLA Ops:
  1.0 4.1 %collective-permute-start.1 = (bf16[24,1024]{1,0:T(8,128)(2,1)S(1)}, bf16[24,1024]{1,0:T(8,128)(2,1)S(1)}, u32[]{:S(2)}, u32[]{:S(2)}) collective-permute-start(bf16[24,1024]{1,0:T(8,128)(2,1)S(1)} %get-tuple-element.86.after), channel_id=1, source_target_pairs={{0,16},{8,24},{16,0},{24,8},{1,17},{9,25},{17,1},{25,9},{2,18},{10... | collective-permute-start | bytes 147464 | tf_op jit(solution)/shard_map/ppermute | solution.py:42
  5.1 3.5 %load.2 = (bf16[1024,1024]{1,0:T(8,128)(2,1)S(1)}, bf16[1024,1024]{1,0:T(8,128)(2,1)S(1)}, bf16[1024,1024]{1,0:T(8,128)(2,1)S(1)}, bf16[1024,1024]{1,0:T(8,128)(2,1)S(1)}, f32[8,128]{1,0:T(8,128)S(1)}) custom-call(bf16[1,1024,8192]{2,1,0:T(8,128)(2,1)} %refs_7_.7, bf16[1,8192,1024]{2,1,0:T(8,128)(2,1)} %refs_8_.9, bf16[24,1024]{1,0:T(8,128)(2,1)S(1)} %get-tuple-element.86.after), custom_call_target="tpu_custom_call" | custom-call | bytes 16777216 | tf_op jit(solution)/shard_map/load/pallas_call | solution.py:130
  8.7 2.5 %collective-permute-start.5 = (bf16[2,24,1024]{2,1,0:T(8,128)(2,1)S(1)}, bf16[2,24,1024]{2,1,0:T(8,128)(2,1)S(1)}, u32[]{:S(2)}, u32[]{:S(2)}) collective-permute-start(bf16[2,24,1024]{2,1,0:T(8,128)(2,1)S(1)} %pack.1.after.refs_0_.refs_1_), channel_id=1, source_target_pairs={{0,6},{1,7},{2,4},{3,5},{4,2},{5,3},{6,0},{7,1},{8,14},{9,15},{10,... | collective-permute-start | bytes 294920 | tf_op jit(solution)/shard_map/ppermute | solution.py:37
  12.2 1.5 %collective-permute-start = (bf16[1,2,24,1024]{3,2,1,0:T(8,128)(2,1)S(1)}, bf16[1,2,24,1024]{3,2,1,0:T(8,128)(2,1)S(1)}, u32[]{:S(2)}, u32[]{:S(2)}) collective-permute-start(bf16[1,2,24,1024]{3,2,1,0:T(8,128)(2,1)S(1)} %get-tuple-element.88), channel_id=1, source_target_pairs={{0,16},{8,24},{16,0},{24,8},{1,17},{9,25},{17,1},{25,9},{2,18},{10... | collective-permute-start | bytes 294920 | tf_op jit(solution)/shard_map/ppermute | solution.py:42
  13.8 4.7 %load.3 = (bf16[1024,1024]{1,0:T(8,128)(2,1)S(1)}, bf16[1024,1024]{1,0:T(8,128)(2,1)S(1)}, bf16[1024,1024]{1,0:T(8,128)(2,1)S(1)}, bf16[1024,1024]{1,0:T(8,128)(...) custom-call(bf16[1,1024,8192]{2,1,0:T(8,128)(2,1)} %refs_7_.7, ...), custom_call_target="tpu_custom_call" | custom-call | bytes 25165824 | tf_op jit(solution)/shard_map/load/pallas_call | solution.py:130
  19.7 1.5 %collective-permute-start.2 = (bf16[1,2,24,1024]{3,2,1,0:T(8,128)(2,1)S(1)}, bf16[1,2,24,1024]{3,2,1,0:T(8,128)(2,1)S(1)}, u32[]{:S(2)}, u32[]{:S(2)}) collective-permute-start(bf16[1,2,24,1024]{3,2,1,0:T(8,128)(2,1)S(1)} %tie.6.one), channel_id=1, source_target_pairs={{0,2},{1,3},{2,0},{3,1},{4,6},{5,7},{6,4},{7,5},{8,10},{9,11},{10,... | collective-permute-start | bytes 294920 | tf_op jit(solution)/shard_map/ppermute | solution.py:37
  21.2 6.5 %gate.5 = (bf16[1024,192]{1,0:T(8,128)(2,1)S(1)}, bf16[1024,192]{1,0:T(8,128)(2,1)S(1)}, bf16[1024,192]{1,0:T(8,128)(2,1)S(1)}, bf16[1024,192]{1,0:T(8,128)(2,1)...) custom-call(bf16[2,24,1024]{2,1,0:T(8,128)(2,1)S(1)} %pack.1.after.r, ...), custom_call_target="tpu_custom_call" | custom-call | flops 3221225472 | bytes 19922944 | tf_op jit(solution)/shard_map/gate/pallas_call | solution.py:246
  27.7 1.6 %collective-permute-start.10 = (bf16[2,2,24,1024]{3,2,1,0:T(8,128)(2,1)S(1)}, bf16[2,2,24,1024]{3,2,1,0:T(8,128)(2,1)S(1)}, u32[]{:S(2)}, u32[]{:S(2)}) collective-permute-start(bf16[2,2,24,1024]{3,2,1,0:T(8,128)(2,1)S(1)} %double.2.one), channel_id=1, source_target_pairs={{0,4},{1,5},{2,6},{3,7},{4,0},{5,1},{6,2},{7,3},{8,12},{9,13},{10,... | collective-permute-start | bytes 589832 | tf_op jit(solution)/shard_map/ppermute | solution.py:37
  29.3 9.7 %back.3 = (f32[96,1024]{1,0:T(8,128)S(1)}, bf16[96,1024]{1,0:T(8,128)(2,1)S(1)}) custom-call(bf16[2,24,1024]{2,1,0:T(8,128)(2,1)S(1)} %pack.1.after.refs_0_.refs_1_, bf16[2,24,1024]{2,1,0:T(8,128)(2,1)S(1)} %get-tuple-element.90.refs_1_.refs_2_.refs_3_, bf16[2,24,1024]{2,1,0:T(8,128)(2,1)S(1)} %get-tuple-element.91.refs_2_, ...), custom_call_target="tpu_custom_call" | custom-call | flops 6442450944 | bytes 36700160 | tf_op jit(solution)/shard_map/back/pallas_call | solution.py:296
  41.2 1.0 collective-permute-start.13
  42.7 2.1 %collective-permute-start.15 = (bf16[2,24,1024]{2,1,0:T(8,128)(2,1)S(1)}, bf16[2,24,1024]{2,1,0:T(8,128)(2,1)S(1)}, u32[]{:S(2)}, u32[]{:S(2)}) collective-permute-start(bf16[2,24,1024]{2,1,0:T(8,128)(2,1)S(1)} %get-tuple-element.124), channel_id=1, source_target_pairs={{0,6},{1,7},{2,4},{3,5},{4,2},{5,3},{6,0},{7,1},{8,14},{9,15},{10,... | collective-permute-start | bytes 294920 | tf_op jit(solution)/shard_map/ppermute | solution.py:37
  44.8 2.2 %gate.6 = (bf16[1024,192]{1,0:T(8,128)(2,1)S(1)}, bf16[1024,192]{1,0:T(8,128)(2,1)S(1)}, bf16[1024,192]{1,0:T(8,128)(2,1)S(1)}, bf16[1024,192]{1,0:T(8,128)(2,1)S(1)}, f32[8,128]{1,0:T(8,128)S(1)}) custom-call(bf16[4,2,24,1024]{3,2,1,0:T(8,128)(2,1)S(1)} %double.3.refs_0_.refs_2_.x_rows, bf16[4,2,24,1024]{3,2,1,0:T(8,128)(2,1)S(1)} %collective-permute-done.16.refs_1_, ...), custom_call_target="tpu_custom_call" | custom-call | flops 1610612736 | bytes 9961472 | tf_op jit(solution)/shard_map/gate/pallas_call | solution.py:246
  47.0 1.9 %collective-permute-done.14.refs_6_ = bf16[2,24,1024]{2,1,0:T(8,128)(2,1)S(1)} collective-permute-done((bf16[2,24,1024]{2,1,0:T(8,128)(2,1)S(1)}, bf16[2,24,1024]{2,1,0:T(8,128)(2,1)S(1)}, u32[]{:S(2)}, u32[]{:S(2)}) %collective-permute-start.14) | collective-permute-done | bytes 98336 | tf_op jit(solution)/shard_map/ppermute | solution.py:37
  49.1 3.2 %collective-permute-start.18 = (bf16[2,24,1024]{2,1,0:T(8,128)(2,1)S(1)}, bf16[2,24,1024]{2,1,0:T(8,128)(2,1)S(1)}, u32[]{:S(2)}, u32[]{:S(2)}) collective-permute-start(bf16[2,24,1024]{2,1,0:T(8,128)(2,1)S(1)} %get-tuple-element.126.refs_9_), channel_id=1, source_target_pairs={{12,0},{13,1},{14,2},{15,3},{8,4},{9,5},{10,6},{11,7},{20,8},{21,9... | collective-permute-start | bytes 294920 | tf_op jit(solution)/shard_map/ppermute | solution.py:52
  52.7 2.0 %gate.7 = (bf16[1024,192]{1,0:T(8,128)(2,1)S(1)}, bf16[1024,192]{1,0:T(8,128)(2,1)S(1)}, bf16[1024,192]{1,0:T(8,128)(2,1)S(1)}, bf16[1024,192]{1,0:T(8,128)(2,1)S(1)}, f32[8,128]{1,0:T(8,128)S(1)}) custom-call(bf16[4,2,24,1024]{3,2,1,0:T(8,128)(2,1)S(1)} %double.3.refs_0_.refs_2_.x_rows, bf16[4,2,24,1024]{3,2,1,0:T(8,128)(2,1)S(1)} %collective-permute-done.16.refs_1_, ...), custom_call_target="tpu_custom_call" | custom-call | flops 1610612736 | bytes 9961472 | tf_op jit(solution)/shard_map/gate/pallas_call | solution.py:246
  55.4 1.5 %collective-permute-done.17.refs_0_ = bf16[2,24,1024]{2,1,0:T(8,128)(2,1)S(1)} collective-permute-done((bf16[2,24,1024]{2,1,0:T(8,128)(2,1)S(1)}, bf16[2,24,1024]{2,1,0:T(8,128)(2,1)S(1)}, u32[]{:S(2)}, u32[]{:S(2)}) %collective-permute-start.17) | collective-permute-done | bytes 98336 | tf_op jit(solution)/shard_map/ppermute | solution.py:52
  58.4 9.7 %back.4 = (f32[96,1024]{1,0:T(8,128)S(1)}, bf16[96,1024]{1,0:T(8,128)(2,1)S(1)}) custom-call(bf16[2,24,1024]{2,1,0:T(8,128)(2,1)S(1)} %get-tuple-element.128.refs_0_.refs_1_.refs_3_, bf16[2,24,1024]{2,1,0:T(8,128)(2,1)S(1)} %get-tuple-element.129.refs_1_, bf16[2,24,1024]{2,1,0:T(8,128)(2,1)S(1)} %collective-permute-done.19.refs_2_, ...), custom_call_target="tpu_custom_call" | custom-call | flops 6442450944 | bytes 36700160 | tf_op jit(solution)/shard_map/back/pallas_call | solution.py:296
  68.5 1.1 %collective-permute-done.21.received = bf16[96,1024]{1,0:T(8,128)(2,1)S(1)} collective-permute-done((bf16[96,1024]{1,0:T(8,128)(2,1)S(1)}, bf16[96,1024]{1,0:T(8,128)(2,1)S(1)}, u32[]{:S(2)}, u32[]{:S(2)}) %collective-permute-start.21) | collective-permute-done | bytes 196640 | tf_op jit(solution)/shard_map/ppermute | solution.py:37
  69.6 1.0 collective-permute-start.22
  70.6 1.1 collective-permute-start.23
  71.6 1.5 %collective-permute-start.24 = (bf16[2,24,1024]{2,1,0:T(8,128)(2,1)S(1)}, bf16[2,24,1024]{2,1,0:T(8,128)(2,1)S(1)}, u32[]{:S(2)}, u32[]{:S(2)}) collective-permute-start(bf16[2,24,1024]{2,1,0:T(8,128)(2,1)S(1)} %get-tuple-element.143), channel_id=1, source_target_pairs={{0,6},{1,7},{2,4},{3,5},{4,2},{5,3},{6,0},{7,1},{8,14},{9,15},{10,... | collective-permute-start | bytes 294920 | tf_op jit(solution)/shard_map/ppermute | solution.py:37
  73.2 2.0 %gate.8 = (bf16[1024,192]{1,0:T(8,128)(2,1)S(1)}, bf16[1024,192]{1,0:T(8,128)(2,1)S(1)}, bf16[1024,192]{1,0:T(8,128)(2,1)S(1)}, bf16[1024,192]{1,0:T(8,128)(2,1)S(1)}, f32[8,128]{1,0:T(8,128)S(1)}) custom-call(bf16[4,2,24,1024]{3,2,1,0:T(8,128)(2,1)S(1)} %double.3.refs_0_.refs_2_.x_rows, bf16[4,2,24,1024]{3,2,1,0:T(8,128)(2,1)S(1)} %collective-permute-done.16.refs_1_, ...), custom_call_target="tpu_custom_call" | custom-call | flops 1610612736 | bytes 9961472 | tf_op jit(solution)/shard_map/gate/pallas_call | solution.py:246
  75.2 2.2 %collective-permute-done.23.refs_6_ = bf16[2,24,1024]{2,1,0:T(8,128)(2,1)S(1)} collective-permute-done((bf16[2,24,1024]{2,1,0:T(8,128)(2,1)S(1)}, bf16[2,24,1024]{2,1,0:T(8,128)(2,1)S(1)}, u32[]{:S(2)}, u32[]{:S(2)}) %collective-permute-start.23) | collective-permute-done | bytes 98336 | tf_op jit(solution)/shard_map/ppermute | solution.py:37
  77.7 3.7 %collective-permute-start.26 = (bf16[2,24,1024]{2,1,0:T(8,128)(2,1)S(1)}, bf16[2,24,1024]{2,1,0:T(8,128)(2,1)S(1)}, u32[]{:S(2)}, u32[]{:S(2)}) collective-permute-start(bf16[2,24,1024]{2,1,0:T(8,128)(2,1)S(1)} %get-tuple-element.145.refs_9_), channel_id=1, source_target_pairs={{12,0},{13,1},{14,2},{15,3},{8,4},{9,5},{10,6},{11,7},{20,8},{21,9... | collective-permute-start | bytes 294920 | tf_op jit(solution)/shard_map/ppermute | solution.py:52
  81.4 2.0 %gate.9 = (bf16[1024,192]{1,0:T(8,128)(2,1)S(1)}, bf16[1024,192]{1,0:T(8,128)(2,1)S(1)}, bf16[1024,192]{1,0:T(8,128)(2,1)S(1)}, bf16[1024,192]{1,0:T(8,128)(2,1)S(1)}, f32[8,128]{1,0:T(8,128)S(1)}) custom-call(bf16[4,2,24,1024]{3,2,1,0:T(8,128)(2,1)S(1)} %double.3.refs_0_.refs_2_.x_rows, bf16[4,2,24,1024]{3,2,1,0:T(8,128)(2,1)S(1)} %collective-permute-done.16.refs_1_, ...), custom_call_target="tpu_custom_call" | custom-call | flops 1610612736 | bytes 9961472 | tf_op jit(solution)/shard_map/gate/pallas_call | solution.py:246
  84.1 1.9 %collective-permute-done.25.refs_0_ = bf16[2,24,1024]{2,1,0:T(8,128)(2,1)S(1)} collective-permute-done((bf16[2,24,1024]{2,1,0:T(8,128)(2,1)S(1)}, bf16[2,24,1024]{2,1,0:T(8,128)(2,1)S(1)}, u32[]{:S(2)}, u32[]{:S(2)}) %collective-permute-start.25) | collective-permute-done | bytes 98336 | tf_op jit(solution)/shard_map/ppermute | solution.py:52
  87.5 9.7 %back.5 = (f32[96,1024]{1,0:T(8,128)S(1)}, bf16[96,1024]{1,0:T(8,128)(2,1)S(1)}) custom-call(bf16[2,24,1024]{2,1,0:T(8,128)(2,1)S(1)} %get-tuple-element.147.refs_0_.incoming, bf16[2,24,1024]{2,1,0:T(8,128)(2,1)S(1)} %get-tuple-element.148.refs_1_, bf16[2,24,1024]{2,1,0:T(8,128)(2,1)S(1)} %collective-permute-done.27.refs_2_, ...), custom_call_target="tpu_custom_call" | custom-call | flops 6442450944 | bytes 36700160 | tf_op jit(solution)/shard_map/back/pallas_call | solution.py:296
  97.6 1.1 %collective-permute-done.29.received = bf16[96,1024]{1,0:T(8,128)(2,1)S(1)} collective-permute-done((bf16[96,1024]{1,0:T(8,128)(2,1)S(1)}, bf16[96,1024]{1,0:T(8,128)(2,1)S(1)}, u32[]{:S(2)}, u32[]{:S(2)}) %collective-permute-start.29) | collective-permute-done | bytes 196640 | tf_op jit(solution)/shard_map/ppermute | solution.py:37
  98.7 1.0 collective-permute-start.30
  99.8 1.4 %collective-permute-start.31 = (bf16[24,1024]{1,0:T(8,128)(2,1)S(1)}, bf16[24,1024]{1,0:T(8,128)(2,1)S(1)}, u32[]{:S(2)}, u32[]{:S(2)}) collective-permute-start(bf16[24,1024]{1,0:T(8,128)(2,1)S(1)} %get-tuple-element.161), channel_id=1, source_target_pairs={{0,4},{1,5},{2,6},{3,7},{4,0},{5,1},{6,2},{7,3},{8,12},{9,13},{10,... | collective-permute-start | bytes 147464 | tf_op jit(solution)/shard_map/ppermute | solution.py:37
  101.1 1.2 %collective-permute-start.32 = (bf16[24,1024]{1,0:T(8,128)(2,1)S(1)}, bf16[24,1024]{1,0:T(8,128)(2,1)S(1)}, u32[]{:S(2)}, u32[]{:S(2)}) collective-permute-start(bf16[24,1024]{1,0:T(8,128)(2,1)S(1)} %get-tuple-element.162), channel_id=1, source_target_pairs={{0,6},{1,7},{2,4},{3,5},{4,2},{5,3},{6,0},{7,1},{8,14},{9,15},{10,... | collective-permute-start | bytes 147464 | tf_op jit(solution)/shard_map/ppermute | solution.py:37
  103.9 2.3 %collective-permute-done.32.refs_2_ = bf16[24,1024]{1,0:T(8,128)(2,1)S(1)} collective-permute-done((bf16[24,1024]{1,0:T(8,128)(2,1)S(1)}, bf16[24,1024]{1,0:T(8,128)(2,1)S(1)}, u32[]{:S(2)}, u32[]{:S(2)}) %collective-permute-start.32) | collective-permute-done | bytes 49184 | tf_op jit(solution)/shard_map/ppermute | solution.py:37
  (66 shorter events, 14.4 us)
Async XLA Ops:
  1.0 7.6 %collective-permute-start.1 = (bf16[24,1024]{1,0:T(8,128)(2,1)S(1)}, bf16[24,1024]{1,0:T(8,128)(2,1)S(1)}, u32[]{:S(2)}, u32[]{:S(2)}) collective-permute-start(bf16[24,1024]{1,0:T(8,128)(2,1)S(1)} %get-tuple-element.86.after), channel_id=1, source_target_pairs={{0,16},{8,24},{16,0},{24,8},{1,17},{9,25},{17,1},{25,9},{2,18},{10... | collective-permute-start | bytes 147464 | tf_op jit(solution)/shard_map/ppermute | solution.py:42
  8.7 9.9 %collective-permute-start.5 = (bf16[2,24,1024]{2,1,0:T(8,128)(2,1)S(1)}, bf16[2,24,1024]{2,1,0:T(8,128)(2,1)S(1)}, u32[]{:S(2)}, u32[]{:S(2)}) collective-permute-start(bf16[2,24,1024]{2,1,0:T(8,128)(2,1)S(1)} %pack.1.after.refs_0_.refs_1_), channel_id=1, source_target_pairs={{0,6},{1,7},{2,4},{3,5},{4,2},{5,3},{6,0},{7,1},{8,14},{9,15},{10,... | collective-permute-start | bytes 294920 | tf_op jit(solution)/shard_map/ppermute | solution.py:37
  11.2 7.4 %collective-permute-start.4 = (bf16[2,24,1024]{2,1,0:T(8,128)(2,1)S(1)}, bf16[2,24,1024]{2,1,0:T(8,128)(2,1)S(1)}, u32[]{:S(2)}, u32[]{:S(2)}) collective-permute-start(bf16[2,24,1024]{2,1,0:T(8,128)(2,1)S(1)} %pack.1.after.refs_0_.refs_1_), channel_id=1, source_target_pairs={{0,4},{1,5},{2,6},{3,7},{4,0},{5,1},{6,2},{7,3},{8,12},{9,13},{10,... | collective-permute-start | bytes 294920 | tf_op jit(solution)/shard_map/ppermute | solution.py:37
  11.7 6.9 %collective-permute-start.3 = (bf16[2,24,1024]{2,1,0:T(8,128)(2,1)S(1)}, bf16[2,24,1024]{2,1,0:T(8,128)(2,1)S(1)}, u32[]{:S(2)}, u32[]{:S(2)}) collective-permute-start(bf16[2,24,1024]{2,1,0:T(8,128)(2,1)S(1)} %pack.1.after.refs_0_.refs_1_), channel_id=1, source_target_pairs={{0,2},{1,3},{2,0},{3,1},{4,6},{5,7},{6,4},{7,5},{8,10},{9,11},{10,... | collective-permute-start | bytes 294920 | tf_op jit(solution)/shard_map/ppermute | solution.py:37
  12.2 7.4 %collective-permute-start = (bf16[1,2,24,1024]{3,2,1,0:T(8,128)(2,1)S(1)}, bf16[1,2,24,1024]{3,2,1,0:T(8,128)(2,1)S(1)}, u32[]{:S(2)}, u32[]{:S(2)}) collective-permute-start(bf16[1,2,24,1024]{3,2,1,0:T(8,128)(2,1)S(1)} %get-tuple-element.88), channel_id=1, source_target_pairs={{0,16},{8,24},{16,0},{24,8},{1,17},{9,25},{17,1},{25,9},{2,18},{10... | collective-permute-start | bytes 294920 | tf_op jit(solution)/shard_map/ppermute | solution.py:42
  13.8 7.4 %collective-permute-start.6 = (bf16[2,24,1024]{2,1,0:T(8,128)(2,1)S(1)}, bf16[2,24,1024]{2,1,0:T(8,128)(2,1)S(1)}, u32[]{:S(2)}, u32[]{:S(2)}) collective-permute-start(bf16[2,24,1024]{2,1,0:T(8,128)(2,1)S(1)} %pack.1.after.refs_0_.refs_1_), channel_id=1, source_target_pairs={{0,1},{1,0},{2,3},{3,2},{4,5},{5,4},{6,7},{7,6},{8,9},{9,8},{10,11... | collective-permute-start | bytes 294920 | tf_op jit(solution)/shard_map/ppermute | solution.py:37
  18.6 2.6 %collective-permute-start.8 = (bf16[2,24,1024]{2,1,0:T(8,128)(2,1)S(1)}, bf16[2,24,1024]{2,1,0:T(8,128)(2,1)S(1)}, u32[]{:S(2)}, u32[]{:S(2)}) collective-permute-start(bf16[2,24,1024]{2,1,0:T(8,128)(2,1)S(1)} %get-tuple-element.91.refs_2_), channel_id=1, source_target_pairs={{0,1},{1,0},{2,3},{3,2},{4,5},{5,4},{6,7},{7,6},{8,9},{9,8},{10,11... | collective-permute-start | bytes 294920 | tf_op jit(solution)/shard_map/ppermute | solution.py:37
  19.2 2.0 %collective-permute-start.9 = (bf16[2,24,1024]{2,1,0:T(8,128)(2,1)S(1)}, bf16[2,24,1024]{2,1,0:T(8,128)(2,1)S(1)}, u32[]{:S(2)}, u32[]{:S(2)}) collective-permute-start(bf16[2,24,1024]{2,1,0:T(8,128)(2,1)S(1)} %get-tuple-element.92.refs_3_), channel_id=1, source_target_pairs={{0,1},{1,0},{2,3},{3,2},{4,5},{5,4},{6,7},{7,6},{8,9},{9,8},{10,11... | collective-permute-start | bytes 294920 | tf_op jit(solution)/shard_map/ppermute | solution.py:37
  19.2 1.9 %collective-permute-start.7 = (bf16[2,24,1024]{2,1,0:T(8,128)(2,1)S(1)}, bf16[2,24,1024]{2,1,0:T(8,128)(2,1)S(1)}, u32[]{:S(2)}, u32[]{:S(2)}) collective-permute-start(bf16[2,24,1024]{2,1,0:T(8,128)(2,1)S(1)} %get-tuple-element.90.refs_1_.refs_2_.refs_3_), channel_id=1, source_target_pairs={{0,1},{1,0},{2,3},{3,2},{4,5},{5,4},{6,7},{7,6},{8,9},{9,8},{10,11... | collective-permute-start | bytes 294920 | tf_op jit(solution)/shard_map/ppermute | solution.py:37
  19.7 8.0 %collective-permute-start.2 = (bf16[1,2,24,1024]{3,2,1,0:T(8,128)(2,1)S(1)}, bf16[1,2,24,1024]{3,2,1,0:T(8,128)(2,1)S(1)}, u32[]{:S(2)}, u32[]{:S(2)}) collective-permute-start(bf16[1,2,24,1024]{3,2,1,0:T(8,128)(2,1)S(1)} %tie.6.one), channel_id=1, source_target_pairs={{0,2},{1,3},{2,0},{3,1},{4,6},{5,7},{6,4},{7,5},{8,10},{9,11},{10,... | collective-permute-start | bytes 294920 | tf_op jit(solution)/shard_map/ppermute | solution.py:37
  27.7 11.3 %collective-permute-start.10 = (bf16[2,2,24,1024]{3,2,1,0:T(8,128)(2,1)S(1)}, bf16[2,2,24,1024]{3,2,1,0:T(8,128)(2,1)S(1)}, u32[]{:S(2)}, u32[]{:S(2)}) collective-permute-start(bf16[2,2,24,1024]{3,2,1,0:T(8,128)(2,1)S(1)} %double.2.one), channel_id=1, source_target_pairs={{0,4},{1,5},{2,6},{3,7},{4,0},{5,1},{6,2},{7,3},{8,12},{9,13},{10,... | collective-permute-start | bytes 589832 | tf_op jit(solution)/shard_map/ppermute | solution.py:37
  39.1 5.7 %collective-permute-start.16 = (bf16[4,2,24,1024]{3,2,1,0:T(8,128)(2,1)S(1)}, bf16[4,2,24,1024]{3,2,1,0:T(8,128)(2,1)S(1)}, u32[]{:S(2)}, u32[]{:S(2)}) collective-permute-start(bf16[4,2,24,1024]{3,2,1,0:T(8,128)(2,1)S(1)} %double.3.refs_0_.refs_2_.x_rows), channel_id=1, source_target_pairs={{0,1},{1,0},{2,3},{3,2},{4,5},{5,4},{6,7},{7,6},{8,9},{9,8},{10,11... | collective-permute-start | bytes 1179656 | tf_op jit(solution)/shard_map/ppermute | solution.py:37
  39.1 2.0 %collective-permute-start.12 = (bf16[96,1024]{1,0:T(8,128)(2,1)S(1)}, bf16[96,1024]{1,0:T(8,128)(2,1)S(1)}, u32[]{:S(2)}, u32[]{:S(2)}) collective-permute-start(bf16[96,1024]{1,0:T(8,128)(2,1)S(1)} %get-tuple-element.120), channel_id=1, source_target_pairs={{0,1},{1,0},{2,3},{3,2},{4,5},{5,4},{6,7},{7,6},{8,9},{9,8},{10,11... | collective-permute-start | bytes 589832 | tf_op jit(solution)/shard_map/ppermute | solution.py:37
  39.6 7.3 %collective-permute-start.11 = (bf16[2,24,1024]{2,1,0:T(8,128)(2,1)S(1)}, bf16[2,24,1024]{2,1,0:T(8,128)(2,1)S(1)}, u32[]{:S(2)}, u32[]{:S(2)}) collective-permute-start(bf16[2,24,1024]{2,1,0:T(8,128)(2,1)S(1)} %get-tuple-element.119), channel_id=1, source_target_pairs={{0,2},{1,3},{2,0},{3,1},{4,6},{5,7},{6,4},{7,5},{8,10},{9,11},{10,... | collective-permute-start | bytes 294920 | tf_op jit(solution)/shard_map/ppermute | solution.py:37
  41.2 5.8 %collective-permute-start.13 = (bf16[2,24,1024]{2,1,0:T(8,128)(2,1)S(1)}, bf16[2,24,1024]{2,1,0:T(8,128)(2,1)S(1)}, u32[]{:S(2)}, u32[]{:S(2)}) collective-permute-start(bf16[2,24,1024]{2,1,0:T(8,128)(2,1)S(1)} %get-tuple-element.122), channel_id=1, source_target_pairs={{0,2},{1,3},{2,0},{3,1},{4,6},{5,7},{6,4},{7,5},{8,10},{9,11},{10,... | collective-permute-start | bytes 294920 | tf_op jit(solution)/shard_map/ppermute | solution.py:37
  42.2 6.7 %collective-permute-start.14 = (bf16[2,24,1024]{2,1,0:T(8,128)(2,1)S(1)}, bf16[2,24,1024]{2,1,0:T(8,128)(2,1)S(1)}, u32[]{:S(2)}, u32[]{:S(2)}) collective-permute-start(bf16[2,24,1024]{2,1,0:T(8,128)(2,1)S(1)} %get-tuple-element.123), channel_id=1, source_target_pairs={{0,4},{1,5},{2,6},{3,7},{4,0},{5,1},{6,2},{7,3},{8,12},{9,13},{10,... | collective-permute-start | bytes 294920 | tf_op jit(solution)/shard_map/ppermute | solution.py:37
  42.7 6.2 %collective-permute-start.15 = (bf16[2,24,1024]{2,1,0:T(8,128)(2,1)S(1)}, bf16[2,24,1024]{2,1,0:T(8,128)(2,1)S(1)}, u32[]{:S(2)}, u32[]{:S(2)}) collective-permute-start(bf16[2,24,1024]{2,1,0:T(8,128)(2,1)S(1)} %get-tuple-element.124), channel_id=1, source_target_pairs={{0,6},{1,7},{2,4},{3,5},{4,2},{5,3},{6,0},{7,1},{8,14},{9,15},{10,... | collective-permute-start | bytes 294920 | tf_op jit(solution)/shard_map/ppermute | solution.py:37
  49.1 6.3 %collective-permute-start.18 = (bf16[2,24,1024]{2,1,0:T(8,128)(2,1)S(1)}, bf16[2,24,1024]{2,1,0:T(8,128)(2,1)S(1)}, u32[]{:S(2)}, u32[]{:S(2)}) collective-permute-start(bf16[2,24,1024]{2,1,0:T(8,128)(2,1)S(1)} %get-tuple-element.126.refs_9_), channel_id=1, source_target_pairs={{12,0},{13,1},{14,2},{15,3},{8,4},{9,5},{10,6},{11,7},{20,8},{21,9... | collective-permute-start | bytes 294920 | tf_op jit(solution)/shard_map/ppermute | solution.py:52
  52.3 4.6 %collective-permute-start.17 = (bf16[2,24,1024]{2,1,0:T(8,128)(2,1)S(1)}, bf16[2,24,1024]{2,1,0:T(8,128)(2,1)S(1)}, u32[]{:S(2)}, u32[]{:S(2)}) collective-permute-start(bf16[2,24,1024]{2,1,0:T(8,128)(2,1)S(1)} %get-tuple-element.126.refs_9_), channel_id=1, source_target_pairs={{8,0},{9,1},{10,2},{11,3},{12,4},{13,5},{14,6},{15,7},{16,8},{17,9... | collective-permute-start | bytes 294920 | tf_op jit(solution)/shard_map/ppermute | solution.py:52
  56.9 1.3 %collective-permute-start.20 = (bf16[2,24,1024]{2,1,0:T(8,128)(2,1)S(1)}, bf16[2,24,1024]{2,1,0:T(8,128)(2,1)S(1)}, u32[]{:S(2)}, u32[]{:S(2)}) collective-permute-start(bf16[2,24,1024]{2,1,0:T(8,128)(2,1)S(1)} %get-tuple-element.129.refs_1_), channel_id=1, source_target_pairs={{0,1},{1,0},{2,3},{3,2},{4,5},{5,4},{6,7},{7,6},{8,9},{9,8},{10,11... | collective-permute-start | bytes 294920 | tf_op jit(solution)/shard_map/ppermute | solution.py:37
  56.9 1.5 %collective-permute-start.19 = (bf16[2,24,1024]{2,1,0:T(8,128)(2,1)S(1)}, bf16[2,24,1024]{2,1,0:T(8,128)(2,1)S(1)}, u32[]{:S(2)}, u32[]{:S(2)}) collective-permute-start(bf16[2,24,1024]{2,1,0:T(8,128)(2,1)S(1)} %get-tuple-element.128.refs_0_.refs_1_.refs_3_), channel_id=1, source_target_pairs={{0,1},{1,0},{2,3},{3,2},{4,5},{5,4},{6,7},{7,6},{8,9},{9,8},{10,11... | collective-permute-start | bytes 294920 | tf_op jit(solution)/shard_map/ppermute | solution.py:37
  68.1 1.5 %collective-permute-start.21 = (bf16[96,1024]{1,0:T(8,128)(2,1)S(1)}, bf16[96,1024]{1,0:T(8,128)(2,1)S(1)}, u32[]{:S(2)}, u32[]{:S(2)}) collective-permute-start(bf16[96,1024]{1,0:T(8,128)(2,1)S(1)} %get-tuple-element.139), channel_id=1, source_target_pairs={{0,1},{1,0},{2,3},{3,2},{4,5},{5,4},{6,7},{7,6},{8,9},{9,8},{10,11... | collective-permute-start | bytes 589832 | tf_op jit(solution)/shard_map/ppermute | solution.py:37
  69.6 5.6 %collective-permute-start.22 = (bf16[2,24,1024]{2,1,0:T(8,128)(2,1)S(1)}, bf16[2,24,1024]{2,1,0:T(8,128)(2,1)S(1)}, u32[]{:S(2)}, u32[]{:S(2)}) collective-permute-start(bf16[2,24,1024]{2,1,0:T(8,128)(2,1)S(1)} %get-tuple-element.141), channel_id=1, source_target_pairs={{0,2},{1,3},{2,0},{3,1},{4,6},{5,7},{6,4},{7,5},{8,10},{9,11},{10,... | collective-permute-start | bytes 294920 | tf_op jit(solution)/shard_map/ppermute | solution.py:37
  70.6 6.9 %collective-permute-start.23 = (bf16[2,24,1024]{2,1,0:T(8,128)(2,1)S(1)}, bf16[2,24,1024]{2,1,0:T(8,128)(2,1)S(1)}, u32[]{:S(2)}, u32[]{:S(2)}) collective-permute-start(bf16[2,24,1024]{2,1,0:T(8,128)(2,1)S(1)} %get-tuple-element.142), channel_id=1, source_target_pairs={{0,4},{1,5},{2,6},{3,7},{4,0},{5,1},{6,2},{7,3},{8,12},{9,13},{10,... | collective-permute-start | bytes 294920 | tf_op jit(solution)/shard_map/ppermute | solution.py:37
  71.6 5.8 %collective-permute-start.24 = (bf16[2,24,1024]{2,1,0:T(8,128)(2,1)S(1)}, bf16[2,24,1024]{2,1,0:T(8,128)(2,1)S(1)}, u32[]{:S(2)}, u32[]{:S(2)}) collective-permute-start(bf16[2,24,1024]{2,1,0:T(8,128)(2,1)S(1)} %get-tuple-element.143), channel_id=1, source_target_pairs={{0,6},{1,7},{2,4},{3,5},{4,2},{5,3},{6,0},{7,1},{8,14},{9,15},{10,... | collective-permute-start | bytes 294920 | tf_op jit(solution)/shard_map/ppermute | solution.py:37
  77.7 6.5 %collective-permute-start.26 = (bf16[2,24,1024]{2,1,0:T(8,128)(2,1)S(1)}, bf16[2,24,1024]{2,1,0:T(8,128)(2,1)S(1)}, u32[]{:S(2)}, u32[]{:S(2)}) collective-permute-start(bf16[2,24,1024]{2,1,0:T(8,128)(2,1)S(1)} %get-tuple-element.145.refs_9_), channel_id=1, source_target_pairs={{12,0},{13,1},{14,2},{15,3},{8,4},{9,5},{10,6},{11,7},{20,8},{21,9... | collective-permute-start | bytes 294920 | tf_op jit(solution)/shard_map/ppermute | solution.py:52
  81.4 4.6 %collective-permute-start.25 = (bf16[2,24,1024]{2,1,0:T(8,128)(2,1)S(1)}, bf16[2,24,1024]{2,1,0:T(8,128)(2,1)S(1)}, u32[]{:S(2)}, u32[]{:S(2)}) collective-permute-start(bf16[2,24,1024]{2,1,0:T(8,128)(2,1)S(1)} %get-tuple-element.145.refs_9_), channel_id=1, source_target_pairs={{8,0},{9,1},{10,2},{11,3},{12,4},{13,5},{14,6},{15,7},{16,8},{17,9... | collective-permute-start | bytes 294920 | tf_op jit(solution)/shard_map/ppermute | solution.py:52
  86.0 1.5 %collective-permute-start.27 = (bf16[2,24,1024]{2,1,0:T(8,128)(2,1)S(1)}, bf16[2,24,1024]{2,1,0:T(8,128)(2,1)S(1)}, u32[]{:S(2)}, u32[]{:S(2)}) collective-permute-start(bf16[2,24,1024]{2,1,0:T(8,128)(2,1)S(1)} %get-tuple-element.147.refs_0_.incoming), channel_id=1, source_target_pairs={{0,1},{1,0},{2,3},{3,2},{4,5},{5,4},{6,7},{7,6},{8,9},{9,8},{10,11... | collective-permute-start | bytes 294920 | tf_op jit(solution)/shard_map/ppermute | solution.py:37
  97.2 1.5 %collective-permute-start.29 = (bf16[96,1024]{1,0:T(8,128)(2,1)S(1)}, bf16[96,1024]{1,0:T(8,128)(2,1)S(1)}, u32[]{:S(2)}, u32[]{:S(2)}) collective-permute-start(bf16[96,1024]{1,0:T(8,128)(2,1)S(1)} %get-tuple-element.158), channel_id=1, source_target_pairs={{0,1},{1,0},{2,3},{3,2},{4,5},{5,4},{6,7},{7,6},{8,9},{9,8},{10,11... | collective-permute-start | bytes 589832 | tf_op jit(solution)/shard_map/ppermute | solution.py:37
  98.7 4.2 %collective-permute-start.30 = (bf16[24,1024]{1,0:T(8,128)(2,1)S(1)}, bf16[24,1024]{1,0:T(8,128)(2,1)S(1)}, u32[]{:S(2)}, u32[]{:S(2)}) collective-permute-start(bf16[24,1024]{1,0:T(8,128)(2,1)S(1)} %get-tuple-element.160), channel_id=1, source_target_pairs={{0,2},{1,3},{2,0},{3,1},{4,6},{5,7},{6,4},{7,5},{8,10},{9,11},{10,... | collective-permute-start | bytes 147464 | tf_op jit(solution)/shard_map/ppermute | solution.py:37
  99.8 4.1 %collective-permute-start.31 = (bf16[24,1024]{1,0:T(8,128)(2,1)S(1)}, bf16[24,1024]{1,0:T(8,128)(2,1)S(1)}, u32[]{:S(2)}, u32[]{:S(2)}) collective-permute-start(bf16[24,1024]{1,0:T(8,128)(2,1)S(1)} %get-tuple-element.161), channel_id=1, source_target_pairs={{0,4},{1,5},{2,6},{3,7},{4,0},{5,1},{6,2},{7,3},{8,12},{9,13},{10,... | collective-permute-start | bytes 147464 | tf_op jit(solution)/shard_map/ppermute | solution.py:37
  101.1 5.0 %collective-permute-start.32 = (bf16[24,1024]{1,0:T(8,128)(2,1)S(1)}, bf16[24,1024]{1,0:T(8,128)(2,1)S(1)}, u32[]{:S(2)}, u32[]{:S(2)}) collective-permute-start(bf16[24,1024]{1,0:T(8,128)(2,1)S(1)} %get-tuple-element.162), channel_id=1, source_target_pairs={{0,6},{1,7},{2,4},{3,5},{4,2},{5,3},{6,0},{7,1},{8,14},{9,15},{10,... | collective-permute-start | bytes 147464 | tf_op jit(solution)/shard_map/ppermute | solution.py:37
  (4 other events, 29.2 us)

commit v3 on v2

--- a/solution.py
+++ b/solution.py
@@ -93,7 +93,7 @@
 
 
 PIECES = 8
-FIRST, SECOND = 4, 10
+FIRST, SECOND = 5, 11
 
 
 def piece_copies(wanted, weights, outs, sems):
@@ -418,7 +418,7 @@
     chips = [swapped(packed, mask) for mask in masks]
     more, token = load(weights, stages[1], packed)
     loaded += more
-    chips = tie(chips, token)
+    chips = [tie([value], token)[0] for value in chips]
     gathered = with_cores([packed, *chips])
     x_blocks, x_places = gathered, [(block, 0) for block in range(parts)]
     in_blocks, in_places = gathered, [(block, 1) for block in range(parts)]
@@ -470,7 +470,7 @@
             later, next_places, gain, w_ins[half:], 1024, weights, [], (outgoing, *w_outs)
         )
         gates = gates_a + gates_b
-        in_blocks = with_cores(list(tie(came, token)))
+        in_blocks = with_cores([tie([value], token)[0] for value in came])
         in_places = [(block, at) for block in range(parts // 2) for at in (0, 1)]
         x_blocks, x_places = later, next_places
 

time: 107 us -> 106 us (level)
  starting transfers between devices: 34.7 us -> 33.2 us
    ppermute x27, starting transfers between devices: 21.7 us -> 20.3 us  [swapped(): lax.ppermute(value, 'tp', [(i, i ^ mask) for i in range(lax.axis_size('tp...]
  transfers between devices with their start and end apart: 33 -> 33, of which waited for: 16 -> 14; matrix products, arithmetic and copies ran while one was open for 0% -> 0% of each run, Pallas kernels for 31% -> 31%
where the time goes in v3:
time: 106 us
  Pallas kernels  54.4 us (51%)
  starting transfers between devices  33.2 us (31%)
  waiting for transfers between devices  18.4 us (17%)
    pallas_call x3, Pallas kernels, back(): pl.pallas_call(functools.partial(back_kernel, places, len(blocks), chunk)...  29 us
    ppermute x27, starting transfers between devices, swapped(): lax.ppermute(value, 'tp', [(i, i ^ mask) for i in range(lax.axis_size('tp...  20.3 us
    pallas_call x5, Pallas kernels, gate(): pl.pallas_call(functools.partial(gate_kernel, places, (len(blocks), count...  14 us
    ppermute x27, waiting for transfers between devices, swapped(): lax.ppermute(value, 'tp', [(i, i ^ mask) for i in range(lax.axis_size('tp...  13.7 us
    pallas_call x2, Pallas kernels, load(): pl.pallas_call(functools.partial(load_kernel, wanted), out_shape=(*shapes...  8.88 us
    ppermute x4, starting transfers between devices, from_above(): return lax.ppermute(value, ('section', 'tp'), pairs)  7.9 us
    ppermute x2, starting transfers between devices, from_mirror(): lax.ppermute(value, 'section', [(i, (i + count // 2) % count) for i in ra...  5.03 us
    ppermute x4, waiting for transfers between devices, from_above(): return lax.ppermute(value, ('section', 'tp'), pairs)  4.75 us
  transfers between devices with their start and end apart: 33, of which 14 were waited for; matrix products, arithmetic and copies ran while one was open for 0% of the time, Pallas kernels for 31%

profile of v3, /device:TPU:0, one launch (start us, length us, event | category | flops | bytes accessed | tf_op | source)
XLA Modules:
  0.0 106.3 jit_solution(7447098246707830357)
XLA Ops:
  1.0 4.1 %collective-permute-start.1 = (bf16[24,1024]{1,0:T(8,128)(2,1)S(1)}, bf16[24,1024]{1,0:T(8,128)(2,1)S(1)}, u32[]{:S(2)}, u32[]{:S(2)}) collective-permute-start(bf16[24,1024]{1,0:T(8,128)(2,1)S(1)} %get-tuple-element.79.after), channel_id=1, source_target_pairs={{0,16},{8,24},{16,0},{24,8},{1,17},{9,25},{17,1},{25,9},{2,18},{10... | collective-permute-start | bytes 147464 | tf_op jit(solution)/shard_map/ppermute | solution.py:42
  5.1 4.1 %load.2 = (bf16[1024,1024]{1,0:T(8,128)(2,1)S(1)}, bf16[1024,1024]{1,0:T(8,128)(2,1)S(1)}, bf16[1024,1024]{1,0:T(8,128)(2,1)S(1)}, bf16[1024,1024]{1,0:T(8,128)(...) custom-call(bf16[1,1024,8192]{2,1,0:T(8,128)(2,1)} %refs_7_.7, bf16[1,8192,1024]{2,1,0:T(8,128)(2,1)} %refs_8_.9, ...), custom_call_target="tpu_custom_call" | custom-call | bytes 20971520 | tf_op jit(solution)/shard_map/load/pallas_call | solution.py:130
  9.3 1.6 %collective-permute-start.4 = (bf16[2,24,1024]{2,1,0:T(8,128)(2,1)S(1)}, bf16[2,24,1024]{2,1,0:T(8,128)(2,1)S(1)}, u32[]{:S(2)}, u32[]{:S(2)}) collective-permute-start(bf16[2,24,1024]{2,1,0:T(8,128)(2,1)S(1)} %pack.1.after.refs_0_.refs_1_), channel_id=1, source_target_pairs={{0,4},{1,5},{2,6},{3,7},{4,0},{5,1},{6,2},{7,3},{8,12},{9,13},{10,... | collective-permute-start | bytes 294920 | tf_op jit(solution)/shard_map/ppermute | solution.py:37
  10.9 1.4 %collective-permute-start.5 = (bf16[2,24,1024]{2,1,0:T(8,128)(2,1)S(1)}, bf16[2,24,1024]{2,1,0:T(8,128)(2,1)S(1)}, u32[]{:S(2)}, u32[]{:S(2)}) collective-permute-start(bf16[2,24,1024]{2,1,0:T(8,128)(2,1)S(1)} %pack.1.after.refs_0_.refs_1_), channel_id=1, source_target_pairs={{0,6},{1,7},{2,4},{3,5},{4,2},{5,3},{6,0},{7,1},{8,14},{9,15},{10,... | collective-permute-start | bytes 294920 | tf_op jit(solution)/shard_map/ppermute | solution.py:37
  13.8 4.7 %load.3 = (bf16[1024,1024]{1,0:T(8,128)(2,1)S(1)}, bf16[1024,1024]{1,0:T(8,128)(2,1)S(1)}, bf16[1024,1024]{1,0:T(8,128)(2,1)S(1)}, bf16[1024,1024]{1,0:T(8,128)(...) custom-call(bf16[1,1024,8192]{2,1,0:T(8,128)(2,1)} %refs_7_.7, ...), custom_call_target="tpu_custom_call" | custom-call | bytes 25165824 | tf_op jit(solution)/shard_map/load/pallas_call | solution.py:130
  19.7 1.5 %collective-permute-start.2 = (bf16[1,2,24,1024]{3,2,1,0:T(8,128)(2,1)S(1)}, bf16[1,2,24,1024]{3,2,1,0:T(8,128)(2,1)S(1)}, u32[]{:S(2)}, u32[]{:S(2)}) collective-permute-start(bf16[1,2,24,1024]{3,2,1,0:T(8,128)(2,1)S(1)} %tie.10.one), channel_id=1, source_target_pairs={{0,2},{1,3},{2,0},{3,1},{4,6},{5,7},{6,4},{7,5},{8,10},{9,11},{10,... | collective-permute-start | bytes 294920 | tf_op jit(solution)/shard_map/ppermute | solution.py:37
  21.2 5.8 %gate.5 = (bf16[1024,192]{1,0:T(8,128)(2,1)S(1)}, bf16[1024,192]{1,0:T(8,128)(2,1)S(1)}, bf16[1024,192]{1,0:T(8,128)(2,1)S(1)}, bf16[1024,192]{1,0:T(8,128)(2,1)...) custom-call(bf16[2,24,1024]{2,1,0:T(8,128)(2,1)S(1)} %pack.1.after.r, ...), custom_call_target="tpu_custom_call" | custom-call | flops 3221225472 | bytes 19922944 | tf_op jit(solution)/shard_map/gate/pallas_call | solution.py:246
  27.0 1.6 %collective-permute-start.10 = (bf16[2,2,24,1024]{3,2,1,0:T(8,128)(2,1)S(1)}, bf16[2,2,24,1024]{3,2,1,0:T(8,128)(2,1)S(1)}, u32[]{:S(2)}, u32[]{:S(2)}) collective-permute-start(bf16[2,2,24,1024]{3,2,1,0:T(8,128)(2,1)S(1)} %double.2.one), channel_id=1, source_target_pairs={{0,4},{1,5},{2,6},{3,7},{4,0},{5,1},{6,2},{7,3},{8,12},{9,13},{10,... | collective-permute-start | bytes 589832 | tf_op jit(solution)/shard_map/ppermute | solution.py:37
  28.6 9.7 %back.3 = (f32[96,1024]{1,0:T(8,128)S(1)}, bf16[96,1024]{1,0:T(8,128)(2,1)S(1)}) custom-call(bf16[2,24,1024]{2,1,0:T(8,128)(2,1)S(1)} %pack.1.after.refs_0_.refs_1_, bf16[2,24,1024]{2,1,0:T(8,128)(2,1)S(1)} %tie.11.refs_1_.refs_2_.refs_3_, bf16[2,24,1024]{2,1,0:T(8,128)(2,1)S(1)} %tie.12.refs_2_, bf16[2,24,1024]{2,1,0:T(8,128)(2,1)S(1)} %tie.13.refs_3_, ...), custom_call_target="tpu_custom_call" | custom-call | flops 6442450944 | bytes 36700160 | tf_op jit(solution)/shard_map/back/pallas_call | solution.py:296
  41.9 2.1 %collective-permute-start.15 = (bf16[2,24,1024]{2,1,0:T(8,128)(2,1)S(1)}, bf16[2,24,1024]{2,1,0:T(8,128)(2,1)S(1)}, u32[]{:S(2)}, u32[]{:S(2)}) collective-permute-start(bf16[2,24,1024]{2,1,0:T(8,128)(2,1)S(1)} %get-tuple-element.114), channel_id=1, source_target_pairs={{0,6},{1,7},{2,4},{3,5},{4,2},{5,3},{6,0},{7,1},{8,14},{9,15},{10,... | collective-permute-start | bytes 294920 | tf_op jit(solution)/shard_map/ppermute | solution.py:37
  44.0 2.2 %gate.6 = (bf16[1024,192]{1,0:T(8,128)(2,1)S(1)}, bf16[1024,192]{1,0:T(8,128)(2,1)S(1)}, bf16[1024,192]{1,0:T(8,128)(2,1)S(1)}, bf16[1024,192]{1,0:T(8,128)(2,1)S(1)}, f32[8,128]{1,0:T(8,128)S(1)}) custom-call(bf16[4,2,24,1024]{3,2,1,0:T(8,128)(2,1)S(1)} %double.3.refs_0_.refs_2_.x_rows, bf16[4,2,24,1024]{3,2,1,0:T(8,128)(2,1)S(1)} %collective-permute-done.16.refs_1_, ...), custom_call_target="tpu_custom_call" | custom-call | flops 1610612736 | bytes 9961472 | tf_op jit(solution)/shard_map/gate/pallas_call | solution.py:246
  46.2 1.9 %collective-permute-done.14.refs_6_ = bf16[2,24,1024]{2,1,0:T(8,128)(2,1)S(1)} collective-permute-done((bf16[2,24,1024]{2,1,0:T(8,128)(2,1)S(1)}, bf16[2,24,1024]{2,1,0:T(8,128)(2,1)S(1)}, u32[]{:S(2)}, u32[]{:S(2)}) %collective-permute-start.14) | collective-permute-done | bytes 98336 | tf_op jit(solution)/shard_map/ppermute | solution.py:37
  48.4 3.8 %collective-permute-start.18 = (bf16[2,24,1024]{2,1,0:T(8,128)(2,1)S(1)}, bf16[2,24,1024]{2,1,0:T(8,128)(2,1)S(1)}, u32[]{:S(2)}, u32[]{:S(2)}) collective-permute-start(bf16[2,24,1024]{2,1,0:T(8,128)(2,1)S(1)} %get-tuple-element.116.refs_9_), channel_id=1, source_target_pairs={{12,0},{13,1},{14,2},{15,3},{8,4},{9,5},{10,6},{11,7},{20,8},{21,9... | collective-permute-start | bytes 294920 | tf_op jit(solution)/shard_map/ppermute | solution.py:52
  52.6 2.0 %gate.7 = (bf16[1024,192]{1,0:T(8,128)(2,1)S(1)}, bf16[1024,192]{1,0:T(8,128)(2,1)S(1)}, bf16[1024,192]{1,0:T(8,128)(2,1)S(1)}, bf16[1024,192]{1,0:T(8,128)(2,1)S(1)}, f32[8,128]{1,0:T(8,128)S(1)}) custom-call(bf16[4,2,24,1024]{3,2,1,0:T(8,128)(2,1)S(1)} %double.3.refs_0_.refs_2_.x_rows, bf16[4,2,24,1024]{3,2,1,0:T(8,128)(2,1)S(1)} %collective-permute-done.16.refs_1_, ...), custom_call_target="tpu_custom_call" | custom-call | flops 1610612736 | bytes 9961472 | tf_op jit(solution)/shard_map/gate/pallas_call | solution.py:246
  54.8 1.9 %collective-permute-done.17.refs_0_ = bf16[2,24,1024]{2,1,0:T(8,128)(2,1)S(1)} collective-permute-done((bf16[2,24,1024]{2,1,0:T(8,128)(2,1)S(1)}, bf16[2,24,1024]{2,1,0:T(8,128)(2,1)S(1)}, u32[]{:S(2)}, u32[]{:S(2)}) %collective-permute-start.17) | collective-permute-done | bytes 98336 | tf_op jit(solution)/shard_map/ppermute | solution.py:52
  56.8 1.3 %collective-permute-done.19.refs_2_ = bf16[2,24,1024]{2,1,0:T(8,128)(2,1)S(1)} collective-permute-done((bf16[2,24,1024]{2,1,0:T(8,128)(2,1)S(1)}, bf16[2,24,1024]{2,1,0:T(8,128)(2,1)S(1)}, u32[]{:S(2)}, u32[]{:S(2)}) %collective-permute-start.19) | collective-permute-done | bytes 98336 | tf_op jit(solution)/shard_map/ppermute | solution.py:37
  58.1 9.7 %back.4 = (f32[96,1024]{1,0:T(8,128)S(1)}, bf16[96,1024]{1,0:T(8,128)(2,1)S(1)}) custom-call(bf16[2,24,1024]{2,1,0:T(8,128)(2,1)S(1)} %tie.14.refs_0_.refs_1_.refs_3_, bf16[2,24,1024]{2,1,0:T(8,128)(2,1)S(1)} %tie.15.refs_1_, bf16[2,24,1024]{2,1,0:T(8,128)(2,1)S(1)} %collective-permute-done.19.refs_2_, ...), custom_call_target="tpu_custom_call" | custom-call | flops 6442450944 | bytes 36700160 | tf_op jit(solution)/shard_map/back/pallas_call | solution.py:296
  68.0 1.3 %collective-permute-done.21.received = bf16[96,1024]{1,0:T(8,128)(2,1)S(1)} collective-permute-done((bf16[96,1024]{1,0:T(8,128)(2,1)S(1)}, bf16[96,1024]{1,0:T(8,128)(2,1)S(1)}, u32[]{:S(2)}, u32[]{:S(2)}) %collective-permute-start.21) | collective-permute-done | bytes 196640 | tf_op jit(solution)/shard_map/ppermute | solution.py:37
  71.3 1.6 %collective-permute-start.24 = (bf16[2,24,1024]{2,1,0:T(8,128)(2,1)S(1)}, bf16[2,24,1024]{2,1,0:T(8,128)(2,1)S(1)}, u32[]{:S(2)}, u32[]{:S(2)}) collective-permute-start(bf16[2,24,1024]{2,1,0:T(8,128)(2,1)S(1)} %get-tuple-element.131), channel_id=1, source_target_pairs={{0,6},{1,7},{2,4},{3,5},{4,2},{5,3},{6,0},{7,1},{8,14},{9,15},{10,... | collective-permute-start | bytes 294920 | tf_op jit(solution)/shard_map/ppermute | solution.py:37
  72.8 2.0 %gate.8 = (bf16[1024,192]{1,0:T(8,128)(2,1)S(1)}, bf16[1024,192]{1,0:T(8,128)(2,1)S(1)}, bf16[1024,192]{1,0:T(8,128)(2,1)S(1)}, bf16[1024,192]{1,0:T(8,128)(2,1)S(1)}, f32[8,128]{1,0:T(8,128)S(1)}) custom-call(bf16[4,2,24,1024]{3,2,1,0:T(8,128)(2,1)S(1)} %double.3.refs_0_.refs_2_.x_rows, bf16[4,2,24,1024]{3,2,1,0:T(8,128)(2,1)S(1)} %collective-permute-done.16.refs_1_, ...), custom_call_target="tpu_custom_call" | custom-call | flops 1610612736 | bytes 9961472 | tf_op jit(solution)/shard_map/gate/pallas_call | solution.py:246
  74.9 2.1 %collective-permute-done.23.refs_6_ = bf16[2,24,1024]{2,1,0:T(8,128)(2,1)S(1)} collective-permute-done((bf16[2,24,1024]{2,1,0:T(8,128)(2,1)S(1)}, bf16[2,24,1024]{2,1,0:T(8,128)(2,1)S(1)}, u32[]{:S(2)}, u32[]{:S(2)}) %collective-permute-start.23) | collective-permute-done | bytes 98336 | tf_op jit(solution)/shard_map/ppermute | solution.py:37
  77.2 3.7 %collective-permute-start.26 = (bf16[2,24,1024]{2,1,0:T(8,128)(2,1)S(1)}, bf16[2,24,1024]{2,1,0:T(8,128)(2,1)S(1)}, u32[]{:S(2)}, u32[]{:S(2)}) collective-permute-start(bf16[2,24,1024]{2,1,0:T(8,128)(2,1)S(1)} %get-tuple-element.133.refs_9_), channel_id=1, source_target_pairs={{12,0},{13,1},{14,2},{15,3},{8,4},{9,5},{10,6},{11,7},{20,8},{21,9... | collective-permute-start | bytes 294920 | tf_op jit(solution)/shard_map/ppermute | solution.py:52
  80.9 2.0 %gate.9 = (bf16[1024,192]{1,0:T(8,128)(2,1)S(1)}, bf16[1024,192]{1,0:T(8,128)(2,1)S(1)}, bf16[1024,192]{1,0:T(8,128)(2,1)S(1)}, bf16[1024,192]{1,0:T(8,128)(2,1)S(1)}, f32[8,128]{1,0:T(8,128)S(1)}) custom-call(bf16[4,2,24,1024]{3,2,1,0:T(8,128)(2,1)S(1)} %double.3.refs_0_.refs_2_.x_rows, bf16[4,2,24,1024]{3,2,1,0:T(8,128)(2,1)S(1)} %collective-permute-done.16.refs_1_, ...), custom_call_target="tpu_custom_call" | custom-call | flops 1610612736 | bytes 9961472 | tf_op jit(solution)/shard_map/gate/pallas_call | solution.py:246
  83.4 2.1 %collective-permute-done.25.refs_0_ = bf16[2,24,1024]{2,1,0:T(8,128)(2,1)S(1)} collective-permute-done((bf16[2,24,1024]{2,1,0:T(8,128)(2,1)S(1)}, bf16[2,24,1024]{2,1,0:T(8,128)(2,1)S(1)}, u32[]{:S(2)}, u32[]{:S(2)}) %collective-permute-start.25) | collective-permute-done | bytes 98336 | tf_op jit(solution)/shard_map/ppermute | solution.py:52
  85.5 1.3 %collective-permute-done.27.refs_2_ = bf16[2,24,1024]{2,1,0:T(8,128)(2,1)S(1)} collective-permute-done((bf16[2,24,1024]{2,1,0:T(8,128)(2,1)S(1)}, bf16[2,24,1024]{2,1,0:T(8,128)(2,1)S(1)}, u32[]{:S(2)}, u32[]{:S(2)}) %collective-permute-start.27) | collective-permute-done | bytes 98336 | tf_op jit(solution)/shard_map/ppermute | solution.py:37
  86.8 9.7 %back.5 = (f32[96,1024]{1,0:T(8,128)S(1)}, bf16[96,1024]{1,0:T(8,128)(2,1)S(1)}) custom-call(bf16[2,24,1024]{2,1,0:T(8,128)(2,1)S(1)} %tie.16.refs_0_.incoming, bf16[2,24,1024]{2,1,0:T(8,128)(2,1)S(1)} %tie.17.refs_1_, bf16[2,24,1024]{2,1,0:T(8,128)(2,1)S(1)} %collective-permute-done.27.refs_2_, bf16[2,24,1024]{2,1,0:T(8,128)(2,1)S(1)} %collective-permute-done.28.refs_3_, ...), custom_call_target="tpu_custom_call" | custom-call | flops 6442450944 | bytes 36700160 | tf_op jit(solution)/shard_map/back/pallas_call | solution.py:296
  96.7 1.3 %collective-permute-done.29.received = bf16[96,1024]{1,0:T(8,128)(2,1)S(1)} collective-permute-done((bf16[96,1024]{1,0:T(8,128)(2,1)S(1)}, bf16[96,1024]{1,0:T(8,128)(2,1)S(1)}, u32[]{:S(2)}, u32[]{:S(2)}) %collective-permute-start.29) | collective-permute-done | bytes 196640 | tf_op jit(solution)/shard_map/ppermute | solution.py:37
  98.0 1.2 %collective-permute-start.30 = (bf16[24,1024]{1,0:T(8,128)(2,1)S(1)}, bf16[24,1024]{1,0:T(8,128)(2,1)S(1)}, u32[]{:S(2)}, u32[]{:S(2)}) collective-permute-start(bf16[24,1024]{1,0:T(8,128)(2,1)S(1)} %get-tuple-element.146), channel_id=1, source_target_pairs={{0,2},{1,3},{2,0},{3,1},{4,6},{5,7},{6,4},{7,5},{8,10},{9,11},{10,... | collective-permute-start | bytes 147464 | tf_op jit(solution)/shard_map/ppermute | solution.py:37
  99.2 1.2 %collective-permute-start.31 = (bf16[24,1024]{1,0:T(8,128)(2,1)S(1)}, bf16[24,1024]{1,0:T(8,128)(2,1)S(1)}, u32[]{:S(2)}, u32[]{:S(2)}) collective-permute-start(bf16[24,1024]{1,0:T(8,128)(2,1)S(1)} %get-tuple-element.147), channel_id=1, source_target_pairs={{0,4},{1,5},{2,6},{3,7},{4,0},{5,1},{6,2},{7,3},{8,12},{9,13},{10,... | collective-permute-start | bytes 147464 | tf_op jit(solution)/shard_map/ppermute | solution.py:37
  100.5 1.1 %collective-permute-start.32 = (bf16[24,1024]{1,0:T(8,128)(2,1)S(1)}, bf16[24,1024]{1,0:T(8,128)(2,1)S(1)}, u32[]{:S(2)}, u32[]{:S(2)}) collective-permute-start(bf16[24,1024]{1,0:T(8,128)(2,1)S(1)} %get-tuple-element.148), channel_id=1, source_target_pairs={{0,6},{1,7},{2,4},{3,5},{4,2},{5,3},{6,0},{7,1},{8,14},{9,15},{10,... | collective-permute-start | bytes 147464 | tf_op jit(solution)/shard_map/ppermute | solution.py:37
  102.2 1.1 %collective-permute-done.31.refs_1_ = bf16[24,1024]{1,0:T(8,128)(2,1)S(1)} collective-permute-done((bf16[24,1024]{1,0:T(8,128)(2,1)S(1)}, bf16[24,1024]{1,0:T(8,128)(2,1)S(1)}, u32[]{:S(2)}, u32[]{:S(2)}) %collective-permute-start.31) | collective-permute-done | bytes 49184 | tf_op jit(solution)/shard_map/ppermute | solution.py:37
  103.3 2.1 %collective-permute-done.32.refs_2_ = bf16[24,1024]{1,0:T(8,128)(2,1)S(1)} collective-permute-done((bf16[24,1024]{1,0:T(8,128)(2,1)S(1)}, bf16[24,1024]{1,0:T(8,128)(2,1)S(1)}, u32[]{:S(2)}, u32[]{:S(2)}) %collective-permute-start.32) | collective-permute-done | bytes 49184 | tf_op jit(solution)/shard_map/ppermute | solution.py:37
  (70 shorter events, 12.8 us)
Async XLA Ops:
  1.0 8.3 %collective-permute-start.1 = (bf16[24,1024]{1,0:T(8,128)(2,1)S(1)}, bf16[24,1024]{1,0:T(8,128)(2,1)S(1)}, u32[]{:S(2)}, u32[]{:S(2)}) collective-permute-start(bf16[24,1024]{1,0:T(8,128)(2,1)S(1)} %get-tuple-element.79.after), channel_id=1, source_target_pairs={{0,16},{8,24},{16,0},{24,8},{1,17},{9,25},{17,1},{25,9},{2,18},{10... | collective-permute-start | bytes 147464 | tf_op jit(solution)/shard_map/ppermute | solution.py:42
  9.3 9.3 %collective-permute-start.4 = (bf16[2,24,1024]{2,1,0:T(8,128)(2,1)S(1)}, bf16[2,24,1024]{2,1,0:T(8,128)(2,1)S(1)}, u32[]{:S(2)}, u32[]{:S(2)}) collective-permute-start(bf16[2,24,1024]{2,1,0:T(8,128)(2,1)S(1)} %pack.1.after.refs_0_.refs_1_), channel_id=1, source_target_pairs={{0,4},{1,5},{2,6},{3,7},{4,0},{5,1},{6,2},{7,3},{8,12},{9,13},{10,... | collective-permute-start | bytes 294920 | tf_op jit(solution)/shard_map/ppermute | solution.py:37
  10.9 8.3 %collective-permute-start.5 = (bf16[2,24,1024]{2,1,0:T(8,128)(2,1)S(1)}, bf16[2,24,1024]{2,1,0:T(8,128)(2,1)S(1)}, u32[]{:S(2)}, u32[]{:S(2)}) collective-permute-start(bf16[2,24,1024]{2,1,0:T(8,128)(2,1)S(1)} %pack.1.after.refs_0_.refs_1_), channel_id=1, source_target_pairs={{0,6},{1,7},{2,4},{3,5},{4,2},{5,3},{6,0},{7,1},{8,14},{9,15},{10,... | collective-permute-start | bytes 294920 | tf_op jit(solution)/shard_map/ppermute | solution.py:37
  12.3 6.9 %collective-permute-start.3 = (bf16[2,24,1024]{2,1,0:T(8,128)(2,1)S(1)}, bf16[2,24,1024]{2,1,0:T(8,128)(2,1)S(1)}, u32[]{:S(2)}, u32[]{:S(2)}) collective-permute-start(bf16[2,24,1024]{2,1,0:T(8,128)(2,1)S(1)} %pack.1.after.refs_0_.refs_1_), channel_id=1, source_target_pairs={{0,2},{1,3},{2,0},{3,1},{4,6},{5,7},{6,4},{7,5},{8,10},{9,11},{10,... | collective-permute-start | bytes 294920 | tf_op jit(solution)/shard_map/ppermute | solution.py:37
  12.9 6.8 %collective-permute-start = (bf16[1,2,24,1024]{3,2,1,0:T(8,128)(2,1)S(1)}, bf16[1,2,24,1024]{3,2,1,0:T(8,128)(2,1)S(1)}, u32[]{:S(2)}, u32[]{:S(2)}) collective-permute-start(bf16[1,2,24,1024]{3,2,1,0:T(8,128)(2,1)S(1)} %get-tuple-element.81), channel_id=1, source_target_pairs={{0,16},{8,24},{16,0},{24,8},{1,17},{9,25},{17,1},{25,9},{2,18},{10... | collective-permute-start | bytes 294920 | tf_op jit(solution)/shard_map/ppermute | solution.py:42
  13.8 7.4 %collective-permute-start.6 = (bf16[2,24,1024]{2,1,0:T(8,128)(2,1)S(1)}, bf16[2,24,1024]{2,1,0:T(8,128)(2,1)S(1)}, u32[]{:S(2)}, u32[]{:S(2)}) collective-permute-start(bf16[2,24,1024]{2,1,0:T(8,128)(2,1)S(1)} %pack.1.after.refs_0_.refs_1_), channel_id=1, source_target_pairs={{0,1},{1,0},{2,3},{3,2},{4,5},{5,4},{6,7},{7,6},{8,9},{9,8},{10,11... | collective-permute-start | bytes 294920 | tf_op jit(solution)/shard_map/ppermute | solution.py:37
  18.6 2.6 %collective-permute-start.8 = (bf16[2,24,1024]{2,1,0:T(8,128)(2,1)S(1)}, bf16[2,24,1024]{2,1,0:T(8,128)(2,1)S(1)}, u32[]{:S(2)}, u32[]{:S(2)}) collective-permute-start(bf16[2,24,1024]{2,1,0:T(8,128)(2,1)S(1)} %tie.12.refs_2_), channel_id=1, source_target_pairs={{0,1},{1,0},{2,3},{3,2},{4,5},{5,4},{6,7},{7,6},{8,9},{9,8},{10,11... | collective-permute-start | bytes 294920 | tf_op jit(solution)/shard_map/ppermute | solution.py:37
  19.1 2.0 %collective-permute-start.9 = (bf16[2,24,1024]{2,1,0:T(8,128)(2,1)S(1)}, bf16[2,24,1024]{2,1,0:T(8,128)(2,1)S(1)}, u32[]{:S(2)}, u32[]{:S(2)}) collective-permute-start(bf16[2,24,1024]{2,1,0:T(8,128)(2,1)S(1)} %tie.13.refs_3_), channel_id=1, source_target_pairs={{0,1},{1,0},{2,3},{3,2},{4,5},{5,4},{6,7},{7,6},{8,9},{9,8},{10,11... | collective-permute-start | bytes 294920 | tf_op jit(solution)/shard_map/ppermute | solution.py:37
  19.2 1.9 %collective-permute-start.7 = (bf16[2,24,1024]{2,1,0:T(8,128)(2,1)S(1)}, bf16[2,24,1024]{2,1,0:T(8,128)(2,1)S(1)}, u32[]{:S(2)}, u32[]{:S(2)}) collective-permute-start(bf16[2,24,1024]{2,1,0:T(8,128)(2,1)S(1)} %tie.11.refs_1_.refs_2_.refs_3_), channel_id=1, source_target_pairs={{0,1},{1,0},{2,3},{3,2},{4,5},{5,4},{6,7},{7,6},{8,9},{9,8},{10,11... | collective-permute-start | bytes 294920 | tf_op jit(solution)/shard_map/ppermute | solution.py:37
  19.7 7.3 %collective-permute-start.2 = (bf16[1,2,24,1024]{3,2,1,0:T(8,128)(2,1)S(1)}, bf16[1,2,24,1024]{3,2,1,0:T(8,128)(2,1)S(1)}, u32[]{:S(2)}, u32[]{:S(2)}) collective-permute-start(bf16[1,2,24,1024]{3,2,1,0:T(8,128)(2,1)S(1)} %tie.10.one), channel_id=1, source_target_pairs={{0,2},{1,3},{2,0},{3,1},{4,6},{5,7},{6,4},{7,5},{8,10},{9,11},{10,... | collective-permute-start | bytes 294920 | tf_op jit(solution)/shard_map/ppermute | solution.py:37
  27.0 11.3 %collective-permute-start.10 = (bf16[2,2,24,1024]{3,2,1,0:T(8,128)(2,1)S(1)}, bf16[2,2,24,1024]{3,2,1,0:T(8,128)(2,1)S(1)}, u32[]{:S(2)}, u32[]{:S(2)}) collective-permute-start(bf16[2,2,24,1024]{3,2,1,0:T(8,128)(2,1)S(1)} %double.2.one), channel_id=1, source_target_pairs={{0,4},{1,5},{2,6},{3,7},{4,0},{5,1},{6,2},{7,3},{8,12},{9,13},{10,... | collective-permute-start | bytes 589832 | tf_op jit(solution)/shard_map/ppermute | solution.py:37
  38.3 5.7 %collective-permute-start.16 = (bf16[4,2,24,1024]{3,2,1,0:T(8,128)(2,1)S(1)}, bf16[4,2,24,1024]{3,2,1,0:T(8,128)(2,1)S(1)}, u32[]{:S(2)}, u32[]{:S(2)}) collective-permute-start(bf16[4,2,24,1024]{3,2,1,0:T(8,128)(2,1)S(1)} %double.3.refs_0_.refs_2_.x_rows), channel_id=1, source_target_pairs={{0,1},{1,0},{2,3},{3,2},{4,5},{5,4},{6,7},{7,6},{8,9},{9,8},{10,11... | collective-permute-start | bytes 1179656 | tf_op jit(solution)/shard_map/ppermute | solution.py:37
  38.4 2.0 %collective-permute-start.12 = (bf16[96,1024]{1,0:T(8,128)(2,1)S(1)}, bf16[96,1024]{1,0:T(8,128)(2,1)S(1)}, u32[]{:S(2)}, u32[]{:S(2)}) collective-permute-start(bf16[96,1024]{1,0:T(8,128)(2,1)S(1)} %get-tuple-element.110), channel_id=1, source_target_pairs={{0,1},{1,0},{2,3},{3,2},{4,5},{5,4},{6,7},{7,6},{8,9},{9,8},{10,11... | collective-permute-start | bytes 589832 | tf_op jit(solution)/shard_map/ppermute | solution.py:37
  38.9 7.3 %collective-permute-start.11 = (bf16[2,24,1024]{2,1,0:T(8,128)(2,1)S(1)}, bf16[2,24,1024]{2,1,0:T(8,128)(2,1)S(1)}, u32[]{:S(2)}, u32[]{:S(2)}) collective-permute-start(bf16[2,24,1024]{2,1,0:T(8,128)(2,1)S(1)} %get-tuple-element.109), channel_id=1, source_target_pairs={{0,2},{1,3},{2,0},{3,1},{4,6},{5,7},{6,4},{7,5},{8,10},{9,11},{10,... | collective-permute-start | bytes 294920 | tf_op jit(solution)/shard_map/ppermute | solution.py:37
  40.4 5.8 %collective-permute-start.13 = (bf16[2,24,1024]{2,1,0:T(8,128)(2,1)S(1)}, bf16[2,24,1024]{2,1,0:T(8,128)(2,1)S(1)}, u32[]{:S(2)}, u32[]{:S(2)}) collective-permute-start(bf16[2,24,1024]{2,1,0:T(8,128)(2,1)S(1)} %get-tuple-element.112), channel_id=1, source_target_pairs={{0,2},{1,3},{2,0},{3,1},{4,6},{5,7},{6,4},{7,5},{8,10},{9,11},{10,... | collective-permute-start | bytes 294920 | tf_op jit(solution)/shard_map/ppermute | solution.py:37
  41.4 6.7 %collective-permute-start.14 = (bf16[2,24,1024]{2,1,0:T(8,128)(2,1)S(1)}, bf16[2,24,1024]{2,1,0:T(8,128)(2,1)S(1)}, u32[]{:S(2)}, u32[]{:S(2)}) collective-permute-start(bf16[2,24,1024]{2,1,0:T(8,128)(2,1)S(1)} %get-tuple-element.113), channel_id=1, source_target_pairs={{0,4},{1,5},{2,6},{3,7},{4,0},{5,1},{6,2},{7,3},{8,12},{9,13},{10,... | collective-permute-start | bytes 294920 | tf_op jit(solution)/shard_map/ppermute | solution.py:37
  41.9 6.2 %collective-permute-start.15 = (bf16[2,24,1024]{2,1,0:T(8,128)(2,1)S(1)}, bf16[2,24,1024]{2,1,0:T(8,128)(2,1)S(1)}, u32[]{:S(2)}, u32[]{:S(2)}) collective-permute-start(bf16[2,24,1024]{2,1,0:T(8,128)(2,1)S(1)} %get-tuple-element.114), channel_id=1, source_target_pairs={{0,6},{1,7},{2,4},{3,5},{4,2},{5,3},{6,0},{7,1},{8,14},{9,15},{10,... | collective-permute-start | bytes 294920 | tf_op jit(solution)/shard_map/ppermute | solution.py:37
  48.4 6.5 %collective-permute-start.18 = (bf16[2,24,1024]{2,1,0:T(8,128)(2,1)S(1)}, bf16[2,24,1024]{2,1,0:T(8,128)(2,1)S(1)}, u32[]{:S(2)}, u32[]{:S(2)}) collective-permute-start(bf16[2,24,1024]{2,1,0:T(8,128)(2,1)S(1)} %get-tuple-element.116.refs_9_), channel_id=1, source_target_pairs={{12,0},{13,1},{14,2},{15,3},{8,4},{9,5},{10,6},{11,7},{20,8},{21,9... | collective-permute-start | bytes 294920 | tf_op jit(solution)/shard_map/ppermute | solution.py:52
  52.1 4.6 %collective-permute-start.17 = (bf16[2,24,1024]{2,1,0:T(8,128)(2,1)S(1)}, bf16[2,24,1024]{2,1,0:T(8,128)(2,1)S(1)}, u32[]{:S(2)}, u32[]{:S(2)}) collective-permute-start(bf16[2,24,1024]{2,1,0:T(8,128)(2,1)S(1)} %get-tuple-element.116.refs_9_), channel_id=1, source_target_pairs={{8,0},{9,1},{10,2},{11,3},{12,4},{13,5},{14,6},{15,7},{16,8},{17,9... | collective-permute-start | bytes 294920 | tf_op jit(solution)/shard_map/ppermute | solution.py:52
  54.8 2.0 %collective-permute-start.20 = (bf16[2,24,1024]{2,1,0:T(8,128)(2,1)S(1)}, bf16[2,24,1024]{2,1,0:T(8,128)(2,1)S(1)}, u32[]{:S(2)}, u32[]{:S(2)}) collective-permute-start(bf16[2,24,1024]{2,1,0:T(8,128)(2,1)S(1)} %tie.15.refs_1_), channel_id=1, source_target_pairs={{0,1},{1,0},{2,3},{3,2},{4,5},{5,4},{6,7},{7,6},{8,9},{9,8},{10,11... | collective-permute-start | bytes 294920 | tf_op jit(solution)/shard_map/ppermute | solution.py:37
  56.8 1.3 %collective-permute-start.19 = (bf16[2,24,1024]{2,1,0:T(8,128)(2,1)S(1)}, bf16[2,24,1024]{2,1,0:T(8,128)(2,1)S(1)}, u32[]{:S(2)}, u32[]{:S(2)}) collective-permute-start(bf16[2,24,1024]{2,1,0:T(8,128)(2,1)S(1)} %tie.14.refs_0_.refs_1_.refs_3_), channel_id=1, source_target_pairs={{0,1},{1,0},{2,3},{3,2},{4,5},{5,4},{6,7},{7,6},{8,9},{9,8},{10,11... | collective-permute-start | bytes 294920 | tf_op jit(solution)/shard_map/ppermute | solution.py:37
  67.7 1.5 %collective-permute-start.21 = (bf16[96,1024]{1,0:T(8,128)(2,1)S(1)}, bf16[96,1024]{1,0:T(8,128)(2,1)S(1)}, u32[]{:S(2)}, u32[]{:S(2)}) collective-permute-start(bf16[96,1024]{1,0:T(8,128)(2,1)S(1)} %get-tuple-element.127), channel_id=1, source_target_pairs={{0,1},{1,0},{2,3},{3,2},{4,5},{5,4},{6,7},{7,6},{8,9},{9,8},{10,11... | collective-permute-start | bytes 589832 | tf_op jit(solution)/shard_map/ppermute | solution.py:37
  69.3 5.6 %collective-permute-start.22 = (bf16[2,24,1024]{2,1,0:T(8,128)(2,1)S(1)}, bf16[2,24,1024]{2,1,0:T(8,128)(2,1)S(1)}, u32[]{:S(2)}, u32[]{:S(2)}) collective-permute-start(bf16[2,24,1024]{2,1,0:T(8,128)(2,1)S(1)} %get-tuple-element.129), channel_id=1, source_target_pairs={{0,2},{1,3},{2,0},{3,1},{4,6},{5,7},{6,4},{7,5},{8,10},{9,11},{10,... | collective-permute-start | bytes 294920 | tf_op jit(solution)/shard_map/ppermute | solution.py:37
  70.2 6.7 %collective-permute-start.23 = (bf16[2,24,1024]{2,1,0:T(8,128)(2,1)S(1)}, bf16[2,24,1024]{2,1,0:T(8,128)(2,1)S(1)}, u32[]{:S(2)}, u32[]{:S(2)}) collective-permute-start(bf16[2,24,1024]{2,1,0:T(8,128)(2,1)S(1)} %get-tuple-element.130), channel_id=1, source_target_pairs={{0,4},{1,5},{2,6},{3,7},{4,0},{5,1},{6,2},{7,3},{8,12},{9,13},{10,... | collective-permute-start | bytes 294920 | tf_op jit(solution)/shard_map/ppermute | solution.py:37
  71.3 5.7 %collective-permute-start.24 = (bf16[2,24,1024]{2,1,0:T(8,128)(2,1)S(1)}, bf16[2,24,1024]{2,1,0:T(8,128)(2,1)S(1)}, u32[]{:S(2)}, u32[]{:S(2)}) collective-permute-start(bf16[2,24,1024]{2,1,0:T(8,128)(2,1)S(1)} %get-tuple-element.131), channel_id=1, source_target_pairs={{0,6},{1,7},{2,4},{3,5},{4,2},{5,3},{6,0},{7,1},{8,14},{9,15},{10,... | collective-permute-start | bytes 294920 | tf_op jit(solution)/shard_map/ppermute | solution.py:37
  77.2 6.2 %collective-permute-start.26 = (bf16[2,24,1024]{2,1,0:T(8,128)(2,1)S(1)}, bf16[2,24,1024]{2,1,0:T(8,128)(2,1)S(1)}, u32[]{:S(2)}, u32[]{:S(2)}) collective-permute-start(bf16[2,24,1024]{2,1,0:T(8,128)(2,1)S(1)} %get-tuple-element.133.refs_9_), channel_id=1, source_target_pairs={{12,0},{13,1},{14,2},{15,3},{8,4},{9,5},{10,6},{11,7},{20,8},{21,9... | collective-permute-start | bytes 294920 | tf_op jit(solution)/shard_map/ppermute | solution.py:52
  80.9 4.6 %collective-permute-start.25 = (bf16[2,24,1024]{2,1,0:T(8,128)(2,1)S(1)}, bf16[2,24,1024]{2,1,0:T(8,128)(2,1)S(1)}, u32[]{:S(2)}, u32[]{:S(2)}) collective-permute-start(bf16[2,24,1024]{2,1,0:T(8,128)(2,1)S(1)} %get-tuple-element.133.refs_9_), channel_id=1, source_target_pairs={{8,0},{9,1},{10,2},{11,3},{12,4},{13,5},{14,6},{15,7},{16,8},{17,9... | collective-permute-start | bytes 294920 | tf_op jit(solution)/shard_map/ppermute | solution.py:52
  83.4 2.1 %collective-permute-start.28 = (bf16[2,24,1024]{2,1,0:T(8,128)(2,1)S(1)}, bf16[2,24,1024]{2,1,0:T(8,128)(2,1)S(1)}, u32[]{:S(2)}, u32[]{:S(2)}) collective-permute-start(bf16[2,24,1024]{2,1,0:T(8,128)(2,1)S(1)} %tie.17.refs_1_), channel_id=1, source_target_pairs={{0,1},{1,0},{2,3},{3,2},{4,5},{5,4},{6,7},{7,6},{8,9},{9,8},{10,11... | collective-permute-start | bytes 294920 | tf_op jit(solution)/shard_map/ppermute | solution.py:37
  96.5 1.5 %collective-permute-start.29 = (bf16[96,1024]{1,0:T(8,128)(2,1)S(1)}, bf16[96,1024]{1,0:T(8,128)(2,1)S(1)}, u32[]{:S(2)}, u32[]{:S(2)}) collective-permute-start(bf16[96,1024]{1,0:T(8,128)(2,1)S(1)} %get-tuple-element.144), channel_id=1, source_target_pairs={{0,1},{1,0},{2,3},{3,2},{4,5},{5,4},{6,7},{7,6},{8,9},{9,8},{10,11... | collective-permute-start | bytes 589832 | tf_op jit(solution)/shard_map/ppermute | solution.py:37
  98.0 4.2 %collective-permute-start.30 = (bf16[24,1024]{1,0:T(8,128)(2,1)S(1)}, bf16[24,1024]{1,0:T(8,128)(2,1)S(1)}, u32[]{:S(2)}, u32[]{:S(2)}) collective-permute-start(bf16[24,1024]{1,0:T(8,128)(2,1)S(1)} %get-tuple-element.146), channel_id=1, source_target_pairs={{0,2},{1,3},{2,0},{3,1},{4,6},{5,7},{6,4},{7,5},{8,10},{9,11},{10,... | collective-permute-start | bytes 147464 | tf_op jit(solution)/shard_map/ppermute | solution.py:37
  99.2 4.1 %collective-permute-start.31 = (bf16[24,1024]{1,0:T(8,128)(2,1)S(1)}, bf16[24,1024]{1,0:T(8,128)(2,1)S(1)}, u32[]{:S(2)}, u32[]{:S(2)}) collective-permute-start(bf16[24,1024]{1,0:T(8,128)(2,1)S(1)} %get-tuple-element.147), channel_id=1, source_target_pairs={{0,4},{1,5},{2,6},{3,7},{4,0},{5,1},{6,2},{7,3},{8,12},{9,13},{10,... | collective-permute-start | bytes 147464 | tf_op jit(solution)/shard_map/ppermute | solution.py:37
  100.5 5.0 %collective-permute-start.32 = (bf16[24,1024]{1,0:T(8,128)(2,1)S(1)}, bf16[24,1024]{1,0:T(8,128)(2,1)S(1)}, u32[]{:S(2)}, u32[]{:S(2)}) collective-permute-start(bf16[24,1024]{1,0:T(8,128)(2,1)S(1)} %get-tuple-element.148), channel_id=1, source_target_pairs={{0,6},{1,7},{2,4},{3,5},{4,2},{5,3},{6,0},{7,1},{8,14},{9,15},{10,... | collective-permute-start | bytes 147464 | tf_op jit(solution)/shard_map/ppermute | solution.py:37
  (4 other events, 29.8 us)
